TPU v7x, 512 devices: a whole 4x8x8 slice. The times are simulated.
512 devices in a mesh: ctx: 64 (over z, x, core), head: 8 (over y).
Axes of the slice: x: 4, y: 8, z: 8, core: 2. Of those that a mesh axis runs over, the one named last changes fastest.
Arguments:
- queries: bfloat16 [16384, 64, 128], P(('ctx', 'head'))
- keys: bfloat16 [16384, 8, 128], P(('ctx', 'head'))
- values: bfloat16 [16384, 8, 128], P(('ctx', 'head')), may hold values from -6 to 6
- output_gradient: bfloat16 [16384, 64, 128], P(('ctx', 'head')), may hold values from -6 to 6
- kv_list: int32 [128, 8], replicated, may hold values from 0 to 127, as said below
- kv_type: int32 [128, 8], replicated, may hold values from 0 to 3, as said below
- session_id: int32 [16384], replicated, may hold values from 0 to 31, never falling along the last dimension, each value on 1 to 1024 neighbouring positions
Outputs:
- attended: bfloat16 [16384, 64, 128], P(('ctx', 'head'))
- query_gradient: bfloat16 [16384, 64, 128], P(('ctx', 'head'))
- key_grad: bfloat16 [16384, 8, 128], P(('ctx', 'head'))
- value_grad: bfloat16 [16384, 8, 128], P(('ctx', 'head'))
Inputs may be any that keep to these rules, and one draw needn't show every extreme that they name: `kv_list`: entry 0 of query block i is block i, and it is the only listed block owned by the same index of ctx as block i. No list names a block twice. The query blocks of one index d of ctx (blocks d * 2 to d * 2 + 1) list at most one block owned by any other index of ctx, and every index but 0 lists exactly one block of index 0. Every query block from 2 on lists block 0 as entry 1. `kv_type`: entry 0 has type 0; entry 1 has type 1 where it names block 0.
All inputs are finite; a program needn't handle non-finite values.
Results may differ from a plain program's by a relative error of at most 0.029.
Values may be sent and summed in bfloat16 or wider, within the bound.
No kernel may reach another device: no remote copies, remote signals or barrier semaphores. Data moves between devices by JAX's collectives and lax.ppermute only.
A program may use at most 64 MiB of HBM per device.

v0:
```python
import jax
import jax.numpy as jnp
from jax import lax
from jax.sharding import PartitionSpec as P

BLOCK_TOKENS = 128


def visible(query_pos, key_pos, query_sess, key_sess, kind_rows, block_len):
    query_col = query_pos[:, None, None]
    key_grid = key_pos[None, :, :]
    same_session = query_sess[:, None, None] == key_sess[None, :, :]
    kind_grid = kind_rows[None, :, None]
    causal = (key_grid <= query_col) & same_session
    aligned = key_grid % block_len <= query_col % block_len
    allowed = jnp.where(
        kind_grid == 0,
        causal,
        jnp.where(
            kind_grid == 1, jnp.ones_like(causal), jnp.where(kind_grid == 2, same_session, aligned)
        ),
    )
    return allowed.reshape(query_pos.shape[0], -1)


def softmax_grads(query_piece, gradient_piece, key_piece, value_piece, allowed, score_scale):
    scores = (
        jnp.einsum("qkgd,skd->kgqs", query_piece, key_piece, preferred_element_type=jnp.float32)
        * score_scale
    )
    scores = jnp.where(allowed, scores, -jnp.inf)
    row_max = jnp.max(scores, axis=-1, keepdims=True)
    log_total = row_max + jnp.log(jnp.sum(jnp.exp(scores - row_max), axis=-1, keepdims=True))
    softmax_weight = jnp.exp(scores - log_total).astype(jnp.bfloat16)
    attended = jnp.einsum(
        "kgqs,skd->qkgd", softmax_weight, value_piece, preferred_element_type=jnp.float32
    ).astype(jnp.bfloat16)
    row_dot = jnp.einsum(
        "qkgd,qkgd->kgq", gradient_piece, attended, preferred_element_type=jnp.float32
    )
    prob_grad = jnp.einsum(
        "qkgd,skd->kgqs", gradient_piece, value_piece, preferred_element_type=jnp.float32
    )
    score_gradient = (
        softmax_weight.astype(jnp.float32) * (prob_grad - row_dot[..., None]) * score_scale
    ).astype(jnp.bfloat16)
    return (attended, softmax_weight, score_gradient)


def key_terms(score_gradient, query_piece):
    return jnp.einsum(
        "anbx,bano->xao", score_gradient, query_piece, preferred_element_type=jnp.float32
    )


def value_terms(softmax_weight, gradient_piece):
    return jnp.einsum(
        "anbx,bano->xao", softmax_weight, gradient_piece, preferred_element_type=jnp.float32
    )


def spread(weights, parts):
    return jnp.einsum("be,eqkd->bqkd", weights, parts, precision=lax.Precision.HIGHEST)


def per_device(queries, keys, values, output_gradient, kv_list, kv_type, session_id):
    queries, keys, values, output_gradient = (
        lax.all_to_all(queries, "head", split_axis=1, concat_axis=0, tiled=True),
        lax.all_to_all(keys, "head", split_axis=1, concat_axis=0, tiled=True),
        lax.all_to_all(values, "head", split_axis=1, concat_axis=0, tiled=True),
        lax.all_to_all(output_gradient, "head", split_axis=1, concat_axis=0, tiled=True),
    )
    tok_rows, query_heads, head_width = queries.shape
    kv_heads = keys.shape[1]
    group_width = query_heads // kv_heads
    blocks_dev = tok_rows // BLOCK_TOKENS
    devices = lax.axis_size("ctx")
    my_index = lax.axis_index("ctx")
    first_row = my_index * blocks_dev
    list_len = kv_list.shape[1]
    owner_of = kv_list // blocks_dev
    my_lists = lax.dynamic_slice_in_dim(kv_list, first_row, blocks_dev, 0)
    my_kinds = lax.dynamic_slice_in_dim(kv_type, first_row, blocks_dev, 0)
    my_owners = my_lists // blocks_dev
    remote = my_owners != my_index
    peer_ids = jnp.arange(devices, dtype=jnp.int32)
    local_rows = jnp.arange(blocks_dev, dtype=jnp.int32)
    asked_blocks = kv_list.reshape(devices, blocks_dev * list_len)
    asked_owner = owner_of.reshape(devices, blocks_dev * list_len)
    matches = (asked_owner == my_index) & (peer_ids[:, None] != my_index)
    wanted = jnp.max(jnp.where(matches, asked_blocks - first_row, -1), axis=1)
    picked = jnp.maximum(wanted, 0)
    key_block_rows = keys.reshape(blocks_dev, BLOCK_TOKENS, kv_heads, head_width)
    value_block_rows = values.reshape(blocks_dev, BLOCK_TOKENS, kv_heads, head_width)
    fetched_keys, fetched_values = (
        lax.all_to_all(key_block_rows[picked], "ctx", split_axis=0, concat_axis=0, tiled=True),
        lax.all_to_all(value_block_rows[picked], "ctx", split_axis=0, concat_axis=0, tiled=True),
    )
    source = jnp.where(remote, blocks_dev + my_owners, my_lists - first_row)
    key_tiles = jnp.concatenate([key_block_rows, fetched_keys], 0)[source]
    value_tiles = jnp.concatenate([value_block_rows, fetched_values], 0)[source]
    offsets = jnp.arange(BLOCK_TOKENS, dtype=jnp.int32)
    score_scale = head_width ** (-0.5)
    block_ids = first_row + local_rows
    query_view = queries.reshape(blocks_dev, BLOCK_TOKENS, kv_heads, group_width, head_width)
    grad_view = output_gradient.reshape(blocks_dev, BLOCK_TOKENS, kv_heads, group_width, head_width)
    from_peers = (wanted[None, :] == local_rows[:, None]).astype(jnp.float32)

    def block_mask(listed_entries, kind_rows, block_index):
        query_pos = block_index * BLOCK_TOKENS + offsets
        key_pos = listed_entries[:, None] * BLOCK_TOKENS + offsets[None, :]
        return visible(
            query_pos, key_pos, session_id[query_pos], session_id[key_pos], kind_rows, BLOCK_TOKENS
        )[None, None]

    def per_block(pieces):
        (
            query_piece,
            gradient_piece,
            key_piece,
            value_piece,
            listed_entries,
            kind_rows,
            block_index,
        ) = pieces
        key_flat = key_piece.reshape(-1, kv_heads, head_width)
        value_flat = value_piece.reshape(-1, kv_heads, head_width)
        allowed = block_mask(listed_entries, kind_rows, block_index)
        attended, softmax_weight, score_gradient = softmax_grads(
            query_piece, gradient_piece, key_flat, value_flat, allowed, score_scale
        )
        query_gradient = jnp.einsum(
            "kgqs,skd->qkgd", score_gradient, key_flat, preferred_element_type=jnp.float32
        ).astype(jnp.bfloat16)
        return (
            attended,
            query_gradient,
            key_terms(score_gradient, query_piece),
            value_terms(softmax_weight, gradient_piece),
        )

    attended, query_gradient, key_parts, value_parts = lax.map(
        per_block, (query_view, grad_view, key_tiles, value_tiles, my_lists, my_kinds, block_ids)
    )
    key_parts = key_parts.reshape(blocks_dev * list_len, BLOCK_TOKENS, kv_heads, head_width)
    value_parts = value_parts.reshape(blocks_dev * list_len, BLOCK_TOKENS, kv_heads, head_width)
    flat_lists = my_lists.reshape(-1)
    flat_owners = my_owners.reshape(-1)
    flat_remote = remote.reshape(-1)
    to_local = (
        jnp.logical_not(flat_remote)[None, :]
        & (flat_lists[None, :] - first_row == local_rows[:, None])
    ).astype(jnp.float32)
    to_peers = (flat_remote[None, :] & (flat_owners[None, :] == peer_ids[:, None])).astype(
        jnp.float32
    )
    returned_keys, returned_values = (
        lax.all_to_all(
            spread(to_peers, key_parts).astype(jnp.bfloat16),
            "ctx",
            split_axis=0,
            concat_axis=0,
            tiled=True,
        ).astype(jnp.float32),
        lax.all_to_all(
            spread(to_peers, value_parts).astype(jnp.bfloat16),
            "ctx",
            split_axis=0,
            concat_axis=0,
            tiled=True,
        ).astype(jnp.float32),
    )
    key_sum = spread(to_local, key_parts) + spread(from_peers, returned_keys)
    value_sum = spread(to_local, value_parts) + spread(from_peers, returned_values)
    return (
        lax.all_to_all(
            attended.reshape(tok_rows, query_heads, head_width),
            "head",
            split_axis=0,
            concat_axis=1,
            tiled=True,
        ),
        lax.all_to_all(
            query_gradient.reshape(tok_rows, query_heads, head_width),
            "head",
            split_axis=0,
            concat_axis=1,
            tiled=True,
        ),
        lax.all_to_all(
            key_sum.reshape(tok_rows, kv_heads, head_width).astype(jnp.bfloat16),
            "head",
            split_axis=0,
            concat_axis=1,
            tiled=True,
        ),
        lax.all_to_all(
            value_sum.reshape(tok_rows, kv_heads, head_width).astype(jnp.bfloat16),
            "head",
            split_axis=0,
            concat_axis=1,
            tiled=True,
        ),
    )


def solution(mesh):
    placed = (
        P(("ctx", "head"), None, None),
        P(("ctx", "head"), None, None),
        P(("ctx", "head"), None, None),
        P(("ctx", "head"), None, None),
        P(),
        P(),
        P(),
    )
    return jax.shard_map(
        per_device,
        mesh=mesh,
        in_specs=placed,
        out_specs=(
            P(("ctx", "head"), None, None),
            P(("ctx", "head"), None, None),
            P(("ctx", "head"), None, None),
            P(("ctx", "head"), None, None),
        ),
        check_vma=False,
    )
```

profile of v0, /device:TPU:1, one launch (start us, length us, event | category | flops | bytes accessed | tf_op | source)
XLA Modules:
  0.0 430.8 jit_solution(11312188817425857552)
XLA Ops:
  2.2 7.7 %all-to-all-start = ((bf16[32,8,128]{2,0,1:T(8,128)(2,1)}), bf16[32,8,128]{2,0,1:T(8,128)(2,1)S(1)}, u32[]{:S(2)}, u32[]{:S(2)}) async-start(bf16[32,8,128]{2,0,1:T(8,128)(2,1)} %copy.91), calls=%async_computation | async-start | bytes 131072 | tf_op jit(solution)/shard_map/all_to_all | solution.py:70
  11.3 5.7 %all-to-all-done = bf16[32,8,128]{2,0,1:T(8,128)(2,1)S(1)} async-done(((bf16[32,8,128]{2,0,1:T(8,128)(2,1)}), bf16[32,8,128]{2,0,1:T(8,128)(2,1)S(1)}, u32[]{:S(2)}, u32[]{:S(2)}) %all-to-all-start) | async-done | bytes 65568 | tf_op jit(solution)/shard_map/all_to_all | solution.py:70
  17.1 3.4 all-to-all-start.2
  22.6 5.0 %all-to-all-done.2 = bf16[32,8,128]{2,0,1:T(8,128)(2,1)S(1)} async-done(((bf16[32,8,128]{2,0,1:T(8,128)(2,1)}), bf16[32,8,128]{2,0,1:T(8,128)(2,1)S(1)}, u32[]{:S(2)}, u32[]{:S(2)}) %all-to-all-start.2) | async-done | bytes 65568 | tf_op jit(solution)/shard_map/all_to_all | solution.py:69
  27.6 3.5 all-to-all-start.4
  32.2 10.6 %all-to-all-done.4 = bf16[32,64,128]{2,0,1:T(8,128)(2,1)S(1)} async-done(((bf16[32,64,128]{2,0,1:T(8,128)(2,1)}), bf16[32,64,128]{2,0,1:T(8,128)(2,1)S(1)}, u32[]{:S(2)}, u32[]{:S(2)}) %all-to-all-start.4) | async-done | bytes 524320 | tf_op jit(solution)/shard_map/all_to_all | solution.py:68
  42.9 3.5 all-to-all-start.5
  49.1 9.4 %all-to-all-done.5 = bf16[32,64,128]{2,0,1:T(8,128)(2,1)S(1)} async-done(((bf16[32,64,128]{2,0,1:T(8,128)(2,1)}), bf16[32,64,128]{2,0,1:T(8,128)(2,1)S(1)}, u32[]{:S(2)}, u32[]{:S(2)}) %all-to-all-start.5) | async-done | bytes 524320 | tf_op jit(solution)/shard_map/all_to_all | solution.py:71
  59.3 21.9 %all-to-all-start.1 = ((bf16[64,128,1,128]{3,1,2,0:T(8,128)(2,1)}), bf16[64,128,1,128]{3,1,2,0:T(8,128)(2,1)S(1)}, u32[]{:S(2)}, u32[]{:S(2)}) async-start(bf16[64,128,1,128]{3,1,2,0:T(8,128)(2,1)} %bitcast.308), calls=%async_computation.1 | async-start | bytes 4194304 | tf_op jit(solution)/shard_map/all_to_all | solution.py:97
  83.3 47.5 %all-to-all-done.1 = bf16[64,128,1,128]{3,1,2,0:T(8,128)(2,1)S(1)} async-done(((bf16[64,128,1,128]{3,1,2,0:T(8,128)(2,1)}), bf16[64,128,1,128]{3,1,2,0:T(8,128)(2,1)S(1)}, u32[]{:S(2)}, u32[]{:S(2)}) %all-to-all-start.1) | async-done | bytes 2097184 | tf_op jit(solution)/shard_map/all_to_all | solution.py:97
  130.9 7.4 %all-to-all-start.3 = ((bf16[64,128,1,128]{3,1,2,0:T(8,128)(2,1)}), bf16[64,128,1,128]{3,1,2,0:T(8,128)(2,1)}, u32[]{:S(2)}, u32[]{:S(2)}) async-start(bf16[64,128,1,128]{3,1,2,0:T(8,128)(2,1)} %bitcast.307), calls=%async_computation.3 | async-start | bytes 4194304 | tf_op jit(solution)/shard_map/all_to_all | solution.py:96
  142.6 3.0 gather_fusion.3
  145.6 42.2 %all-to-all-done.3 = bf16[64,128,1,128]{3,1,2,0:T(8,128)(2,1)} async-done(((bf16[64,128,1,128]{3,1,2,0:T(8,128)(2,1)}), bf16[64,128,1,128]{3,1,2,0:T(8,128)(2,1)}, u32[]{:S(2)}, u32[]{:S(2)}) %all-to-all-start.3) | async-done | bytes 2097184 | tf_op jit(solution)/shard_map/all_to_all | solution.py:96
  191.1 60.4 %while.20 = (s32[]{:T(128)}, bf16[2,128,1,8,128]{4,3,1,0,2:T(8,128)(2,1)}, bf16[2,128,1,8,128]{4,3,1,0,2:T(8,128)(2,1)}, f32[2,1024,1,128]{3,1,0,2:T(8,128)}, f3...) while((s32[]{:T(128)}, ...), condition=%wide.region_5.6_spmd.clone.clone, body=%wide.region_2.5_spmd.clone.clone.sunk | while | flops 1629112448 | bytes 64324132 | solution.py:142
  193.7 6.1 %gather_fusion.1 = s32[1024]{0:T(1024)S(1)} fusion(s32[16384]{0:T(1024)S(1)} %get-tuple-element.492, s32[1024]{0:T(1024)S(1)} %fusion.121), kind=kCustom, calls=%fused_computation.1.clone.clone.1 | custom fusion | bytes 12288 | tf_op jit(solution)/shard_map/while/body/eval_jaxpr/gather | solution.py:113
  207.9 2.2 multiply_reduce_fusion.2
  223.9 6.1 %gather_fusion.1 = s32[1024]{0:T(1024)S(1)} fusion(s32[16384]{0:T(1024)S(1)} %get-tuple-element.492, s32[1024]{0:T(1024)S(1)} %fusion.121), kind=kCustom, calls=%fused_computation.1.clone.clone.1 | custom fusion | bytes 12288 | tf_op jit(solution)/shard_map/while/body/eval_jaxpr/gather | solution.py:113
  238.1 2.2 multiply_reduce_fusion.2
  251.5 18.8 %all_to_all.152 = bf16[256,8,128]{2,1,0:T(8,128)(2,1)} all-to-all(bf16[256,8,128]{2,1,0:T(8,128)(2,1)} %bitcast.320), channel_id=1, replica_groups=mesh['ctx'=64,'head'=8] {'head'}, dimensions={0} | all-to-all | bytes 1048576 | tf_op jit(solution)/shard_map/all_to_all | solution.py:183
  270.3 3.7 all-to-all-start.6
  276.4 2.7 copy.123
  279.0 8.8 %all-to-all-done.6 = bf16[256,8,128]{2,1,0:T(8,128)(2,1)S(1)} async-done(((bf16[256,8,128]{2,1,0:T(8,128)(2,1)}), bf16[256,8,128]{2,1,0:T(8,128)(2,1)S(1)}, u32[]{:S(2)}, u32[]{:S(2)}) %all-to-all-start.6) | async-done | bytes 524320 | tf_op jit(solution)/shard_map/all_to_all | solution.py:176
  288.6 12.8 %all-to-all-start.10 = ((bf16[64,128,1,128]{3,1,2,0:T(8,128)(2,1)}), bf16[64,128,1,128]{3,1,2,0:T(8,128)(2,1)S(1)}, u32[]{:S(2)}, u32[]{:S(2)}) async-start(bf16[64,128,1,128]{3,1,2,0:T(8,128)(2,1)} %copy.123), calls=%async_computation.10 | async-start | bytes 4194304 | tf_op jit(solution)/shard_map/all_to_all | solution.py:165
  303.5 2.7 copy.116
  306.2 44.8 %all-to-all-done.10 = bf16[64,128,1,128]{3,1,2,0:T(8,128)(2,1)S(1)} async-done(((bf16[64,128,1,128]{3,1,2,0:T(8,128)(2,1)}), bf16[64,128,1,128]{3,1,2,0:T(8,128)(2,1)S(1)}, u32[]{:S(2)}, u32[]{:S(2)}) %all-to-all-start.10) | async-done | bytes 2097184 | tf_op jit(solution)/shard_map/all_to_all | solution.py:165
  352.3 7.0 %all-to-all-start.8 = ((bf16[64,128,1,128]{3,1,2,0:T(8,128)(2,1)}), bf16[64,128,1,128]{3,1,2,0:T(8,128)(2,1)S(1)}, u32[]{:S(2)}, u32[]{:S(2)}) async-start(bf16[64,128,1,128]{3,1,2,0:T(8,128)(2,1)} %copy.116), calls=%async_computation.8 | async-start | bytes 4194304 | tf_op jit(solution)/shard_map/all_to_all | solution.py:158
  359.5 2.4 fusion.62
  366.1 43.0 %all-to-all-done.8 = bf16[64,128,1,128]{3,1,2,0:T(8,128)(2,1)S(1)} async-done(((bf16[64,128,1,128]{3,1,2,0:T(8,128)(2,1)}), bf16[64,128,1,128]{3,1,2,0:T(8,128)(2,1)S(1)}, u32[]{:S(2)}, u32[]{:S(2)}) %all-to-all-start.8) | async-done | bytes 2097184 | tf_op jit(solution)/shard_map/all_to_all | solution.py:158
  409.0 3.4 all-to-all-start.11
  415.0 4.6 %all-to-all-done.11 = bf16[8,2,2048]{2,1,0:T(2,128)(2,1)S(1)} async-done(((bf16[8,2,2048]{2,1,0:T(2,128)(2,1)}), bf16[8,2,2048]{2,1,0:T(2,128)(2,1)S(1)}, u32[]{:S(2)}, u32[]{:S(2)}) %all-to-all-start.11) | async-done | bytes 65568 | tf_op jit(solution)/shard_map/all_to_all | solution.py:197
  419.5 3.4 all-to-all-start.9
  425.5 4.5 %all-to-all-done.9 = bf16[8,2,2048]{2,1,0:T(2,128)(2,1)S(1)} async-done(((bf16[8,2,2048]{2,1,0:T(2,128)(2,1)}), bf16[8,2,2048]{2,1,0:T(2,128)(2,1)S(1)}, u32[]{:S(2)}, u32[]{:S(2)}) %all-to-all-start.9) | async-done | bytes 65568 | tf_op jit(solution)/shard_map/all_to_all | solution.py:190
  (169 shorter events, 78.2 us)
Async XLA Ops:
  0.6 30.4 %copy-start.14 = (bf16[32,64,128]{2,1,0:T(8,128)(2,1)S(1)}, bf16[32,64,128]{2,1,0:T(8,128)(2,1)}, u32[]{:S(2)}) copy-start(bf16[32,64,128]{2,1,0:T(8,128)(2,1)} %param.12) | copy-start | bytes 1572868
  2.2 14.9 %all-to-all-start = ((bf16[32,8,128]{2,0,1:T(8,128)(2,1)}), bf16[32,8,128]{2,0,1:T(8,128)(2,1)S(1)}, u32[]{:S(2)}, u32[]{:S(2)}) async-start(bf16[32,8,128]{2,0,1:T(8,128)(2,1)} %copy.91), calls=%async_computation | async-start | bytes 131072 | tf_op jit(solution)/shard_map/all_to_all | solution.py:70
  17.1 10.5 %all-to-all-start.2 = ((bf16[32,8,128]{2,0,1:T(8,128)(2,1)}), bf16[32,8,128]{2,0,1:T(8,128)(2,1)S(1)}, u32[]{:S(2)}, u32[]{:S(2)}) async-start(bf16[32,8,128]{2,0,1:T(8,128)(2,1)} %copy.96), calls=%async_computation.2 | async-start | bytes 131072 | tf_op jit(solution)/shard_map/all_to_all | solution.py:69
  20.4 26.2 %copy-start.15 = (s32[128,8]{0,1:T(8,128)S(1)}, s32[128,8]{0,1:T(8,128)}, u32[]{:S(2)}) copy-start(s32[128,8]{0,1:T(8,128)} %param.13) | copy-start | bytes 12292
  27.6 15.3 %all-to-all-start.4 = ((bf16[32,64,128]{2,0,1:T(8,128)(2,1)}), bf16[32,64,128]{2,0,1:T(8,128)(2,1)S(1)}, u32[]{:S(2)}, u32[]{:S(2)}) async-start(bf16[32,64,128]{2,0,1:T(8,128)(2,1)} %copy.99), calls=%async_computation.4 | async-start | bytes 1048576 | tf_op jit(solution)/shard_map/all_to_all | solution.py:68
  42.9 15.7 %all-to-all-start.5 = ((bf16[32,64,128]{2,0,1:T(8,128)(2,1)}), bf16[32,64,128]{2,0,1:T(8,128)(2,1)S(1)}, u32[]{:S(2)}, u32[]{:S(2)}) async-start(bf16[32,64,128]{2,0,1:T(8,128)(2,1)} %copy.102), calls=%async_computation.5 | async-start | bytes 1048576 | tf_op jit(solution)/shard_map/all_to_all | solution.py:71
  58.5 0.8 copy-start.13
  59.3 71.6 %all-to-all-start.1 = ((bf16[64,128,1,128]{3,1,2,0:T(8,128)(2,1)}), bf16[64,128,1,128]{3,1,2,0:T(8,128)(2,1)S(1)}, u32[]{:S(2)}, u32[]{:S(2)}) async-start(bf16[64,128,1,128]{3,1,2,0:T(8,128)(2,1)} %bitcast.308), calls=%async_computation.1 | async-start | bytes 4194304 | tf_op jit(solution)/shard_map/all_to_all | solution.py:97
  130.9 7.4 %copy-start.16 = (s32[128,8]{0,1:T(8,128)S(1)}, s32[128,8]{0,1:T(8,128)}, u32[]{:S(2)}) copy-start(s32[128,8]{0,1:T(8,128)} %param.14) | copy-start | bytes 12292
  130.9 56.9 %all-to-all-start.3 = ((bf16[64,128,1,128]{3,1,2,0:T(8,128)(2,1)}), bf16[64,128,1,128]{3,1,2,0:T(8,128)(2,1)}, u32[]{:S(2)}, u32[]{:S(2)}) async-start(bf16[64,128,1,128]{3,1,2,0:T(8,128)(2,1)} %bitcast.307), calls=%async_computation.3 | async-start | bytes 4194304 | tf_op jit(solution)/shard_map/all_to_all | solution.py:96
  187.8 3.2 copy-start
  191.1 14.8 %copy-start.6 = (bf16[2,128,1,8,128]{4,3,1,0,2:T(8,128)(2,1)}, bf16[2,128,1,8,128]{4,3,1,0,2:T(8,128)(2,1)S(1)}, u32[]{:S(2)}) copy-start(bf16[2,128,1,8,128]{4,3,1,0,2:T(8,128)(2,1)S(1)} %get-tuple-element.495) | copy-start | bytes 1572868 | tf_op jit(solution)/shard_map/while
  211.0 1.3 copy-start.1
  216.8 2.4 copy-start.2
  219.3 0.9 copy-start.3
  219.3 2.0 copy-start.7
  221.3 14.8 %copy-start.6 = (bf16[2,128,1,8,128]{4,3,1,0,2:T(8,128)(2,1)}, bf16[2,128,1,8,128]{4,3,1,0,2:T(8,128)(2,1)S(1)}, u32[]{:S(2)}) copy-start(bf16[2,128,1,8,128]{4,3,1,0,2:T(8,128)(2,1)S(1)} %get-tuple-element.495) | copy-start | bytes 1572868 | tf_op jit(solution)/shard_map/while
  241.2 1.3 copy-start.1
  247.0 2.5 copy-start.2
  249.5 0.9 copy-start.3
  249.5 2.0 copy-start.7
  251.5 22.7 %copy-start.9 = (f32[2,1024,1,128]{3,1,0,2:T(8,128)S(1)}, f32[2,1024,1,128]{3,1,0,2:T(8,128)}, u32[]{:S(2)}) copy-start(f32[2,1024,1,128]{3,1,0,2:T(8,128)} %get-tuple-element.190) | copy-start | bytes 3145732
  270.3 17.5 %all-to-all-start.6 = ((bf16[256,8,128]{2,1,0:T(8,128)(2,1)}), bf16[256,8,128]{2,1,0:T(8,128)(2,1)S(1)}, u32[]{:S(2)}, u32[]{:S(2)}) async-start(bf16[256,8,128]{2,1,0:T(8,128)(2,1)} %bitcast.319), calls=%async_computation.6 | async-start | bytes 1048576 | tf_op jit(solution)/shard_map/all_to_all | solution.py:176
  279.0 22.3 %copy-start.8 = (f32[2,1024,1,128]{3,1,0,2:T(8,128)S(1)}, f32[2,1024,1,128]{3,1,0,2:T(8,128)}, u32[]{:S(2)}) copy-start(f32[2,1024,1,128]{3,1,0,2:T(8,128)} %get-tuple-element.189) | copy-start | bytes 3145732
  288.6 62.4 %all-to-all-start.10 = ((bf16[64,128,1,128]{3,1,2,0:T(8,128)(2,1)}), bf16[64,128,1,128]{3,1,2,0:T(8,128)(2,1)S(1)}, u32[]{:S(2)}, u32[]{:S(2)}) async-start(bf16[64,128,1,128]{3,1,2,0:T(8,128)(2,1)} %copy.123), calls=%async_computation.10 | async-start | bytes 4194304 | tf_op jit(solution)/shard_map/all_to_all | solution.py:165
  351.0 1.3 copy-start.4
  352.3 56.7 %all-to-all-start.8 = ((bf16[64,128,1,128]{3,1,2,0:T(8,128)(2,1)}), bf16[64,128,1,128]{3,1,2,0:T(8,128)(2,1)S(1)}, u32[]{:S(2)}, u32[]{:S(2)}) async-start(bf16[64,128,1,128]{3,1,2,0:T(8,128)(2,1)} %copy.116), calls=%async_computation.8 | async-start | bytes 4194304 | tf_op jit(solution)/shard_map/all_to_all | solution.py:158
  359.5 3.5 copy-start.5
  364.2 58.7 %copy-start.10 = (bf16[256,8,128]{2,1,0:T(8,128)(2,1)S(1)}, bf16[256,8,128]{2,1,0:T(8,128)(2,1)}, u32[]{:S(2)}) copy-start(bf16[256,8,128]{2,1,0:T(8,128)(2,1)} %all_to_all.152) | copy-start | bytes 1572868
  365.4 58.4 %copy-start.12 = (bf16[256,8,128]{2,1,0:T(8,128)(2,1)S(1)}, bf16[256,8,128]{2,1,0:T(8,128)(2,1)}, u32[]{:S(2)}) copy-start(bf16[256,8,128]{2,1,0:T(8,128)(2,1)} %copy-done.11) | copy-start | bytes 1572868
  409.0 10.5 %all-to-all-start.11 = ((bf16[8,2,2048]{2,1,0:T(2,128)(2,1)}), bf16[8,2,2048]{2,1,0:T(2,128)(2,1)S(1)}, u32[]{:S(2)}, u32[]{:S(2)}) async-start(bf16[8,2,2048]{2,1,0:T(2,128)(2,1)} %reshape.686), calls=%async_computation.11 | async-start | bytes 131072 | tf_op jit(solution)/shard_map/all_to_all | solution.py:197
  419.5 10.5 %all-to-all-start.9 = ((bf16[8,2,2048]{2,1,0:T(2,128)(2,1)}), bf16[8,2,2048]{2,1,0:T(2,128)(2,1)S(1)}, u32[]{:S(2)}, u32[]{:S(2)}) async-start(bf16[8,2,2048]{2,1,0:T(2,128)(2,1)} %reshape.684), calls=%async_computation.9 | async-start | bytes 131072 | tf_op jit(solution)/shard_map/all_to_all | solution.py:190
  (1 other events, 0.8 us)
where the time goes:
time: 436 us; the launch traced here: 431 us
  waiting for transfers between devices  226 us (52%)
  starting transfers between devices  77.4 us (18%)
  local copies, waits for them, and re-layouts  69.2 us (16%)
  matrix products  25.3 us (6%)
  blocking collectives  18.8 us (4%)
  other arithmetic  11.2 us (3%)
    all_to_all x1, waiting for transfers between devices, per_device(): lax.all_to_all(value_block_rows[picked], 'ctx', split_axis=0, concat_axis...  47.5 us
    all_to_all x1, waiting for transfers between devices, per_device(): lax.all_to_all(spread(to_peers, value_parts).astype(jnp.bfloat16), 'ctx',...  44.8 us
    all_to_all x1, waiting for transfers between devices, per_device(): lax.all_to_all(spread(to_peers, key_parts).astype(jnp.bfloat16), 'ctx', s...  43 us
    all_to_all x1, waiting for transfers between devices, per_device(): lax.all_to_all(key_block_rows[picked], 'ctx', split_axis=0, concat_axis=0...  42.2 us
    all_to_all x1, starting transfers between devices, per_device(): lax.all_to_all(value_block_rows[picked], 'ctx', split_axis=0, concat_axis...  21.9 us
    all_to_all x1, blocking collectives, per_device(): lax.all_to_all(query_gradient.reshape(tok_rows, query_heads, head_width),...  18.8 us
    all_to_all x1, starting transfers between devices, per_device(): lax.all_to_all(spread(to_peers, value_parts).astype(jnp.bfloat16), 'ctx',...  12.8 us
    gather x2, local copies, waits for them, and re-layouts, block_mask(): session_id[key_pos]  12.3 us
  transfers between devices with their start and end apart: 11, of which 11 were waited for; matrix products, arithmetic and copies ran while one was open for 9% of the time, Pallas kernels for 0%

commit v1 on v0

v1 whole, which is shorter than its diff:
```python
import functools

import jax
import jax.numpy as jnp
from jax import lax
from jax.experimental import pallas as pl
from jax.experimental.pallas import tpu as pltpu
from jax.sharding import Mesh, PartitionSpec as P

BLOCK = 128
WIDTH = 128
LISTED = 8
ENTRIES = 16
Z, X, CORE, HEAD = 8, 4, 2, 8
CTX = Z * X * CORE
GROUP = 8
QUARTER = 32
MOST = 14
LOG2E = 1.4426950408889634
MIB = 1 << 20

SMEM = pl.BlockSpec(memory_space=pltpu.SMEM)
VMEM = pl.BlockSpec(memory_space=pltpu.VMEM)


def owner_x(block):
    return lax.rem(lax.shift_right_logical(block, 2), X)


def owner_core(block):
    return lax.rem(lax.shift_right_logical(block, 1), CORE)


def slab_row(block):
    return lax.shift_right_logical(block, 4) * 2 + lax.rem(block, 2)


def gather_kernel(place, ent, slot, first, own_ref, oth_ref, s1, s2, s3):
    z, x, core = place[0], place[1], place[2]
    for k, out in ((1, s1), (2, s2), (3, s3)):
        base = (z * (X * CORE) + lax.rem(x + k, X) * CORE + core) * ENTRIES

        @pl.loop(0, ENTRIES)
        def _(e):
            block = ent[base + e]
            row = slab_row(block)
            sl = slot[base + e]
            mine = (first[base + e] == e) & (owner_x(block) == x)
            same_core = owner_core(block) == core

            @pl.when(mine & same_core)
            def _():
                out[sl] = own_ref[row]

            @pl.when(mine & jnp.logical_not(same_core))
            def _():
                out[sl] = oth_ref[row]


def scatter_kernel(place, ent, slot, first, g0, g1, g2, g3, own_out, oth_out, acc):
    z, x, core = place[0], place[1], place[2]
    acc[...] = jnp.zeros_like(acc)
    for k, buf in ((0, g0), (1, g1), (2, g2), (3, g3)):
        base = (z * (X * CORE) + lax.rem(x + k, X) * CORE + core) * ENTRIES

        @pl.loop(0, ENTRIES)
        def _(e):
            block = ent[base + e]
            mine = (first[base + e] == e) & (owner_x(block) == x)

            @pl.when(mine)
            def _():
                away = jnp.where(owner_core(block) == core, 0, ENTRIES)
                row = slab_row(block) + away
                acc[row] += buf[slot[base + e]].astype(jnp.float32)

    own_out[...] = acc[:ENTRIES].astype(jnp.bfloat16)
    oth_out[...] = acc[ENTRIES:].astype(jnp.bfloat16)


def attend_kernel(
    place, ent, kind, slot, first,
    qd, own_ref, oth_ref, r1, r2, r3, sess,
    out, g0, g1, g2, g3,
    kc, vc, kt, vt, mask, s_scr, p_scr, d_scr, dk, dv,
):
    z, x, core = place[0], place[1], place[2]
    me = z * (X * CORE) + x * CORE + core
    base = me * ENTRIES
    scale = WIDTH**-0.5
    rows = 2 * BLOCK
    contract_last = (((1,), (1,)), ((), ()))

    @pl.loop(0, 2)
    def _(b):
        index = me * 2 + b
        sess_q = sess[pl.ds(index, 1), :]
        key_iota = lax.broadcasted_iota(jnp.int32, (BLOCK, BLOCK), 0)
        query_iota = lax.broadcasted_iota(jnp.int32, (BLOCK, BLOCK), 1)

        @pl.loop(0, LISTED)
        def _(l):
            e = base + b * LISTED + l
            block = ent[e]
            row = slab_row(block)
            sl = slot[e]
            away = lax.rem(x - owner_x(block) + X, X)
            same_core = owner_core(block) == core
            at = pl.ds(pl.multiple_of(l * BLOCK, BLOCK), BLOCK)

            def take(tile):
                kc[at, :] = tile[:BLOCK]
                vc[at, :] = tile[BLOCK:]

            @pl.when((away == 0) & same_core)
            def _():
                take(own_ref[row])

            @pl.when((away == 0) & jnp.logical_not(same_core))
            def _():
                take(oth_ref[row])

            for k, buf in ((1, r1), (2, r2), (3, r3)):

                @pl.when(away == k)
                def _():
                    take(buf[sl])

            t = kind[e]
            sess_k = jnp.broadcast_to(sess[pl.ds(block, 1), :], (BLOCK, BLOCK)).T
            needs = jnp.where((t == 0) | (t == 2), 1.0, 0.0)
            shift = jnp.where(t == 0, (block - index) * BLOCK, jnp.where(t == 3, 0, -(1 << 20)))
            seen = ((sess_k - sess_q) * needs == 0.0) & (key_iota + shift <= query_iota)
            mask[at, :] = jnp.where(seen, jnp.inf, -jnp.inf)

        for l in range(LISTED):
            at = slice(l * BLOCK, (l + 1) * BLOCK)
            kt[:, at] = kc[at, :].astype(jnp.float32).T.astype(jnp.bfloat16)
            vt[:, at] = vc[at, :].astype(jnp.float32).T.astype(jnp.bfloat16)

        for l in range(LISTED):
            dk[b * LISTED + l] = jnp.zeros((BLOCK, WIDTH), jnp.float32)
            dv[b * LISTED + l] = jnp.zeros((BLOCK, WIDTH), jnp.float32)

        @pl.loop(0, GROUP // 2)
        def _(pair):
            quarters = pl.ds(b * 4, 4)

            def both(what):
                return jnp.concatenate(
                    [
                        qd[quarters, what, 2 * pair + i].reshape(BLOCK, WIDTH)
                        for i in range(2)
                    ],
                    axis=0,
                )

            q = both(0)
            do = both(1)
            top = jnp.full((8, rows), -jnp.inf, jnp.float32)
            for l in range(LISTED):
                at = slice(l * BLOCK, (l + 1) * BLOCK)
                s = lax.dot_general(
                    kc[at, :], q, contract_last, preferred_element_type=jnp.float32
                )
                m = mask[at, :]
                s = jnp.minimum(s, jnp.concatenate([m, m], axis=1))
                s_scr[at, :] = s
                top = jnp.maximum(top, jnp.max(s.reshape(BLOCK // 8, 8, rows), axis=0))
            top = jnp.max(top, axis=0, keepdims=True)
            total = jnp.zeros((8, rows), jnp.float32)
            for l in range(LISTED):
                at = slice(l * BLOCK, (l + 1) * BLOCK)
                w = jnp.exp2((s_scr[at, :] - top) * (scale * LOG2E))
                s_scr[at, :] = w
                total = total + jnp.sum(w.reshape(BLOCK // 8, 8, rows), axis=0)
            inverse = 1.0 / jnp.sum(total, axis=0, keepdims=True)
            for l in range(LISTED):
                at = slice(l * BLOCK, (l + 1) * BLOCK)
                p_scr[at, :] = (s_scr[at, :] * inverse).astype(jnp.bfloat16)
            o_t = jnp.dot(vt[...], p_scr[...], preferred_element_type=jnp.float32)
            do_t = do.astype(jnp.float32).T
            o_round = o_t.astype(jnp.bfloat16).astype(jnp.float32)
            row_dot = jnp.sum(o_round * do_t, axis=0, keepdims=True)
            scaled = inverse * scale
            for l in range(LISTED):
                at = slice(l * BLOCK, (l + 1) * BLOCK)
                dp = lax.dot_general(
                    vc[at, :], do, contract_last, preferred_element_type=jnp.float32
                )
                ds = ((s_scr[at, :] * scaled) * (dp - row_dot)).astype(jnp.bfloat16)
                d_scr[at, :] = ds
                dk[b * LISTED + l] += jnp.dot(ds, q, preferred_element_type=jnp.float32)
                dv[b * LISTED + l] += jnp.dot(
                    p_scr[at, :], do, preferred_element_type=jnp.float32
                )
            dq_t = jnp.dot(kt[...], d_scr[...], preferred_element_type=jnp.float32)
            o = o_t.T.astype(jnp.bfloat16)
            dq = dq_t.T.astype(jnp.bfloat16)
            for i in range(2):
                at = slice(i * BLOCK, (i + 1) * BLOCK)
                out[quarters, 0, 2 * pair + i] = o[at].reshape(4, QUARTER, WIDTH)
                out[quarters, 1, 2 * pair + i] = dq[at].reshape(4, QUARTER, WIDTH)

    @pl.loop(LISTED, ENTRIES)
    def _(e):
        f = first[base + e]

        @pl.when(f != e)
        def _():
            dk[f] += dk[e]
            dv[f] += dv[e]

    @pl.loop(0, ENTRIES)
    def _(e):
        away = lax.rem(x - owner_x(ent[base + e]) + X, X)
        sl = slot[base + e]
        keep = first[base + e] == e
        for k, buf in ((0, g0), (1, g1), (2, g2), (3, g3)):

            @pl.when(keep & (away == k))
            def _():
                buf[sl, :BLOCK, :] = dk[e].astype(jnp.bfloat16)
                buf[sl, BLOCK:, :] = dv[e].astype(jnp.bfloat16)


def blocks(count):
    return jax.ShapeDtypeStruct((count, 2 * BLOCK, WIDTH), jnp.bfloat16)


def shift(array, axis, by):
    size = lax.axis_size(axis)
    return lax.ppermute(array, axis, [(i, (i + by) % size) for i in range(size)])


def params(mib):
    return pltpu.CompilerParams(vmem_limit_bytes=mib * MIB)


def exchange(array, axis):
    return lax.all_to_all(array, axis, split_axis=0, concat_axis=0, tiled=True)


def per_device(slots, queries, keys, values, output_gradient, kv_list, kv_type, session_id):
    place = jnp.stack(
        [lax.axis_index("z"), lax.axis_index("x"), lax.axis_index("core")]
    ).astype(jnp.int32)

    ent = kv_list.reshape(CTX, ENTRIES)
    order = jnp.arange(ENTRIES, dtype=jnp.int32)
    equal = ent[:, :, None] == ent[:, None, :]
    first = jnp.min(jnp.where(equal, order[None, None, :], ENTRIES), axis=2)
    fresh = first == order[None, :]
    column = owner_x(ent)
    before = (
        fresh[:, None, :]
        & (column[:, :, None] == column[:, None, :])
        & (order[None, None, :] < first[:, :, None])
    )
    slot = jnp.sum(before.astype(jnp.int32), axis=2)
    ent, first, slot = ent.reshape(-1), first.reshape(-1), slot.reshape(-1)
    kind = kv_type.reshape(-1)
    sess = session_id.astype(jnp.float32).reshape(-1, BLOCK)

    kv = jnp.stack([keys, values]).transpose(2, 0, 1, 3)
    kv = exchange(kv, "head")
    kv = kv.reshape(2, 4, 2, QUARTER, WIDTH).transpose(0, 2, 1, 3, 4)
    kv = kv.reshape(1, 2, 2 * BLOCK, WIDTH)
    own = exchange(jnp.broadcast_to(kv, (Z, 2, 2 * BLOCK, WIDTH)), "z")
    own = own.reshape(ENTRIES, 2 * BLOCK, WIDTH)
    other = shift(own, "core", 1)

    sends = pl.pallas_call(
        gather_kernel,
        out_shape=[blocks(slots)] * 3,
        in_specs=[SMEM] * 4 + [VMEM] * 2,
        out_specs=[VMEM] * 3,
        compiler_params=params(16),
    )(place, ent, slot, first, own, other)
    fetched = [shift(sends[k - 1], "x", k) for k in (1, 2, 3)]

    qd = jnp.stack([queries, output_gradient]).reshape(2, QUARTER, HEAD, GROUP, WIDTH)
    qd = qd.transpose(2, 0, 3, 1, 4)
    qd, own = lax.optimization_barrier((qd, own))
    qd = exchange(qd, "head")

    out, g0, g1, g2, g3 = pl.pallas_call(
        attend_kernel,
        out_shape=[jax.ShapeDtypeStruct((HEAD, 2, GROUP, QUARTER, WIDTH), jnp.bfloat16), blocks(ENTRIES)]
        + [blocks(slots)] * 3,
        in_specs=[SMEM] * 5 + [VMEM] * 7,
        out_specs=[VMEM] * 5,
        scratch_shapes=[
            pltpu.VMEM((LISTED * BLOCK, WIDTH), jnp.bfloat16),
            pltpu.VMEM((LISTED * BLOCK, WIDTH), jnp.bfloat16),
            pltpu.VMEM((WIDTH, LISTED * BLOCK), jnp.bfloat16),
            pltpu.VMEM((WIDTH, LISTED * BLOCK), jnp.bfloat16),
            pltpu.VMEM((LISTED * BLOCK, BLOCK), jnp.float32),
            pltpu.VMEM((LISTED * BLOCK, 2 * BLOCK), jnp.float32),
            pltpu.VMEM((LISTED * BLOCK, 2 * BLOCK), jnp.bfloat16),
            pltpu.VMEM((LISTED * BLOCK, 2 * BLOCK), jnp.bfloat16),
            pltpu.VMEM((ENTRIES, BLOCK, WIDTH), jnp.float32),
            pltpu.VMEM((ENTRIES, BLOCK, WIDTH), jnp.float32),
        ],
        compiler_params=params(40),
        cost_estimate=pl.CostEstimate(
            flops=5 * 2 * 2048 * 1024 * 128, bytes_accessed=8 * MIB, transcendentals=2048 * 1024
        ),
    )(place, ent, kind, slot, first, qd, own, other, *fetched, sess)

    returned = [shift(g, "x", -k) for k, g in ((1, g1), (2, g2), (3, g3))]
    out = exchange(out, "head")
    own_sum, other_sum = pl.pallas_call(
        scatter_kernel,
        out_shape=[blocks(ENTRIES)] * 2,
        in_specs=[SMEM] * 4 + [VMEM] * 4,
        out_specs=[VMEM] * 2,
        scratch_shapes=[pltpu.VMEM((2 * ENTRIES, 2 * BLOCK, WIDTH), jnp.float32)],
        compiler_params=params(24),
    )(place, ent, slot, first, g0, *returned)
    from_core = shift(other_sum, "core", 1)
    column_sum = (own_sum.astype(jnp.float32) + from_core.astype(jnp.float32)).astype(jnp.bfloat16)
    parts = exchange(column_sum.reshape(Z, 2, 2, BLOCK, WIDTH), "z")
    total = jnp.sum(parts.astype(jnp.float32), axis=0).astype(jnp.bfloat16)
    total = total.reshape(2, 2, 4, QUARTER, WIDTH).transpose(0, 2, 1, 3, 4)
    total = exchange(total.reshape(HEAD, 2, QUARTER, WIDTH), "head")
    total = total.transpose(1, 2, 0, 3)

    out = out.transpose(1, 3, 0, 2, 4).reshape(2, QUARTER, HEAD * GROUP, WIDTH)
    return out[0], out[1], total[0], total[1]


def solution(mesh):
    fine = Mesh(mesh.devices.reshape(Z, X, CORE, HEAD), ("z", "x", "core", "head"))
    split = P(("z", "x", "core", "head"), None, None)
    return jax.shard_map(
        functools.partial(per_device, MOST),
        mesh=fine,
        in_specs=(split,) * 4 + (P(),) * 3,
        out_specs=(split,) * 4,
        check_vma=False,
    )
```

time: 436 us -> 280 us (0.64); the launches traced: 431 us -> 279 us
  waiting for transfers between devices: 226 us -> 140 us
  local copies, waits for them, and re-layouts: 69.2 us -> 7.12 us
  Pallas kernels: 0 us -> 31.3 us
  blocking collectives: 18.8 us -> 47 us
  starting transfers between devices: 77.4 us -> 51 us
  matrix products: 25.3 us -> 0 us
  other arithmetic: 11.2 us -> 2.4 us
    all_to_all x11 -> x4, waiting for transfers between devices: 226 us -> 74.9 us  [exchange(): return lax.all_to_all(array, axis, split_axis=0, concat_axis=0, tiled=True)]
    ppermute x0 -> x8, waiting for transfers between devices: none -> 64.8 us  [shift(): lax.ppermute(array, axis, [(i, (i + by) % size) for i in range(size)])]
    all_to_all x11 -> x4, starting transfers between devices: 77.4 us -> 23.6 us  [exchange(): return lax.all_to_all(array, axis, split_axis=0, concat_axis=0, tiled=True)]
    pallas_call x0 -> x3, Pallas kernels: none -> 31.3 us  [the longest x1 25.2 us: per_device(): pl.pallas_call(attend_kernel, out_shape=[jax.ShapeDtypeStruct((HEAD, 2, G...]
    all_to_all x1 -> x2, blocking collectives: 18.8 us -> 47 us  [exchange(): return lax.all_to_all(array, axis, split_axis=0, concat_axis=0, tiled=True)]
    ppermute x0 -> x8, starting transfers between devices: none -> 27.4 us  [shift(): lax.ppermute(array, axis, [(i, (i + by) % size) for i in range(size)])]
    dot_general x18 -> x0, matrix products: 25.3 us -> none  [the longest x6 10.3 us: spread(): jnp.einsum('be,eqkd->bqkd', weights, parts, precision=lax.Precision.HIGHEST)]
    gather x8 -> x0, local copies, waits for them, and re-layouts: 23.3 us -> none  [the longest x2 12.3 us: block_mask(): session_id[key_pos]]
  transfers between devices with their start and end apart: 11 -> 12, of which waited for: 11 -> 11; matrix products, arithmetic and copies ran while one was open for 9% -> 2% of each run, Pallas kernels for 0% -> 1%
where the time goes in v1:
time: 280 us; the launch traced here: 279 us
  waiting for transfers between devices  140 us (50%)
  starting transfers between devices  51 us (18%)
  blocking collectives  47 us (17%)
  Pallas kernels  31.3 us (11%)
  local copies, waits for them, and re-layouts  7.12 us (3%)
    all_to_all x4, waiting for transfers between devices, exchange(): return lax.all_to_all(array, axis, split_axis=0, concat_axis=0, tiled=True)  74.9 us
    ppermute x8, waiting for transfers between devices, shift(): lax.ppermute(array, axis, [(i, (i + by) % size) for i in range(size)])  64.8 us
    all_to_all x2, blocking collectives, exchange(): return lax.all_to_all(array, axis, split_axis=0, concat_axis=0, tiled=True)  47 us
    ppermute x8, starting transfers between devices, shift(): lax.ppermute(array, axis, [(i, (i + by) % size) for i in range(size)])  27.4 us
    pallas_call x1, Pallas kernels, per_device(): pl.pallas_call(attend_kernel, out_shape=[jax.ShapeDtypeStruct((HEAD, 2, G...  25.2 us
    all_to_all x4, starting transfers between devices, exchange(): return lax.all_to_all(array, axis, split_axis=0, concat_axis=0, tiled=True)  23.6 us
  transfers between devices with their start and end apart: 12, of which 11 were waited for; matrix products, arithmetic and copies ran while one was open for 2% of the time, Pallas kernels for 1%

profile of v1, /device:TPU:1, one launch (start us, length us, event | category | flops | bytes accessed | tf_op | source)
XLA Modules:
  0.0 279.4 jit_solution(6794974077603472579)
XLA Ops:
  0.6 0.9 copy_bitcast_fusion
  1.5 15.4 %all_to_all.30 = bf16[8,2,32,128]{3,2,1,0:T(8,128)(2,1)S(1)} all-to-all(bf16[8,2,32,128]{3,2,1,0:T(8,128)(2,1)S(1)} %maximum_bitcast_fusion.1), channel_id=1, replica_groups=mesh['z'=8,'x'=4,'core'=2,'head'=8] {'head'}, dimensions={0} | all-to-all | bytes 262144 | tf_op jit(solution)/shard_map/all_to_all | solution.py:241
  16.9 1.2 broadcast_in_dim.32
  18.1 10.0 %all-to-all-start.1 = ((bf16[8,2,256,128]{3,2,1,0:T(8,128)(2,1)}), bf16[8,2,256,128]{3,2,1,0:T(8,128)(2,1)S(1)}, u32[]{:S(2)}, u32[]{:S(2)}) async-start(bf16[8,2,256,128]{3,2,1,0:T(8,128)(2,1)} %broadcast_in_dim.32), calls=%async_computation.1 | async-start | bytes 2097152 | tf_op jit(solution)/shard_map/all_to_all | solution.py:241
  28.9 26.6 %all-to-all-done.1 = bf16[8,2,256,128]{3,2,1,0:T(8,128)(2,1)S(1)} async-done(((bf16[8,2,256,128]{3,2,1,0:T(8,128)(2,1)}), bf16[8,2,256,128]{3,2,1,0:T(8,128)(2,1)S(1)}, u32[]{:S(2)}, u32[]{:S(2)}) %all-to-all-start.1) | async-done | bytes 1048608 | tf_op jit(solution)/shard_map/all_to_all | solution.py:241
  55.5 4.2 %collective-permute-start = (bf16[16,256,128]{2,1,0:T(8,128)(2,1)S(1)}, bf16[16,256,128]{2,1,0:T(8,128)(2,1)S(1)}, u32[]{:S(2)}, u32[]{:S(2)}) collective-permute-start(bf16[16,256,128]{2,1,0:T(8,128)(2,1)S(1)} %bitcast.30), channel_id=1, source_target_pairs={{0,8},{8,0},{1,9},{9,1},{2,10},{10,2},{3,11},{11,3},{4,12},{12,4},... | collective-permute-start | bytes 3145736 | tf_op jit(solution)/shard_map/ppermute | solution.py:233
  59.7 1.1 maximum_bitcast_fusion
  60.8 3.7 %all-to-all-start.2 = ((bf16[8,2,8,32,128]{4,3,2,1,0:T(8,128)(2,1)}), bf16[8,2,8,32,128]{4,3,2,1,0:T(8,128)(2,1)S(1)}, u32[]{:S(2)}, u32[]{:S(2)}) async-start(bf16[8,2,8,32,128]{4,3,2,1,0:T(8,128)(2,1)} %maximum_bitcast_fusion), calls=%async_computation.2 | async-start | bytes 2097152 | tf_op jit(solution)/shard_map/all_to_all | solution.py:241
  65.5 3.5 %shard_map.102 = (bf16[14,256,128]{2,1,0:T(8,128)(2,1)}, bf16[14,256,128]{2,1,0:T(8,128)(2,1)}, bf16[14,256,128]{2,1,0:T(8,128)(2,1)}) custom-call(s32[3]{0:T(128)S(1)} %pad_add_fusion.place, s32[1024]{0:T(1024)S(1)} %reshape_reshape.3.ent, s32[1024]{0:T(1024)S(1)} %reshape.80.slot, s32[1024]{0:T(1024)S(1)} %reshape.81.first, ...), custom_call_target="tpu_custom_call" | custom-call | tf_op jit(solution)/shard_map/pallas_call | solution.py:273
  69.0 3.1 %collective-permute-start.1 = (bf16[14,256,128]{2,1,0:T(8,128)(2,1)}, bf16[14,256,128]{2,1,0:T(8,128)(2,1)}, u32[]{:S(2)}, u32[]{:S(2)}) collective-permute-start(bf16[14,256,128]{2,1,0:T(8,128)(2,1)} %get-tuple-element.18), channel_id=1, source_target_pairs={{0,16},{16,32},{32,48},{48,0},{1,17},{17,33},{33,49},{49,1},{2,18}... | collective-permute-start | bytes 2752520 | tf_op jit(solution)/shard_map/ppermute | solution.py:233
  72.1 4.4 %collective-permute-start.2 = (bf16[14,256,128]{2,1,0:T(8,128)(2,1)}, bf16[14,256,128]{2,1,0:T(8,128)(2,1)}, u32[]{:S(2)}, u32[]{:S(2)}) collective-permute-start(bf16[14,256,128]{2,1,0:T(8,128)(2,1)} %get-tuple-element.19), channel_id=1, source_target_pairs={{0,32},{16,48},{32,0},{48,16},{1,33},{17,49},{33,1},{49,17},{2,34}... | collective-permute-start | bytes 2752520 | tf_op jit(solution)/shard_map/ppermute | solution.py:233
  76.5 3.1 %collective-permute-start.3 = (bf16[14,256,128]{2,1,0:T(8,128)(2,1)}, bf16[14,256,128]{2,1,0:T(8,128)(2,1)}, u32[]{:S(2)}, u32[]{:S(2)}) collective-permute-start(bf16[14,256,128]{2,1,0:T(8,128)(2,1)} %get-tuple-element.20), channel_id=1, source_target_pairs={{0,48},{16,0},{32,16},{48,32},{1,49},{17,1},{33,17},{49,33},{2,50}... | collective-permute-start | bytes 2752520 | tf_op jit(solution)/shard_map/ppermute | solution.py:233
  79.8 13.9 %all-to-all-done.2.qd = bf16[8,2,8,32,128]{4,3,2,1,0:T(8,128)(2,1)S(1)} async-done(((bf16[8,2,8,32,128]{4,3,2,1,0:T(8,128)(2,1)}), bf16[8,2,8,32,128]{4,3,2,1,0:T(8,128)(2,1)S(1)}, u32[]{:S(2)}, u32[]{:S(2)}) %all-to-all-start.2) | async-done | bytes 1048608 | tf_op jit(solution)/shard_map/all_to_all | solution.py:241
  94.4 20.7 %collective-permute-done.2.r2 = bf16[14,256,128]{2,1,0:T(8,128)(2,1)} collective-permute-done((bf16[14,256,128]{2,1,0:T(8,128)(2,1)}, bf16[14,256,128]{2,1,0:T(8,128)(2,1)}, u32[]{:S(2)}, u32[]{:S(2)}) %collective-permute-start.2) | collective-permute-done | bytes 917536 | tf_op jit(solution)/shard_map/ppermute | solution.py:233
  115.1 1.2 collective-permute-done.3.r3
  116.3 25.2 %shard_map.103 = (bf16[8,2,8,32,128]{4,3,2,1,0:T(8,128)(2,1)}, bf16[16,256,128]{2,1,0:T(8,128)(2,1)S(1)}, bf16[14,256,128]{2,1,0:T(8,128)(2,1)S(1)}, bf16[14,256...) custom-call(s32[3]{0:T(128)S(1)} %pad_add_fusion.place, s32[1024]{0:T(1024)S(1)} %reshape_reshape.3.ent, ...), custom_call_target="tpu_custom_call" | custom-call | flops 2684354560 | bytes 8388608 | tf_op jit(solution)/shard_map/pallas_call | solution.py:287
  141.5 4.9 %collective-permute-start.4 = (bf16[14,256,128]{2,1,0:T(8,128)(2,1)S(1)}, bf16[14,256,128]{2,1,0:T(8,128)(2,1)S(1)}, u32[]{:S(2)}, u32[]{:S(2)}) collective-permute-start(bf16[14,256,128]{2,1,0:T(8,128)(2,1)S(1)} %get-tuple-element.23), channel_id=1, source_target_pairs={{0,48},{16,0},{32,16},{48,32},{1,49},{17,1},{33,17},{49,33},{2,50}... | collective-permute-start | bytes 2752520 | tf_op jit(solution)/shard_map/ppermute | solution.py:233
  146.3 3.5 %collective-permute-start.5 = (bf16[14,256,128]{2,1,0:T(8,128)(2,1)S(1)}, bf16[14,256,128]{2,1,0:T(8,128)(2,1)S(1)}, u32[]{:S(2)}, u32[]{:S(2)}) collective-permute-start(bf16[14,256,128]{2,1,0:T(8,128)(2,1)S(1)} %get-tuple-element.24), channel_id=1, source_target_pairs={{0,32},{16,48},{32,0},{48,16},{1,33},{17,49},{33,1},{49,17},{2,34}... | collective-permute-start | bytes 2752520 | tf_op jit(solution)/shard_map/ppermute | solution.py:233
  149.8 1.9 collective-permute-start.6
  151.7 14.6 %collective-permute-done.4.g1 = bf16[14,256,128]{2,1,0:T(8,128)(2,1)S(1)} collective-permute-done((bf16[14,256,128]{2,1,0:T(8,128)(2,1)S(1)}, bf16[14,256,128]{2,1,0:T(8,128)(2,1)S(1)}, u32[]{:S(2)}, u32[]{:S(2)}) %collective-permute-start.4) | collective-permute-done | bytes 917536 | tf_op jit(solution)/shard_map/ppermute | solution.py:233
  166.4 4.5 %collective-permute-done.5.g2 = bf16[14,256,128]{2,1,0:T(8,128)(2,1)S(1)} collective-permute-done((bf16[14,256,128]{2,1,0:T(8,128)(2,1)S(1)}, bf16[14,256,128]{2,1,0:T(8,128)(2,1)S(1)}, u32[]{:S(2)}, u32[]{:S(2)}) %collective-permute-start.5) | collective-permute-done | bytes 917536 | tf_op jit(solution)/shard_map/ppermute | solution.py:233
  170.9 20.8 %collective-permute-done.6.g3 = bf16[14,256,128]{2,1,0:T(8,128)(2,1)S(1)} collective-permute-done((bf16[14,256,128]{2,1,0:T(8,128)(2,1)S(1)}, bf16[14,256,128]{2,1,0:T(8,128)(2,1)S(1)}, u32[]{:S(2)}, u32[]{:S(2)}) %collective-permute-start.6) | collective-permute-done | bytes 917536 | tf_op jit(solution)/shard_map/ppermute | solution.py:233
  191.7 2.6 shard_map.104
  194.3 2.4 collective-permute-start.7
  196.7 2.3 collective-permute-done.7
  199.2 31.6 %all_to_all.31 = bf16[8,2,2,128,128]{4,3,2,1,0:T(8,128)(2,1)S(1)} all-to-all(bf16[8,2,2,128,128]{4,3,2,1,0:T(8,128)(2,1)S(1)} %bitcast.33), channel_id=1, replica_groups=mesh['z'=8,'x'=4,'core'=2,'head'=8] {'z'}, dimensions={0} | all-to-all | bytes 2097152 | tf_op jit(solution)/shard_map/all_to_all | solution.py:241
  230.8 6.5 %all-to-all-start.3 = ((bf16[8,2,8,32,128]{4,3,2,1,0:T(8,128)(2,1)}), bf16[8,2,8,32,128]{4,3,2,1,0:T(8,128)(2,1)S(1)}, u32[]{:S(2)}, u32[]{:S(2)}) async-start(bf16[8,2,8,32,128]{4,3,2,1,0:T(8,128)(2,1)} %get-tuple-element.21), calls=%async_computation.3 | async-start | bytes 2097152 | tf_op jit(solution)/shard_map/all_to_all | solution.py:241
  238.2 28.4 %all-to-all-done.3 = bf16[8,2,8,32,128]{4,3,2,1,0:T(8,128)(2,1)S(1)} async-done(((bf16[8,2,8,32,128]{4,3,2,1,0:T(8,128)(2,1)}), bf16[8,2,8,32,128]{4,3,2,1,0:T(8,128)(2,1)S(1)}, u32[]{:S(2)}, u32[]{:S(2)}) %all-to-all-start.3) | async-done | bytes 1048608 | tf_op jit(solution)/shard_map/all_to_all | solution.py:241
  266.6 3.4 %all-to-all-start.5 = ((bf16[8,2,32,128]{3,2,1,0:T(8,128)(2,1)}), bf16[8,2,32,128]{3,2,1,0:T(8,128)(2,1)S(1)}, u32[]{:S(2)}, u32[]{:S(2)}) async-start(bf16[8,2,32,128]{3,2,1,0:T(8,128)(2,1)} %bitcast.18), calls=%async_computation.5 | async-start | bytes 262144 | tf_op jit(solution)/shard_map/all_to_all | solution.py:241
  270.1 1.0 copy.51
  271.1 1.0 copy.50
  272.1 6.0 %all-to-all-done.5 = bf16[8,2,32,128]{3,2,1,0:T(8,128)(2,1)S(1)} async-done(((bf16[8,2,32,128]{3,2,1,0:T(8,128)(2,1)}), bf16[8,2,32,128]{3,2,1,0:T(8,128)(2,1)S(1)}, u32[]{:S(2)}, u32[]{:S(2)}) %all-to-all-start.5) | async-done | bytes 131104 | tf_op jit(solution)/shard_map/all_to_all | solution.py:241
  (41 shorter events, 5.1 us)
Async XLA Ops:
  18.1 10.0 %copy-start = (bf16[32,64,128]{2,1,0:T(8,128)(2,1)S(1)}, bf16[32,64,128]{2,1,0:T(8,128)(2,1)}, u32[]{:S(2)}) copy-start(bf16[32,64,128]{2,1,0:T(8,128)(2,1)} %param.7) | copy-start | bytes 1572868
  18.1 10.4 %copy-start.1 = (bf16[32,64,128]{2,1,0:T(8,128)(2,1)S(1)}, bf16[32,64,128]{2,1,0:T(8,128)(2,1)}, u32[]{:S(2)}) copy-start(bf16[32,64,128]{2,1,0:T(8,128)(2,1)} %param.10) | copy-start | bytes 1572868
  18.1 37.3 %all-to-all-start.1 = ((bf16[8,2,256,128]{3,2,1,0:T(8,128)(2,1)}), bf16[8,2,256,128]{3,2,1,0:T(8,128)(2,1)S(1)}, u32[]{:S(2)}, u32[]{:S(2)}) async-start(bf16[8,2,256,128]{3,2,1,0:T(8,128)(2,1)} %broadcast_in_dim.32), calls=%async_computation.1 | async-start | bytes 2097152 | tf_op jit(solution)/shard_map/all_to_all | solution.py:241
  55.5 10.0 %collective-permute-start = (bf16[16,256,128]{2,1,0:T(8,128)(2,1)S(1)}, bf16[16,256,128]{2,1,0:T(8,128)(2,1)S(1)}, u32[]{:S(2)}, u32[]{:S(2)}) collective-permute-start(bf16[16,256,128]{2,1,0:T(8,128)(2,1)S(1)} %bitcast.30), channel_id=1, source_target_pairs={{0,8},{8,0},{1,9},{9,1},{2,10},{10,2},{3,11},{11,3},{4,12},{12,4},... | collective-permute-start | bytes 3145736 | tf_op jit(solution)/shard_map/ppermute | solution.py:233
  60.8 3.7 %copy-start.3 = (s32[128,8]{0,1:T(8,128)S(1)}, s32[128,8]{0,1:T(8,128)}, u32[]{:S(2)}) copy-start(s32[128,8]{0,1:T(8,128)} %param.11) | copy-start | bytes 12292
  60.8 32.9 %all-to-all-start.2 = ((bf16[8,2,8,32,128]{4,3,2,1,0:T(8,128)(2,1)}), bf16[8,2,8,32,128]{4,3,2,1,0:T(8,128)(2,1)S(1)}, u32[]{:S(2)}, u32[]{:S(2)}) async-start(bf16[8,2,8,32,128]{4,3,2,1,0:T(8,128)(2,1)} %maximum_bitcast_fusion), calls=%async_computation.2 | async-start | bytes 2097152 | tf_op jit(solution)/shard_map/all_to_all | solution.py:241
  65.5 14.1 %copy-start.4 = (s32[128,8]{0,1:T(8,128)S(1)}, s32[128,8]{0,1:T(8,128)}, u32[]{:S(2)}) copy-start(s32[128,8]{0,1:T(8,128)} %param.12) | copy-start | bytes 12292
  65.5 14.3 %copy-start.2 = (s32[16384]{0:T(1024)S(1)}, s32[16384]{0:T(1024)}, u32[]{:S(2)}) copy-start(s32[16384]{0:T(1024)} %param.13) | copy-start | bytes 196612
  69.0 25.4 %collective-permute-start.1 = (bf16[14,256,128]{2,1,0:T(8,128)(2,1)}, bf16[14,256,128]{2,1,0:T(8,128)(2,1)}, u32[]{:S(2)}, u32[]{:S(2)}) collective-permute-start(bf16[14,256,128]{2,1,0:T(8,128)(2,1)} %get-tuple-element.18), channel_id=1, source_target_pairs={{0,16},{16,32},{32,48},{48,0},{1,17},{17,33},{33,49},{49,1},{2,18}... | collective-permute-start | bytes 2752520 | tf_op jit(solution)/shard_map/ppermute | solution.py:233
  72.1 42.9 %collective-permute-start.2 = (bf16[14,256,128]{2,1,0:T(8,128)(2,1)}, bf16[14,256,128]{2,1,0:T(8,128)(2,1)}, u32[]{:S(2)}, u32[]{:S(2)}) collective-permute-start(bf16[14,256,128]{2,1,0:T(8,128)(2,1)} %get-tuple-element.19), channel_id=1, source_target_pairs={{0,32},{16,48},{32,0},{48,16},{1,33},{17,49},{33,1},{49,17},{2,34}... | collective-permute-start | bytes 2752520 | tf_op jit(solution)/shard_map/ppermute | solution.py:233
  76.5 39.8 %collective-permute-start.3 = (bf16[14,256,128]{2,1,0:T(8,128)(2,1)}, bf16[14,256,128]{2,1,0:T(8,128)(2,1)}, u32[]{:S(2)}, u32[]{:S(2)}) collective-permute-start(bf16[14,256,128]{2,1,0:T(8,128)(2,1)} %get-tuple-element.20), channel_id=1, source_target_pairs={{0,48},{16,0},{32,16},{48,32},{1,49},{17,1},{33,17},{49,33},{2,50}... | collective-permute-start | bytes 2752520 | tf_op jit(solution)/shard_map/ppermute | solution.py:233
  141.5 24.9 %collective-permute-start.4 = (bf16[14,256,128]{2,1,0:T(8,128)(2,1)S(1)}, bf16[14,256,128]{2,1,0:T(8,128)(2,1)S(1)}, u32[]{:S(2)}, u32[]{:S(2)}) collective-permute-start(bf16[14,256,128]{2,1,0:T(8,128)(2,1)S(1)} %get-tuple-element.23), channel_id=1, source_target_pairs={{0,48},{16,0},{32,16},{48,32},{1,49},{17,1},{33,17},{49,33},{2,50}... | collective-permute-start | bytes 2752520 | tf_op jit(solution)/shard_map/ppermute | solution.py:233
  146.3 24.5 %collective-permute-start.5 = (bf16[14,256,128]{2,1,0:T(8,128)(2,1)S(1)}, bf16[14,256,128]{2,1,0:T(8,128)(2,1)S(1)}, u32[]{:S(2)}, u32[]{:S(2)}) collective-permute-start(bf16[14,256,128]{2,1,0:T(8,128)(2,1)S(1)} %get-tuple-element.24), channel_id=1, source_target_pairs={{0,32},{16,48},{32,0},{48,16},{1,33},{17,49},{33,1},{49,17},{2,34}... | collective-permute-start | bytes 2752520 | tf_op jit(solution)/shard_map/ppermute | solution.py:233
  149.8 41.9 %collective-permute-start.6 = (bf16[14,256,128]{2,1,0:T(8,128)(2,1)S(1)}, bf16[14,256,128]{2,1,0:T(8,128)(2,1)S(1)}, u32[]{:S(2)}, u32[]{:S(2)}) collective-permute-start(bf16[14,256,128]{2,1,0:T(8,128)(2,1)S(1)} %get-tuple-element.25), channel_id=1, source_target_pairs={{0,16},{16,32},{32,48},{48,0},{1,17},{17,33},{33,49},{49,1},{2,18}... | collective-permute-start | bytes 2752520 | tf_op jit(solution)/shard_map/ppermute | solution.py:233
  194.3 4.7 %collective-permute-start.7 = (bf16[16,256,128]{2,1,0:T(8,128)(2,1)S(1)}, bf16[16,256,128]{2,1,0:T(8,128)(2,1)S(1)}, u32[]{:S(2)}, u32[]{:S(2)}) collective-permute-start(bf16[16,256,128]{2,1,0:T(8,128)(2,1)S(1)} %get-tuple-element.27), channel_id=1, source_target_pairs={{0,8},{8,0},{1,9},{9,1},{2,10},{10,2},{3,11},{11,3},{4,12},{12,4},... | collective-permute-start | bytes 3145736 | tf_op jit(solution)/shard_map/ppermute | solution.py:233
  230.8 35.8 %all-to-all-start.3 = ((bf16[8,2,8,32,128]{4,3,2,1,0:T(8,128)(2,1)}), bf16[8,2,8,32,128]{4,3,2,1,0:T(8,128)(2,1)S(1)}, u32[]{:S(2)}, u32[]{:S(2)}) async-start(bf16[8,2,8,32,128]{4,3,2,1,0:T(8,128)(2,1)} %get-tuple-element.21), calls=%async_computation.3 | async-start | bytes 2097152 | tf_op jit(solution)/shard_map/all_to_all | solution.py:241
  266.6 11.4 %all-to-all-start.5 = ((bf16[8,2,32,128]{3,2,1,0:T(8,128)(2,1)}), bf16[8,2,32,128]{3,2,1,0:T(8,128)(2,1)S(1)}, u32[]{:S(2)}, u32[]{:S(2)}) async-start(bf16[8,2,32,128]{3,2,1,0:T(8,128)(2,1)} %bitcast.18), calls=%async_computation.5 | async-start | bytes 262144 | tf_op jit(solution)/shard_map/all_to_all | solution.py:241

commit v2 on v1

--- a/solution.py
+++ b/solution.py
@@ -16,6 +16,7 @@
 GROUP = 8
 QUARTER = 32
 MOST = 14
+FEW = 9
 LOG2E = 1.4426950408889634
 MIB = 1 << 20
 
@@ -109,8 +110,9 @@
             at = pl.ds(pl.multiple_of(l * BLOCK, BLOCK), BLOCK)
 
             def take(tile):
-                kc[at, :] = tile[:BLOCK]
-                vc[at, :] = tile[BLOCK:]
+                tile = tile.reshape(4, 2, QUARTER, WIDTH)
+                kc[at, :] = tile[:, 0].reshape(BLOCK, WIDTH)
+                vc[at, :] = tile[:, 1].reshape(BLOCK, WIDTH)
 
             @pl.when((away == 0) & same_core)
             def _():
@@ -220,8 +222,9 @@
 
             @pl.when(keep & (away == k))
             def _():
-                buf[sl, :BLOCK, :] = dk[e].astype(jnp.bfloat16)
-                buf[sl, BLOCK:, :] = dv[e].astype(jnp.bfloat16)
+                parts = [dk[e].reshape(4, 1, QUARTER, WIDTH), dv[e].reshape(4, 1, QUARTER, WIDTH)]
+                tile = jnp.concatenate(parts, axis=1).astype(jnp.bfloat16)
+                buf[sl] = tile.reshape(2 * BLOCK, WIDTH)
 
 
 def blocks(count):
@@ -241,35 +244,9 @@
     return lax.all_to_all(array, axis, split_axis=0, concat_axis=0, tiled=True)
 
 
-def per_device(slots, queries, keys, values, output_gradient, kv_list, kv_type, session_id):
-    place = jnp.stack(
-        [lax.axis_index("z"), lax.axis_index("x"), lax.axis_index("core")]
-    ).astype(jnp.int32)
-
-    ent = kv_list.reshape(CTX, ENTRIES)
-    order = jnp.arange(ENTRIES, dtype=jnp.int32)
-    equal = ent[:, :, None] == ent[:, None, :]
-    first = jnp.min(jnp.where(equal, order[None, None, :], ENTRIES), axis=2)
-    fresh = first == order[None, :]
-    column = owner_x(ent)
-    before = (
-        fresh[:, None, :]
-        & (column[:, :, None] == column[:, None, :])
-        & (order[None, None, :] < first[:, :, None])
-    )
-    slot = jnp.sum(before.astype(jnp.int32), axis=2)
-    ent, first, slot = ent.reshape(-1), first.reshape(-1), slot.reshape(-1)
-    kind = kv_type.reshape(-1)
-    sess = session_id.astype(jnp.float32).reshape(-1, BLOCK)
-
-    kv = jnp.stack([keys, values]).transpose(2, 0, 1, 3)
-    kv = exchange(kv, "head")
-    kv = kv.reshape(2, 4, 2, QUARTER, WIDTH).transpose(0, 2, 1, 3, 4)
-    kv = kv.reshape(1, 2, 2 * BLOCK, WIDTH)
-    own = exchange(jnp.broadcast_to(kv, (Z, 2, 2 * BLOCK, WIDTH)), "z")
-    own = own.reshape(ENTRIES, 2 * BLOCK, WIDTH)
+def between(slots, place, tables, own, queries, output_gradient, sess):
+    ent, kind, slot, first = tables
     other = shift(own, "core", 1)
-
     sends = pl.pallas_call(
         gather_kernel,
         out_shape=[blocks(slots)] * 3,
@@ -280,9 +257,7 @@
     fetched = [shift(sends[k - 1], "x", k) for k in (1, 2, 3)]
 
     qd = jnp.stack([queries, output_gradient]).reshape(2, QUARTER, HEAD, GROUP, WIDTH)
-    qd = qd.transpose(2, 0, 3, 1, 4)
-    qd, own = lax.optimization_barrier((qd, own))
-    qd = exchange(qd, "head")
+    qd = exchange(qd.transpose(2, 0, 3, 1, 4), "head")
 
     out, g0, g1, g2, g3 = pl.pallas_call(
         attend_kernel,
@@ -310,6 +285,7 @@
 
     returned = [shift(g, "x", -k) for k, g in ((1, g1), (2, g2), (3, g3))]
     out = exchange(out, "head")
+    *returned, out = lax.optimization_barrier((*returned, out))
     own_sum, other_sum = pl.pallas_call(
         scatter_kernel,
         out_shape=[blocks(ENTRIES)] * 2,
@@ -318,12 +294,47 @@
         scratch_shapes=[pltpu.VMEM((2 * ENTRIES, 2 * BLOCK, WIDTH), jnp.float32)],
         compiler_params=params(24),
     )(place, ent, slot, first, g0, *returned)
+    return out, own_sum, other_sum
+
+
+def per_device(queries, keys, values, output_gradient, kv_list, kv_type, session_id):
+    where = [lax.axis_index(axis) for axis in ("z", "x", "core")]
+    place = jnp.stack(where).astype(jnp.int32)
+
+    ent = kv_list.reshape(CTX, ENTRIES)
+    order = jnp.arange(ENTRIES, dtype=jnp.int32)
+    equal = ent[:, :, None] == ent[:, None, :]
+    first = jnp.min(jnp.where(equal, order[None, None, :], ENTRIES), axis=2)
+    fresh = first == order[None, :]
+    column = owner_x(ent)
+    before = (
+        fresh[:, None, :]
+        & (column[:, :, None] == column[:, None, :])
+        & (order[None, None, :] < first[:, :, None])
+    )
+    slot = jnp.sum(before.astype(jnp.int32), axis=2)
+    home = lax.rem(jnp.arange(CTX, dtype=jnp.int32) // CORE, X)
+    most = jnp.max(jnp.where(column == home[:, None], 0, slot + 1))
+    tables = (ent.reshape(-1), kv_type.reshape(-1), slot.reshape(-1), first.reshape(-1))
+    sess = session_id.astype(jnp.float32).reshape(-1, BLOCK)
+
+    kv = jnp.stack([keys, values]).transpose(2, 0, 1, 3)
+    kv = jnp.broadcast_to(kv, (Z, HEAD, 2, QUARTER, WIDTH))
+    own = exchange(kv.reshape(Z * HEAD, 2, QUARTER, WIDTH), ("z", "head"))
+    own = own.reshape(ENTRIES, 2 * BLOCK, WIDTH)
+
+    out, own_sum, other_sum = lax.cond(
+        most <= FEW,
+        functools.partial(between, FEW),
+        functools.partial(between, MOST),
+        place, tables, own, queries, output_gradient, sess,
+    )
+
     from_core = shift(other_sum, "core", 1)
     column_sum = (own_sum.astype(jnp.float32) + from_core.astype(jnp.float32)).astype(jnp.bfloat16)
-    parts = exchange(column_sum.reshape(Z, 2, 2, BLOCK, WIDTH), "z")
+    parts = exchange(column_sum.reshape(Z * HEAD, 2, QUARTER, WIDTH), ("z", "head"))
+    parts = parts.reshape(Z, HEAD, 2, QUARTER, WIDTH)
     total = jnp.sum(parts.astype(jnp.float32), axis=0).astype(jnp.bfloat16)
-    total = total.reshape(2, 2, 4, QUARTER, WIDTH).transpose(0, 2, 1, 3, 4)
-    total = exchange(total.reshape(HEAD, 2, QUARTER, WIDTH), "head")
     total = total.transpose(1, 2, 0, 3)
 
     out = out.transpose(1, 3, 0, 2, 4).reshape(2, QUARTER, HEAD * GROUP, WIDTH)
@@ -334,7 +345,7 @@
     fine = Mesh(mesh.devices.reshape(Z, X, CORE, HEAD), ("z", "x", "core", "head"))
     split = P(("z", "x", "core", "head"), None, None)
     return jax.shard_map(
-        functools.partial(per_device, MOST),
+        per_device,
         mesh=fine,
         in_specs=(split,) * 4 + (P(),) * 3,
         out_specs=(split,) * 4,

time: 280 us -> 219 us (0.78)
  blocking collectives: 47 us -> 0 us
  waiting for transfers between devices: 140 us -> 100 us
  starting transfers between devices: 51 us -> 66.4 us
  local copies, waits for them, and re-layouts: 7.12 us -> 14.7 us
    all_to_all x2 -> x0, blocking collectives: 47 us -> none  [exchange(): return lax.all_to_all(array, axis, split_axis=0, concat_axis=0, tiled=True)]
    all_to_all x4, waiting for transfers between devices: 74.9 us -> 49.4 us  [exchange(): return lax.all_to_all(array, axis, split_axis=0, concat_axis=0, tiled=True)]
    all_to_all x4, starting transfers between devices: 23.6 us -> 38.4 us  [exchange(): return lax.all_to_all(array, axis, split_axis=0, concat_axis=0, tiled=True)]
    ppermute x8, waiting for transfers between devices: 64.8 us -> 51 us  [shift(): lax.ppermute(array, axis, [(i, (i + by) % size) for i in range(size)])]
    cond x0 -> x18, local copies, waits for them, and re-layouts: none -> 7.43 us
  transfers between devices with their start and end apart: 12 -> 12, of which waited for: 11 -> 10; matrix products, arithmetic and copies ran while one was open for 2% -> 2% of each run, Pallas kernels for 1% -> 1%
where the time goes in v2:
time: 219 us; the launch traced here: 217 us
  waiting for transfers between devices  100 us (46%)
  starting transfers between devices  66.4 us (30%)
  Pallas kernels  29.4 us (13%)
  local copies, waits for them, and re-layouts  14.7 us (7%)
  other arithmetic  4.38 us (2%)
    ppermute x8, waiting for transfers between devices, shift(): lax.ppermute(array, axis, [(i, (i + by) % size) for i in range(size)])  51 us
    all_to_all x4, waiting for transfers between devices, exchange(): return lax.all_to_all(array, axis, split_axis=0, concat_axis=0, tiled=True)  49.4 us
    all_to_all x4, starting transfers between devices, exchange(): return lax.all_to_all(array, axis, split_axis=0, concat_axis=0, tiled=True)  38.4 us
    ppermute x8, starting transfers between devices, shift(): lax.ppermute(array, axis, [(i, (i + by) % size) for i in range(size)])  28 us
    pallas_call x1, Pallas kernels, between(): pl.pallas_call(attend_kernel, out_shape=[jax.ShapeDtypeStruct((HEAD, 2, G...  24.7 us
    cond x18, local copies, waits for them, and re-layouts  7.43 us
  transfers between devices with their start and end apart: 12, of which 10 were waited for; matrix products, arithmetic and copies ran while one was open for 2% of the time, Pallas kernels for 1%

profile of v2, /device:TPU:1, one launch (start us, length us, event | category | flops | bytes accessed | tf_op | source)
XLA Modules:
  0.0 216.8 jit_solution(13887440737495350504)
XLA Ops:
  1.5 1.3 broadcast_in_dim.30
  2.8 17.3 %all-to-all-start.4 = ((bf16[64,2,32,128]{3,2,1,0:T(8,128)(2,1)}), bf16[64,2,32,128]{3,2,1,0:T(8,128)(2,1)S(1)}, u32[]{:S(2)}, u32[]{:S(2)}) async-start(bf16[64,2,32,128]{3,2,1,0:T(8,128)(2,1)} %bitcast.9), calls=%async_computation.4 | async-start | bytes 2097152 | tf_op jit(solution)/shard_map/all_to_all | solution.py:244
  23.1 24.4 %all-to-all-done.4 = bf16[64,2,32,128]{3,2,1,0:T(8,128)(2,1)S(1)} async-done(((bf16[64,2,32,128]{3,2,1,0:T(8,128)(2,1)}), bf16[64,2,32,128]{3,2,1,0:T(8,128)(2,1)S(1)}, u32[]{:S(2)}, u32[]{:S(2)}) %all-to-all-start.4) | async-done | bytes 1048608 | tf_op jit(solution)/shard_map/all_to_all | solution.py:244
  47.5 125.4 %conditional.1 = (bf16[8,2,8,32,128]{4,3,2,1,0:T(8,128)(2,1)}, bf16[16,256,128]{2,1,0:T(8,128)(2,1)S(1)}, bf16[16,256,128]{2,1,0:T(8,128)(2,1)S(1)}) conditional(s32[]{:T(128)} %convert_element_type.21, (bf16[32,64,128]{2,1,0:T(8,128)(2,1)S(1)}, bf16[32,64,128]{2,1,0:T(8,128)(2,1)S(1)}, bf16[16,256,128]{2,1,0:T(8,128)(2,1)S(1)}, s32[3]{0:T(128)S(1)}, ...), branch_computations={%region_3.4_spmd, %region_4.5_spmd} | conditional | flops 2684878848 | bytes 75498064 | solution.py:326
  48.2 1.1 maximum_bitcast_fusion.1
  49.3 5.4 %all-to-all-start.2 = ((bf16[8,2,8,32,128]{4,3,2,1,0:T(8,128)(2,1)}), bf16[8,2,8,32,128]{4,3,2,1,0:T(8,128)(2,1)S(1)}, u32[]{:S(2)}, u32[]{:S(2)}) async-start(bf16[8,2,8,32,128]{4,3,2,1,0:T(8,128)(2,1)} %maximum_bitcast_fusion.1), calls=%async_computation.2 | async-start | bytes 2097152 | tf_op jit(solution)/shard_map/cond/branch_1_fun/all_to_all | solution.py:244
  54.7 4.5 %collective-permute-start.7 = (bf16[16,256,128]{2,1,0:T(8,128)(2,1)S(1)}, bf16[16,256,128]{2,1,0:T(8,128)(2,1)S(1)}, u32[]{:S(2)}, u32[]{:S(2)}) collective-permute-start(bf16[16,256,128]{2,1,0:T(8,128)(2,1)S(1)} %get-tuple-element.66.own_ref), channel_id=1, source_target_pairs={{0,8},{8,0},{1,9},{9,1},{2,10},{10,2},{3,11},{11,3},{4,12},{12,4},... | collective-permute-start | bytes 3145736 | tf_op jit(solution)/shard_map/cond/branch_1_fun/ppermute | solution.py:236
  59.2 2.3 %collective-permute-done.7.oth_ref = bf16[16,256,128]{2,1,0:T(8,128)(2,1)S(1)} collective-permute-done((bf16[16,256,128]{2,1,0:T(8,128)(2,1)S(1)}, bf16[16,256,128]{2,1,0:T(8,128)(2,1)S(1)}, u32[]{:S(2)}, u32[]{:S(2)}) %collective-permute-start.7) | collective-permute-done | bytes 1048608 | tf_op jit(solution)/shard_map/cond/branch_1_fun/ppermute | solution.py:236
  61.5 2.0 branch_1_fun.3
  63.5 3.1 %collective-permute-start.8 = (bf16[9,256,128]{2,1,0:T(8,128)(2,1)S(1)}, bf16[9,256,128]{2,1,0:T(8,128)(2,1)S(1)}, u32[]{:S(2)}, u32[]{:S(2)}) collective-permute-start(bf16[9,256,128]{2,1,0:T(8,128)(2,1)S(1)} %get-tuple-element.67), channel_id=1, source_target_pairs={{0,16},{16,32},{32,48},{48,0},{1,17},{17,33},{33,49},{49,1},{2,18}... | collective-permute-start | bytes 1769480 | tf_op jit(solution)/shard_map/cond/branch_1_fun/ppermute | solution.py:236
  66.7 4.4 %collective-permute-start.9 = (bf16[9,256,128]{2,1,0:T(8,128)(2,1)S(1)}, bf16[9,256,128]{2,1,0:T(8,128)(2,1)S(1)}, u32[]{:S(2)}, u32[]{:S(2)}) collective-permute-start(bf16[9,256,128]{2,1,0:T(8,128)(2,1)S(1)} %get-tuple-element.68), channel_id=1, source_target_pairs={{0,32},{16,48},{32,0},{48,16},{1,33},{17,49},{33,1},{49,17},{2,34}... | collective-permute-start | bytes 1769480 | tf_op jit(solution)/shard_map/cond/branch_1_fun/ppermute | solution.py:236
  71.0 3.1 %collective-permute-start.10 = (bf16[9,256,128]{2,1,0:T(8,128)(2,1)S(1)}, bf16[9,256,128]{2,1,0:T(8,128)(2,1)S(1)}, u32[]{:S(2)}, u32[]{:S(2)}) collective-permute-start(bf16[9,256,128]{2,1,0:T(8,128)(2,1)S(1)} %get-tuple-element.69), channel_id=1, source_target_pairs={{0,48},{16,0},{32,16},{48,32},{1,49},{17,1},{33,17},{49,33},{2,50}... | collective-permute-start | bytes 1769480 | tf_op jit(solution)/shard_map/cond/branch_1_fun/ppermute | solution.py:236
  74.1 7.1 %collective-permute-done.8.r1 = bf16[9,256,128]{2,1,0:T(8,128)(2,1)S(1)} collective-permute-done((bf16[9,256,128]{2,1,0:T(8,128)(2,1)S(1)}, bf16[9,256,128]{2,1,0:T(8,128)(2,1)S(1)}, u32[]{:S(2)}, u32[]{:S(2)}) %collective-permute-start.8) | collective-permute-done | bytes 589856 | tf_op jit(solution)/shard_map/cond/branch_1_fun/ppermute | solution.py:236
  82.0 12.8 %collective-permute-done.9.r2 = bf16[9,256,128]{2,1,0:T(8,128)(2,1)S(1)} collective-permute-done((bf16[9,256,128]{2,1,0:T(8,128)(2,1)S(1)}, bf16[9,256,128]{2,1,0:T(8,128)(2,1)S(1)}, u32[]{:S(2)}, u32[]{:S(2)}) %collective-permute-start.9) | collective-permute-done | bytes 589856 | tf_op jit(solution)/shard_map/cond/branch_1_fun/ppermute | solution.py:236
  96.9 1.1 copy-done.9
  97.9 1.1 copy-done.12
  100.1 24.7 %branch_1_fun.4 = (bf16[8,2,8,32,128]{4,3,2,1,0:T(8,128)(2,1)S(1)}, bf16[16,256,128]{2,1,0:T(8,128)(2,1)S(1)}, bf16[9,256,128]{2,1,0:T(8,128)(2,1)}, bf16[9,256,...) custom-call(s32[3]{0:T(128)S(1)} %get-tuple-element.59.place, s32[1024]{0:T(1024)S(1)} %get-tuple-element.60.ent, ...), custom_call_target="tpu_custom_call" | custom-call | flops 2684354560 | bytes 8388608 | tf_op jit(solution)/shard_map/cond/branch_1_fun/pallas_call | solution.py:262
  126.6 7.0 %all-to-all-start.3 = ((bf16[8,2,8,32,128]{4,3,2,1,0:T(8,128)(2,1)}), bf16[8,2,8,32,128]{4,3,2,1,0:T(8,128)(2,1)}, u32[]{:S(2)}, u32[]{:S(2)}) async-start(bf16[8,2,8,32,128]{4,3,2,1,0:T(8,128)(2,1)} %copy-done.1), calls=%async_computation.3 | async-start | bytes 2097152 | tf_op jit(solution)/shard_map/cond/branch_1_fun/all_to_all | solution.py:244
  133.5 5.2 %collective-permute-start.11 = (bf16[9,256,128]{2,1,0:T(8,128)(2,1)}, bf16[9,256,128]{2,1,0:T(8,128)(2,1)S(1)}, u32[]{:S(2)}, u32[]{:S(2)}) collective-permute-start(bf16[9,256,128]{2,1,0:T(8,128)(2,1)} %get-tuple-element.71), channel_id=1, source_target_pairs={{0,48},{16,0},{32,16},{48,32},{1,49},{17,1},{33,17},{49,33},{2,50}... | collective-permute-start | bytes 1769480 | tf_op jit(solution)/shard_map/cond/branch_1_fun/ppermute | solution.py:236
  138.8 3.4 %collective-permute-start.12 = (bf16[9,256,128]{2,1,0:T(8,128)(2,1)}, bf16[9,256,128]{2,1,0:T(8,128)(2,1)S(1)}, u32[]{:S(2)}, u32[]{:S(2)}) collective-permute-start(bf16[9,256,128]{2,1,0:T(8,128)(2,1)} %get-tuple-element.72), channel_id=1, source_target_pairs={{0,32},{16,48},{32,0},{48,16},{1,33},{17,49},{33,1},{49,17},{2,34}... | collective-permute-start | bytes 1769480 | tf_op jit(solution)/shard_map/cond/branch_1_fun/ppermute | solution.py:236
  142.2 1.9 collective-permute-start.13
  144.1 7.6 %collective-permute-done.11.g1 = bf16[9,256,128]{2,1,0:T(8,128)(2,1)S(1)} collective-permute-done((bf16[9,256,128]{2,1,0:T(8,128)(2,1)}, bf16[9,256,128]{2,1,0:T(8,128)(2,1)S(1)}, u32[]{:S(2)}, u32[]{:S(2)}) %collective-permute-start.11) | collective-permute-done | bytes 589856 | tf_op jit(solution)/shard_map/cond/branch_1_fun/ppermute | solution.py:236
  151.7 4.5 %collective-permute-done.12.g2 = bf16[9,256,128]{2,1,0:T(8,128)(2,1)S(1)} collective-permute-done((bf16[9,256,128]{2,1,0:T(8,128)(2,1)}, bf16[9,256,128]{2,1,0:T(8,128)(2,1)S(1)}, u32[]{:S(2)}, u32[]{:S(2)}) %collective-permute-start.12) | collective-permute-done | bytes 589856 | tf_op jit(solution)/shard_map/cond/branch_1_fun/ppermute | solution.py:236
  156.2 14.1 %collective-permute-done.13.g3 = bf16[9,256,128]{2,1,0:T(8,128)(2,1)S(1)} collective-permute-done((bf16[9,256,128]{2,1,0:T(8,128)(2,1)}, bf16[9,256,128]{2,1,0:T(8,128)(2,1)S(1)}, u32[]{:S(2)}, u32[]{:S(2)}) %collective-permute-start.13) | collective-permute-done | bytes 589856 | tf_op jit(solution)/shard_map/cond/branch_1_fun/ppermute | solution.py:236
  170.3 2.6 %branch_1_fun.5 = (bf16[16,256,128]{2,1,0:T(8,128)(2,1)S(1)}, bf16[16,256,128]{2,1,0:T(8,128)(2,1)S(1)}) custom-call(s32[3]{0:T(128)S(1)} %get-tuple-element.59.place, s32[1024]{0:T(1024)S(1)} %get-tuple-element.60.ent, s32[1024]{0:T(1024)S(1)} %get-tuple-element.62.slot, s32[1024]{0:T(1024)S(1)} %get-tuple-element.63.first, ...), custom_call_target="tpu_custom_call" | custom-call | tf_op jit(solution)/shard_map/cond/branch_1_fun/pallas_call | solution.py:289
  172.9 2.4 %collective-permute-start.14 = (bf16[16,256,128]{2,1,0:T(8,128)(2,1)S(1)}, bf16[16,256,128]{2,1,0:T(8,128)(2,1)S(1)}, u32[]{:S(2)}, u32[]{:S(2)}) collective-permute-start(bf16[16,256,128]{2,1,0:T(8,128)(2,1)S(1)} %get-tuple-element.91), channel_id=1, source_target_pairs={{0,8},{8,0},{1,9},{9,1},{2,10},{10,2},{3,11},{11,3},{4,12},{12,4},... | collective-permute-start | bytes 3145736 | tf_op jit(solution)/shard_map/ppermute | solution.py:236
  175.2 2.3 %collective-permute-done.14 = bf16[16,256,128]{2,1,0:T(8,128)(2,1)S(1)} collective-permute-done((bf16[16,256,128]{2,1,0:T(8,128)(2,1)S(1)}, bf16[16,256,128]{2,1,0:T(8,128)(2,1)S(1)}, u32[]{:S(2)}, u32[]{:S(2)}) %collective-permute-start.14) | collective-permute-done | bytes 1048608 | tf_op jit(solution)/shard_map/ppermute | solution.py:236
  177.5 1.3 add_convert_fusion
  178.8 8.9 %all-to-all-start.5 = ((bf16[64,2,32,128]{3,2,1,0:T(8,128)(2,1)}), bf16[64,2,32,128]{3,2,1,0:T(8,128)(2,1)S(1)}, u32[]{:S(2)}, u32[]{:S(2)}) async-start(bf16[64,2,32,128]{3,2,1,0:T(8,128)(2,1)} %bitcast.18), calls=%async_computation.5 | async-start | bytes 2097152 | tf_op jit(solution)/shard_map/all_to_all | solution.py:244
  187.6 1.3 fusion.5
  189.0 1.4 copy_bitcast_fusion
  190.3 25.0 %all-to-all-done.5 = bf16[64,2,32,128]{3,2,1,0:T(8,128)(2,1)S(1)} async-done(((bf16[64,2,32,128]{3,2,1,0:T(8,128)(2,1)}), bf16[64,2,32,128]{3,2,1,0:T(8,128)(2,1)S(1)}, u32[]{:S(2)}, u32[]{:S(2)}) %all-to-all-start.5) | async-done | bytes 1048608 | tf_op jit(solution)/shard_map/all_to_all | solution.py:244
  (61 shorter events, 11.1 us)
Async XLA Ops:
  2.8 17.3 %copy-start.20 = (s32[128,8]{0,1:T(8,128)S(1)}, s32[128,8]{0,1:T(8,128)}, u32[]{:S(2)}) copy-start(s32[128,8]{0,1:T(8,128)} %param.13) | copy-start | bytes 12292
  2.8 20.0 %copy-start.21 = (s32[128,8]{0,1:T(8,128)S(1)}, s32[128,8]{0,1:T(8,128)}, u32[]{:S(2)}) copy-start(s32[128,8]{0,1:T(8,128)} %param.14) | copy-start | bytes 12292
  2.8 44.7 %all-to-all-start.4 = ((bf16[64,2,32,128]{3,2,1,0:T(8,128)(2,1)}), bf16[64,2,32,128]{3,2,1,0:T(8,128)(2,1)S(1)}, u32[]{:S(2)}, u32[]{:S(2)}) async-start(bf16[64,2,32,128]{3,2,1,0:T(8,128)(2,1)} %bitcast.9), calls=%async_computation.4 | async-start | bytes 2097152 | tf_op jit(solution)/shard_map/all_to_all | solution.py:244
  20.1 3.0 %copy-start.19 = (s32[16384]{0:T(1024)S(1)}, s32[16384]{0:T(1024)}, u32[]{:S(2)}) copy-start(s32[16384]{0:T(1024)} %param.15) | copy-start | bytes 196612
  20.1 27.4 %copy-start.17 = (bf16[32,64,128]{2,1,0:T(8,128)(2,1)S(1)}, bf16[32,64,128]{2,1,0:T(8,128)(2,1)}, u32[]{:S(2)}) copy-start(bf16[32,64,128]{2,1,0:T(8,128)(2,1)} %param.9) | copy-start | bytes 1572868
  20.1 27.4 %copy-start.18 = (bf16[32,64,128]{2,1,0:T(8,128)(2,1)S(1)}, bf16[32,64,128]{2,1,0:T(8,128)(2,1)}, u32[]{:S(2)}) copy-start(bf16[32,64,128]{2,1,0:T(8,128)(2,1)} %param.12) | copy-start | bytes 1572868
  47.5 14.0 %copy-start.16 = (bf16[16,256,128]{2,1,0:T(8,128)(2,1)}, bf16[16,256,128]{2,1,0:T(8,128)(2,1)S(1)}, u32[]{:S(2)}) copy-start(bf16[16,256,128]{2,1,0:T(8,128)(2,1)S(1)} %get-tuple-element.66.own_ref) | copy-start | bytes 3145732 | tf_op jit(solution)/shard_map/cond
  49.3 47.6 %all-to-all-start.2 = ((bf16[8,2,8,32,128]{4,3,2,1,0:T(8,128)(2,1)}), bf16[8,2,8,32,128]{4,3,2,1,0:T(8,128)(2,1)S(1)}, u32[]{:S(2)}, u32[]{:S(2)}) async-start(bf16[8,2,8,32,128]{4,3,2,1,0:T(8,128)(2,1)} %maximum_bitcast_fusion.1), calls=%async_computation.2 | async-start | bytes 2097152 | tf_op jit(solution)/shard_map/cond/branch_1_fun/all_to_all | solution.py:244
  54.7 6.8 %collective-permute-start.7 = (bf16[16,256,128]{2,1,0:T(8,128)(2,1)S(1)}, bf16[16,256,128]{2,1,0:T(8,128)(2,1)S(1)}, u32[]{:S(2)}, u32[]{:S(2)}) collective-permute-start(bf16[16,256,128]{2,1,0:T(8,128)(2,1)S(1)} %get-tuple-element.66.own_ref), channel_id=1, source_target_pairs={{0,8},{8,0},{1,9},{9,1},{2,10},{10,2},{3,11},{11,3},{4,12},{12,4},... | collective-permute-start | bytes 3145736 | tf_op jit(solution)/shard_map/cond/branch_1_fun/ppermute | solution.py:236
  63.5 17.7 %collective-permute-start.8 = (bf16[9,256,128]{2,1,0:T(8,128)(2,1)S(1)}, bf16[9,256,128]{2,1,0:T(8,128)(2,1)S(1)}, u32[]{:S(2)}, u32[]{:S(2)}) collective-permute-start(bf16[9,256,128]{2,1,0:T(8,128)(2,1)S(1)} %get-tuple-element.67), channel_id=1, source_target_pairs={{0,16},{16,32},{32,48},{48,0},{1,17},{17,33},{33,49},{49,1},{2,18}... | collective-permute-start | bytes 1769480 | tf_op jit(solution)/shard_map/cond/branch_1_fun/ppermute | solution.py:236
  66.7 28.1 %collective-permute-start.9 = (bf16[9,256,128]{2,1,0:T(8,128)(2,1)S(1)}, bf16[9,256,128]{2,1,0:T(8,128)(2,1)S(1)}, u32[]{:S(2)}, u32[]{:S(2)}) collective-permute-start(bf16[9,256,128]{2,1,0:T(8,128)(2,1)S(1)} %get-tuple-element.68), channel_id=1, source_target_pairs={{0,32},{16,48},{32,0},{48,16},{1,33},{17,49},{33,1},{49,17},{2,34}... | collective-permute-start | bytes 1769480 | tf_op jit(solution)/shard_map/cond/branch_1_fun/ppermute | solution.py:236
  71.0 25.0 %collective-permute-start.10 = (bf16[9,256,128]{2,1,0:T(8,128)(2,1)S(1)}, bf16[9,256,128]{2,1,0:T(8,128)(2,1)S(1)}, u32[]{:S(2)}, u32[]{:S(2)}) collective-permute-start(bf16[9,256,128]{2,1,0:T(8,128)(2,1)S(1)} %get-tuple-element.69), channel_id=1, source_target_pairs={{0,48},{16,0},{32,16},{48,32},{1,49},{17,1},{33,17},{49,33},{2,50}... | collective-permute-start | bytes 1769480 | tf_op jit(solution)/shard_map/cond/branch_1_fun/ppermute | solution.py:236
  81.2 0.8 copy-start.8
  94.8 0.8 copy-start.11
  96.1 0.8 copy-start.13
  96.9 1.1 copy-start.9
  97.9 1.1 copy-start.12
  99.0 1.1 copy-start.14
  124.8 1.0 copy-start.1
  125.7 0.8 copy-start.10
  126.6 43.7 %all-to-all-start.3 = ((bf16[8,2,8,32,128]{4,3,2,1,0:T(8,128)(2,1)}), bf16[8,2,8,32,128]{4,3,2,1,0:T(8,128)(2,1)}, u32[]{:S(2)}, u32[]{:S(2)}) async-start(bf16[8,2,8,32,128]{4,3,2,1,0:T(8,128)(2,1)} %copy-done.1), calls=%async_computation.3 | async-start | bytes 2097152 | tf_op jit(solution)/shard_map/cond/branch_1_fun/all_to_all | solution.py:244
  133.5 18.2 %collective-permute-start.11 = (bf16[9,256,128]{2,1,0:T(8,128)(2,1)}, bf16[9,256,128]{2,1,0:T(8,128)(2,1)S(1)}, u32[]{:S(2)}, u32[]{:S(2)}) collective-permute-start(bf16[9,256,128]{2,1,0:T(8,128)(2,1)} %get-tuple-element.71), channel_id=1, source_target_pairs={{0,48},{16,0},{32,16},{48,32},{1,49},{17,1},{33,17},{49,33},{2,50}... | collective-permute-start | bytes 1769480 | tf_op jit(solution)/shard_map/cond/branch_1_fun/ppermute | solution.py:236
  138.8 17.4 %collective-permute-start.12 = (bf16[9,256,128]{2,1,0:T(8,128)(2,1)}, bf16[9,256,128]{2,1,0:T(8,128)(2,1)S(1)}, u32[]{:S(2)}, u32[]{:S(2)}) collective-permute-start(bf16[9,256,128]{2,1,0:T(8,128)(2,1)} %get-tuple-element.72), channel_id=1, source_target_pairs={{0,32},{16,48},{32,0},{48,16},{1,33},{17,49},{33,1},{49,17},{2,34}... | collective-permute-start | bytes 1769480 | tf_op jit(solution)/shard_map/cond/branch_1_fun/ppermute | solution.py:236
  142.2 28.1 %collective-permute-start.13 = (bf16[9,256,128]{2,1,0:T(8,128)(2,1)}, bf16[9,256,128]{2,1,0:T(8,128)(2,1)S(1)}, u32[]{:S(2)}, u32[]{:S(2)}) collective-permute-start(bf16[9,256,128]{2,1,0:T(8,128)(2,1)} %copy-done.10), channel_id=1, source_target_pairs={{0,16},{16,32},{32,48},{48,0},{1,17},{17,33},{33,49},{49,1},{2,18}... | collective-permute-start | bytes 1769480 | tf_op jit(solution)/shard_map/cond/branch_1_fun/ppermute | solution.py:236
  172.9 4.6 %collective-permute-start.14 = (bf16[16,256,128]{2,1,0:T(8,128)(2,1)S(1)}, bf16[16,256,128]{2,1,0:T(8,128)(2,1)S(1)}, u32[]{:S(2)}, u32[]{:S(2)}) collective-permute-start(bf16[16,256,128]{2,1,0:T(8,128)(2,1)S(1)} %get-tuple-element.91), channel_id=1, source_target_pairs={{0,8},{8,0},{1,9},{9,1},{2,10},{10,2},{3,11},{11,3},{4,12},{12,4},... | collective-permute-start | bytes 3145736 | tf_op jit(solution)/shard_map/ppermute | solution.py:236
  178.8 36.5 %all-to-all-start.5 = ((bf16[64,2,32,128]{3,2,1,0:T(8,128)(2,1)}), bf16[64,2,32,128]{3,2,1,0:T(8,128)(2,1)S(1)}, u32[]{:S(2)}, u32[]{:S(2)}) async-start(bf16[64,2,32,128]{3,2,1,0:T(8,128)(2,1)} %bitcast.18), calls=%async_computation.5 | async-start | bytes 2097152 | tf_op jit(solution)/shard_map/all_to_all | solution.py:244

commit v3 on v2

--- a/solution.py
+++ b/solution.py
@@ -15,8 +15,7 @@
 CTX = Z * X * CORE
 GROUP = 8
 QUARTER = 32
-MOST = 14
-FEW = 9
+SLOTS = (7, 8, 9, 14)
 LOG2E = 1.4426950408889634
 MIB = 1 << 20
 
@@ -79,11 +78,28 @@
     oth_out[...] = acc[ENTRIES:].astype(jnp.bfloat16)
 
 
+def mask_kernel(place, ent, kind, sess, mask):
+    me = (place[0] * X + place[1]) * CORE + place[2]
+    key_iota = lax.broadcasted_iota(jnp.int32, (BLOCK, BLOCK), 0)
+    query_iota = lax.broadcasted_iota(jnp.int32, (BLOCK, BLOCK), 1)
+
+    @pl.loop(0, ENTRIES)
+    def _(e):
+        index = me * 2 + e // LISTED
+        block, t = ent[me * ENTRIES + e], kind[me * ENTRIES + e]
+        sess_q = sess[pl.ds(index, 1), :]
+        sess_k = jnp.broadcast_to(sess[pl.ds(block, 1), :], (BLOCK, BLOCK)).T
+        needs = jnp.where((t == 0) | (t == 2), 1.0, 0.0)
+        shift = jnp.where(t == 0, (block - index) * BLOCK, jnp.where(t == 3, 0, -(1 << 20)))
+        seen = ((sess_k - sess_q) * needs == 0.0) & (key_iota + shift <= query_iota)
+        mask[e] = jnp.where(seen, jnp.inf, -jnp.inf)
+
+
 def attend_kernel(
-    place, ent, kind, slot, first,
-    qd, own_ref, oth_ref, r1, r2, r3, sess,
+    place, ent, slot, first,
+    qd, own_ref, oth_ref, r1, r2, r3, mask,
     out, g0, g1, g2, g3,
-    kc, vc, kt, vt, mask, s_scr, p_scr, d_scr, dk, dv,
+    kc, vc, kt, vt, qs, dos, s_scr, p_scr, d_scr, dk, dv,
 ):
     z, x, core = place[0], place[1], place[2]
     me = z * (X * CORE) + x * CORE + core
@@ -94,11 +110,6 @@
 
     @pl.loop(0, 2)
     def _(b):
-        index = me * 2 + b
-        sess_q = sess[pl.ds(index, 1), :]
-        key_iota = lax.broadcasted_iota(jnp.int32, (BLOCK, BLOCK), 0)
-        query_iota = lax.broadcasted_iota(jnp.int32, (BLOCK, BLOCK), 1)
-
         @pl.loop(0, LISTED)
         def _(l):
             e = base + b * LISTED + l
@@ -128,59 +139,49 @@
                 def _():
                     take(buf[sl])
 
-            t = kind[e]
-            sess_k = jnp.broadcast_to(sess[pl.ds(block, 1), :], (BLOCK, BLOCK)).T
-            needs = jnp.where((t == 0) | (t == 2), 1.0, 0.0)
-            shift = jnp.where(t == 0, (block - index) * BLOCK, jnp.where(t == 3, 0, -(1 << 20)))
-            seen = ((sess_k - sess_q) * needs == 0.0) & (key_iota + shift <= query_iota)
-            mask[at, :] = jnp.where(seen, jnp.inf, -jnp.inf)
-
         for l in range(LISTED):
             at = slice(l * BLOCK, (l + 1) * BLOCK)
             kt[:, at] = kc[at, :].astype(jnp.float32).T.astype(jnp.bfloat16)
             vt[:, at] = vc[at, :].astype(jnp.float32).T.astype(jnp.bfloat16)
 
-        for l in range(LISTED):
-            dk[b * LISTED + l] = jnp.zeros((BLOCK, WIDTH), jnp.float32)
-            dv[b * LISTED + l] = jnp.zeros((BLOCK, WIDTH), jnp.float32)
-
-        @pl.loop(0, GROUP // 2)
-        def _(pair):
-            quarters = pl.ds(b * 4, 4)
-
-            def both(what):
-                return jnp.concatenate(
-                    [
-                        qd[quarters, what, 2 * pair + i].reshape(BLOCK, WIDTH)
-                        for i in range(2)
-                    ],
-                    axis=0,
-                )
-
-            q = both(0)
-            do = both(1)
+        quarters = pl.ds(b * 4, 4)
+        for g in range(GROUP):
+            at = slice(g * BLOCK, (g + 1) * BLOCK)
+            qs[at, :] = qd[quarters, 0, g].reshape(BLOCK, WIDTH)
+            dos[at, :] = qd[quarters, 1, g].reshape(BLOCK, WIDTH)
+
+        def score(pair):
+            q = qs[pair * rows : (pair + 1) * rows, :]
             top = jnp.full((8, rows), -jnp.inf, jnp.float32)
             for l in range(LISTED):
                 at = slice(l * BLOCK, (l + 1) * BLOCK)
                 s = lax.dot_general(
                     kc[at, :], q, contract_last, preferred_element_type=jnp.float32
                 )
-                m = mask[at, :]
+                m = mask[b * LISTED + l]
                 s = jnp.minimum(s, jnp.concatenate([m, m], axis=1))
-                s_scr[at, :] = s
+                s_scr[pair % 2, at, :] = s
                 top = jnp.maximum(top, jnp.max(s.reshape(BLOCK // 8, 8, rows), axis=0))
-            top = jnp.max(top, axis=0, keepdims=True)
+            return jnp.max(top, axis=0, keepdims=True)
+
+        top = score(0)
+        for pair in range(GROUP // 2):
+            cols = slice(pair * rows, (pair + 1) * rows)
+            now = pair % 2
             total = jnp.zeros((8, rows), jnp.float32)
             for l in range(LISTED):
                 at = slice(l * BLOCK, (l + 1) * BLOCK)
-                w = jnp.exp2((s_scr[at, :] - top) * (scale * LOG2E))
-                s_scr[at, :] = w
+                w = jnp.exp2((s_scr[now, at, :] - top) * (scale * LOG2E))
+                s_scr[now, at, :] = w
                 total = total + jnp.sum(w.reshape(BLOCK // 8, 8, rows), axis=0)
             inverse = 1.0 / jnp.sum(total, axis=0, keepdims=True)
+            if pair < GROUP // 2 - 1:
+                top = score(pair + 1)
             for l in range(LISTED):
                 at = slice(l * BLOCK, (l + 1) * BLOCK)
-                p_scr[at, :] = (s_scr[at, :] * inverse).astype(jnp.bfloat16)
-            o_t = jnp.dot(vt[...], p_scr[...], preferred_element_type=jnp.float32)
+                p_scr[at, cols] = (s_scr[now, at, :] * inverse).astype(jnp.bfloat16)
+            o_t = jnp.dot(vt[...], p_scr[:, cols], preferred_element_type=jnp.float32)
+            do = dos[cols, :]
             do_t = do.astype(jnp.float32).T
             o_round = o_t.astype(jnp.bfloat16).astype(jnp.float32)
             row_dot = jnp.sum(o_round * do_t, axis=0, keepdims=True)
@@ -190,13 +191,9 @@
                 dp = lax.dot_general(
                     vc[at, :], do, contract_last, preferred_element_type=jnp.float32
                 )
-                ds = ((s_scr[at, :] * scaled) * (dp - row_dot)).astype(jnp.bfloat16)
-                d_scr[at, :] = ds
-                dk[b * LISTED + l] += jnp.dot(ds, q, preferred_element_type=jnp.float32)
-                dv[b * LISTED + l] += jnp.dot(
-                    p_scr[at, :], do, preferred_element_type=jnp.float32
-                )
-            dq_t = jnp.dot(kt[...], d_scr[...], preferred_element_type=jnp.float32)
+                ds = ((s_scr[now, at, :] * scaled) * (dp - row_dot)).astype(jnp.bfloat16)
+                d_scr[at, cols] = ds
+            dq_t = jnp.dot(kt[...], d_scr[:, cols], preferred_element_type=jnp.float32)
             o = o_t.T.astype(jnp.bfloat16)
             dq = dq_t.T.astype(jnp.bfloat16)
             for i in range(2):
@@ -204,6 +201,10 @@
                 out[quarters, 0, 2 * pair + i] = o[at].reshape(4, QUARTER, WIDTH)
                 out[quarters, 1, 2 * pair + i] = dq[at].reshape(4, QUARTER, WIDTH)
 
+        here = pl.ds(b * LISTED, LISTED)
+        dk[here] = jnp.dot(d_scr[...], qs[...], preferred_element_type=jnp.float32).reshape(LISTED, BLOCK, WIDTH)
+        dv[here] = jnp.dot(p_scr[...], dos[...], preferred_element_type=jnp.float32).reshape(LISTED, BLOCK, WIDTH)
+
     @pl.loop(LISTED, ENTRIES)
     def _(e):
         f = first[base + e]
@@ -242,6 +243,44 @@
 
 def exchange(array, axis):
     return lax.all_to_all(array, axis, split_axis=0, concat_axis=0, tiled=True)
+
+
+def masks(*operands):
+    return pl.pallas_call(
+        mask_kernel,
+        out_shape=jax.ShapeDtypeStruct((ENTRIES, BLOCK, BLOCK), jnp.float32),
+        in_specs=[SMEM] * 3 + [VMEM],
+        out_specs=VMEM,
+        compiler_params=params(4),
+        cost_estimate=pl.CostEstimate(flops=ENTRIES * BLOCK * BLOCK * 8, bytes_accessed=MIB, transcendentals=0),
+    )(*operands)
+
+
+def attend(slots, *operands):
+    return pl.pallas_call(
+        attend_kernel,
+        out_shape=[jax.ShapeDtypeStruct((HEAD, 2, GROUP, QUARTER, WIDTH), jnp.bfloat16), blocks(ENTRIES)]
+        + [blocks(slots)] * 3,
+        in_specs=[SMEM] * 4 + [VMEM] * 7,
+        out_specs=[VMEM] * 5,
+        scratch_shapes=[
+            pltpu.VMEM((LISTED * BLOCK, WIDTH), jnp.bfloat16),
+            pltpu.VMEM((LISTED * BLOCK, WIDTH), jnp.bfloat16),
+            pltpu.VMEM((WIDTH, LISTED * BLOCK), jnp.bfloat16),
+            pltpu.VMEM((WIDTH, LISTED * BLOCK), jnp.bfloat16),
+            pltpu.VMEM((GROUP * BLOCK, WIDTH), jnp.bfloat16),
+            pltpu.VMEM((GROUP * BLOCK, WIDTH), jnp.bfloat16),
+            pltpu.VMEM((2, LISTED * BLOCK, 2 * BLOCK), jnp.float32),
+            pltpu.VMEM((LISTED * BLOCK, GROUP * BLOCK), jnp.bfloat16),
+            pltpu.VMEM((LISTED * BLOCK, GROUP * BLOCK), jnp.bfloat16),
+            pltpu.VMEM((ENTRIES, BLOCK, WIDTH), jnp.float32),
+            pltpu.VMEM((ENTRIES, BLOCK, WIDTH), jnp.float32),
+        ],
+        compiler_params=params(24),
+        cost_estimate=pl.CostEstimate(
+            flops=5 * 2 * 2048 * 1024 * 128, bytes_accessed=8 * MIB, transcendentals=2048 * 1024
+        ),
+    )(*operands)
 
 
 def between(slots, place, tables, own, queries, output_gradient, sess):
@@ -252,36 +291,18 @@
         out_shape=[blocks(slots)] * 3,
         in_specs=[SMEM] * 4 + [VMEM] * 2,
         out_specs=[VMEM] * 3,
-        compiler_params=params(16),
+        compiler_params=params(8),
     )(place, ent, slot, first, own, other)
+    now, *sends = lax.optimization_barrier((place, *sends))
     fetched = [shift(sends[k - 1], "x", k) for k in (1, 2, 3)]
+    mask = masks(now, ent, kind, sess)
 
     qd = jnp.stack([queries, output_gradient]).reshape(2, QUARTER, HEAD, GROUP, WIDTH)
     qd = exchange(qd.transpose(2, 0, 3, 1, 4), "head")
 
-    out, g0, g1, g2, g3 = pl.pallas_call(
-        attend_kernel,
-        out_shape=[jax.ShapeDtypeStruct((HEAD, 2, GROUP, QUARTER, WIDTH), jnp.bfloat16), blocks(ENTRIES)]
-        + [blocks(slots)] * 3,
-        in_specs=[SMEM] * 5 + [VMEM] * 7,
-        out_specs=[VMEM] * 5,
-        scratch_shapes=[
-            pltpu.VMEM((LISTED * BLOCK, WIDTH), jnp.bfloat16),
-            pltpu.VMEM((LISTED * BLOCK, WIDTH), jnp.bfloat16),
-            pltpu.VMEM((WIDTH, LISTED * BLOCK), jnp.bfloat16),
-            pltpu.VMEM((WIDTH, LISTED * BLOCK), jnp.bfloat16),
-            pltpu.VMEM((LISTED * BLOCK, BLOCK), jnp.float32),
-            pltpu.VMEM((LISTED * BLOCK, 2 * BLOCK), jnp.float32),
-            pltpu.VMEM((LISTED * BLOCK, 2 * BLOCK), jnp.bfloat16),
-            pltpu.VMEM((LISTED * BLOCK, 2 * BLOCK), jnp.bfloat16),
-            pltpu.VMEM((ENTRIES, BLOCK, WIDTH), jnp.float32),
-            pltpu.VMEM((ENTRIES, BLOCK, WIDTH), jnp.float32),
-        ],
-        compiler_params=params(40),
-        cost_estimate=pl.CostEstimate(
-            flops=5 * 2 * 2048 * 1024 * 128, bytes_accessed=8 * MIB, transcendentals=2048 * 1024
-        ),
-    )(place, ent, kind, slot, first, qd, own, other, *fetched, sess)
+    out, g0, g1, g2, g3 = attend(
+        slots, place, ent, slot, first, qd, own, other, *fetched, mask
+    )
 
     returned = [shift(g, "x", -k) for k, g in ((1, g1), (2, g2), (3, g3))]
     out = exchange(out, "head")
@@ -292,7 +313,7 @@
         in_specs=[SMEM] * 4 + [VMEM] * 4,
         out_specs=[VMEM] * 2,
         scratch_shapes=[pltpu.VMEM((2 * ENTRIES, 2 * BLOCK, WIDTH), jnp.float32)],
-        compiler_params=params(24),
+        compiler_params=params(14),
     )(place, ent, slot, first, g0, *returned)
     return out, own_sum, other_sum
 
@@ -323,10 +344,9 @@
     own = exchange(kv.reshape(Z * HEAD, 2, QUARTER, WIDTH), ("z", "head"))
     own = own.reshape(ENTRIES, 2 * BLOCK, WIDTH)
 
-    out, own_sum, other_sum = lax.cond(
-        most <= FEW,
-        functools.partial(between, FEW),
-        functools.partial(between, MOST),
+    out, own_sum, other_sum = lax.switch(
+        sum((most > few).astype(jnp.int32) for few in SLOTS[:-1]),
+        [functools.partial(between, slots) for slots in SLOTS],
         place, tables, own, queries, output_gradient, sess,
     )
 

time: 219 us -> 199 us (0.909)
  waiting for transfers between devices: 100 us -> 85.6 us
  Pallas kernels: 29.4 us -> 20.6 us
    ppermute x8, waiting for transfers between devices: 51 us -> 37.5 us  [shift(): lax.ppermute(array, axis, [(i, (i + by) % size) for i in range(size)])]
    pallas_call x1 -> x2, Pallas kernels: 24.7 us -> 14.7 us  [the longest x1 12.4 us: attend(): pl.pallas_call(attend_kernel, out_shape=[jax.ShapeDtypeStruct((HEAD, 2, G...]
    cond x18 -> x28, local copies, waits for them, and re-layouts: 7.43 us -> 8.68 us
  transfers between devices with their start and end apart: 12 -> 12, of which waited for: 10 -> 10; matrix products, arithmetic and copies ran while one was open for 2% -> 2% of each run, Pallas kernels for 1% -> 2%
where the time goes in v3:
time: 199 us; the launch traced here: 197 us
  waiting for transfers between devices  85.6 us (43%)
  starting transfers between devices  66.7 us (34%)
  Pallas kernels  20.6 us (10%)
  local copies, waits for them, and re-layouts  15.9 us (8%)
  other arithmetic  5.56 us (3%)
  between operations  2.73 us (1%)
    all_to_all x4, waiting for transfers between devices, exchange(): return lax.all_to_all(array, axis, split_axis=0, concat_axis=0, tiled=True)  48.1 us
    all_to_all x4, starting transfers between devices, exchange(): return lax.all_to_all(array, axis, split_axis=0, concat_axis=0, tiled=True)  38.5 us
    ppermute x8, waiting for transfers between devices, shift(): lax.ppermute(array, axis, [(i, (i + by) % size) for i in range(size)])  37.5 us
    ppermute x8, starting transfers between devices, shift(): lax.ppermute(array, axis, [(i, (i + by) % size) for i in range(size)])  28.1 us
    pallas_call x1, Pallas kernels, attend(): pl.pallas_call(attend_kernel, out_shape=[jax.ShapeDtypeStruct((HEAD, 2, G...  12.4 us
    cond x28, local copies, waits for them, and re-layouts  8.68 us
  transfers between devices with their start and end apart: 12, of which 10 were waited for; matrix products, arithmetic and copies ran while one was open for 2% of the time, Pallas kernels for 2%

profile of v3, /device:TPU:1, one launch (start us, length us, event | category | flops | bytes accessed | tf_op | source)
XLA Modules:
  0.0 197.1 jit_solution(2250313920932508891)
XLA Ops:
  1.5 1.3 broadcast_in_dim.30
  2.8 17.3 %all-to-all-start.8 = ((bf16[64,2,32,128]{3,2,1,0:T(8,128)(2,1)}), bf16[64,2,32,128]{3,2,1,0:T(8,128)(2,1)S(1)}, u32[]{:S(2)}, u32[]{:S(2)}) async-start(bf16[64,2,32,128]{3,2,1,0:T(8,128)(2,1)} %bitcast.15), calls=%async_computation.8 | async-start | bytes 2097152 | tf_op jit(solution)/shard_map/all_to_all | solution.py:245
  24.4 23.1 %all-to-all-done.8 = bf16[64,2,32,128]{3,2,1,0:T(8,128)(2,1)S(1)} async-done(((bf16[64,2,32,128]{3,2,1,0:T(8,128)(2,1)}), bf16[64,2,32,128]{3,2,1,0:T(8,128)(2,1)S(1)}, u32[]{:S(2)}, u32[]{:S(2)}) %all-to-all-start.8) | async-done | bytes 1048608 | tf_op jit(solution)/shard_map/all_to_all | solution.py:245
  47.5 104.2 %conditional.1 = (bf16[8,2,8,32,128]{4,3,2,1,0:T(8,128)(2,1)}, bf16[16,256,128]{2,1,0:T(8,128)(2,1)}, bf16[16,256,128]{2,1,0:T(8,128)(2,1)}) conditional(s32[]{:T(128)} %clamp.3, (bf16[32,64,128]{2,1,0:T(8,128)(2,1)S(1)}, bf16[32,64,128]{2,1,0:T(8,128)(2,1)S(1)}, bf16[16,256,128]{2,1,0:T(8,128)(2,1)S(1)}, ...), branch_computations={%region_3.4_spmd, %region_4.5_spmd, %region_5.6_spmd, %region_6.7_... | conditional | flops 2686976000 | bytes 91226832 | solution.py:347
  48.2 1.1 maximum_bitcast_fusion
  49.3 5.4 %all-to-all-start = ((bf16[8,2,8,32,128]{4,3,2,1,0:T(8,128)(2,1)}), bf16[8,2,8,32,128]{4,3,2,1,0:T(8,128)(2,1)S(1)}, u32[]{:S(2)}, u32[]{:S(2)}) async-start(bf16[8,2,8,32,128]{4,3,2,1,0:T(8,128)(2,1)} %maximum_bitcast_fusion), calls=%async_computation | async-start | bytes 2097152 | tf_op jit(solution)/shard_map/cond/branch_0_fun/all_to_all | solution.py:245
  54.7 4.5 %collective-permute-start = (bf16[16,256,128]{2,1,0:T(8,128)(2,1)S(1)}, bf16[16,256,128]{2,1,0:T(8,128)(2,1)S(1)}, u32[]{:S(2)}, u32[]{:S(2)}) collective-permute-start(bf16[16,256,128]{2,1,0:T(8,128)(2,1)S(1)} %get-tuple-element.78.own_ref), channel_id=1, source_target_pairs={{0,8},{8,0},{1,9},{9,1},{2,10},{10,2},{3,11},{11,3},{4,12},{12,4},... | collective-permute-start | bytes 3145736 | tf_op jit(solution)/shard_map/cond/branch_0_fun/ppermute | solution.py:237
  59.2 2.3 %collective-permute-done.oth_ref = bf16[16,256,128]{2,1,0:T(8,128)(2,1)S(1)} collective-permute-done((bf16[16,256,128]{2,1,0:T(8,128)(2,1)S(1)}, bf16[16,256,128]{2,1,0:T(8,128)(2,1)S(1)}, u32[]{:S(2)}, u32[]{:S(2)}) %collective-permute-start) | collective-permute-done | bytes 1048608 | tf_op jit(solution)/shard_map/cond/branch_0_fun/ppermute | solution.py:237
  61.5 2.0 %branch_0_fun.4 = (bf16[7,256,128]{2,1,0:T(8,128)(2,1)S(1)}, bf16[7,256,128]{2,1,0:T(8,128)(2,1)S(1)}, bf16[7,256,128]{2,1,0:T(8,128)(2,1)S(1)}) custom-call(s32[3]{0:T(128)S(1)} %get-tuple-element.85.place, s32[1024]{0:T(1024)S(1)} %get-tuple-element.73.ent, s32[1024]{0:T(1024)S(1)} %get-tuple-element.74.slot, s32[1024]{0:T(1024)S(1)} %get-tuple-element.75.first, ...), custom_call_target="tpu_custom_call" | custom-call | tf_op jit(solution)/shard_map/cond/branch_0_fun/pallas_call | solution.py:289
  63.5 3.1 %collective-permute-start.1 = (bf16[7,256,128]{2,1,0:T(8,128)(2,1)S(1)}, bf16[7,256,128]{2,1,0:T(8,128)(2,1)S(1)}, u32[]{:S(2)}, u32[]{:S(2)}) collective-permute-start(bf16[7,256,128]{2,1,0:T(8,128)(2,1)S(1)} %get-tuple-element.82), channel_id=1, source_target_pairs={{0,16},{16,32},{32,48},{48,0},{1,17},{17,33},{33,49},{49,1},{2,18}... | collective-permute-start | bytes 1376264 | tf_op jit(solution)/shard_map/cond/branch_0_fun/ppermute | solution.py:237
  66.7 4.4 %collective-permute-start.2 = (bf16[7,256,128]{2,1,0:T(8,128)(2,1)S(1)}, bf16[7,256,128]{2,1,0:T(8,128)(2,1)S(1)}, u32[]{:S(2)}, u32[]{:S(2)}) collective-permute-start(bf16[7,256,128]{2,1,0:T(8,128)(2,1)S(1)} %get-tuple-element.83), channel_id=1, source_target_pairs={{0,32},{16,48},{32,0},{48,16},{1,33},{17,49},{33,1},{49,17},{2,34}... | collective-permute-start | bytes 1376264 | tf_op jit(solution)/shard_map/cond/branch_0_fun/ppermute | solution.py:237
  71.0 3.1 %collective-permute-start.3 = (bf16[7,256,128]{2,1,0:T(8,128)(2,1)S(1)}, bf16[7,256,128]{2,1,0:T(8,128)(2,1)S(1)}, u32[]{:S(2)}, u32[]{:S(2)}) collective-permute-start(bf16[7,256,128]{2,1,0:T(8,128)(2,1)S(1)} %get-tuple-element.84), channel_id=1, source_target_pairs={{0,48},{16,0},{32,16},{48,32},{1,49},{17,1},{33,17},{49,33},{2,50}... | collective-permute-start | bytes 1376264 | tf_op jit(solution)/shard_map/cond/branch_0_fun/ppermute | solution.py:237
  74.1 2.3 %branch_0_fun.5.mask = f32[16,128,128]{2,1,0:T(8,128)S(1)} custom-call(s32[3]{0:T(128)S(1)} %get-tuple-element.85.place, s32[1024]{0:T(1024)S(1)} %get-tuple-element.73.ent, s32[1024]{0:T(1024)S(1)} %get-tuple-element.86.kind, f32[128,128]{1,0:T(8,128)S(1)} %get-tuple-element.87.sess), custom_call_target="tpu_custom_call" | custom-call | flops 2097152 | bytes 1048576 | tf_op jit(solution)/shard_map/cond/branch_0_fun/pallas_call | solution.py:249
  76.4 1.9 collective-permute-done.1.r1
  79.1 10.1 %collective-permute-done.2.r2 = bf16[7,256,128]{2,1,0:T(8,128)(2,1)S(1)} collective-permute-done((bf16[7,256,128]{2,1,0:T(8,128)(2,1)S(1)}, bf16[7,256,128]{2,1,0:T(8,128)(2,1)S(1)}, u32[]{:S(2)}, u32[]{:S(2)}) %collective-permute-start.2) | collective-permute-done | bytes 458784 | tf_op jit(solution)/shard_map/cond/branch_0_fun/ppermute | solution.py:237
  91.2 1.0 copy-done.33
  94.2 12.4 %branch_0_fun.6 = (bf16[8,2,8,32,128]{4,3,2,1,0:T(8,128)(2,1)}, bf16[16,256,128]{2,1,0:T(8,128)(2,1)S(1)}, bf16[7,256,128]{2,1,0:T(8,128)(2,1)S(1)}, bf16[7,256,...) custom-call(s32[3]{0:T(128)S(1)} %get-tuple-element.85.place, s32[1024]{0:T(1024)S(1)} %get-tuple-element.73.ent, ...), custom_call_target="tpu_custom_call" | custom-call | flops 2684354560 | bytes 8388608 | tf_op jit(solution)/shard_map/cond/branch_0_fun/pallas_call | solution.py:260
  109.9 7.0 %all-to-all-start.1 = ((bf16[8,2,8,32,128]{4,3,2,1,0:T(8,128)(2,1)}), bf16[8,2,8,32,128]{4,3,2,1,0:T(8,128)(2,1)}, u32[]{:S(2)}, u32[]{:S(2)}) async-start(bf16[8,2,8,32,128]{4,3,2,1,0:T(8,128)(2,1)} %get-tuple-element.91), calls=%async_computation.1 | async-start | bytes 2097152 | tf_op jit(solution)/shard_map/cond/branch_0_fun/all_to_all | solution.py:245
  117.0 5.3 %collective-permute-start.4 = (bf16[7,256,128]{2,1,0:T(8,128)(2,1)}, bf16[7,256,128]{2,1,0:T(8,128)(2,1)S(1)}, u32[]{:S(2)}, u32[]{:S(2)}) collective-permute-start(bf16[7,256,128]{2,1,0:T(8,128)(2,1)} %copy-done.42), channel_id=1, source_target_pairs={{0,48},{16,0},{32,16},{48,32},{1,49},{17,1},{33,17},{49,33},{2,50}... | collective-permute-start | bytes 1376264 | tf_op jit(solution)/shard_map/cond/branch_0_fun/ppermute | solution.py:237
  122.3 3.4 %collective-permute-start.5 = (bf16[7,256,128]{2,1,0:T(8,128)(2,1)S(1)}, bf16[7,256,128]{2,1,0:T(8,128)(2,1)S(1)}, u32[]{:S(2)}, u32[]{:S(2)}) collective-permute-start(bf16[7,256,128]{2,1,0:T(8,128)(2,1)S(1)} %copy-done.39), channel_id=1, source_target_pairs={{0,32},{16,48},{32,0},{48,16},{1,33},{17,49},{33,1},{49,17},{2,34}... | collective-permute-start | bytes 1376264 | tf_op jit(solution)/shard_map/cond/branch_0_fun/ppermute | solution.py:237
  125.7 1.9 collective-permute-start.6
  127.6 4.8 %collective-permute-done.4.g1 = bf16[7,256,128]{2,1,0:T(8,128)(2,1)S(1)} collective-permute-done((bf16[7,256,128]{2,1,0:T(8,128)(2,1)}, bf16[7,256,128]{2,1,0:T(8,128)(2,1)S(1)}, u32[]{:S(2)}, u32[]{:S(2)}) %collective-permute-start.4) | collective-permute-done | bytes 458784 | tf_op jit(solution)/shard_map/cond/branch_0_fun/ppermute | solution.py:237
  132.4 4.3 %collective-permute-done.5.g2 = bf16[7,256,128]{2,1,0:T(8,128)(2,1)S(1)} collective-permute-done((bf16[7,256,128]{2,1,0:T(8,128)(2,1)S(1)}, bf16[7,256,128]{2,1,0:T(8,128)(2,1)S(1)}, u32[]{:S(2)}, u32[]{:S(2)}) %collective-permute-start.5) | collective-permute-done | bytes 458784 | tf_op jit(solution)/shard_map/cond/branch_0_fun/ppermute | solution.py:237
  136.8 11.2 %collective-permute-done.6.g3 = bf16[7,256,128]{2,1,0:T(8,128)(2,1)S(1)} collective-permute-done((bf16[7,256,128]{2,1,0:T(8,128)(2,1)S(1)}, bf16[7,256,128]{2,1,0:T(8,128)(2,1)S(1)}, u32[]{:S(2)}, u32[]{:S(2)}) %collective-permute-start.6) | collective-permute-done | bytes 458784 | tf_op jit(solution)/shard_map/cond/branch_0_fun/ppermute | solution.py:237
  147.9 3.8 %branch_0_fun.7 = (bf16[16,256,128]{2,1,0:T(8,128)(2,1)}, bf16[16,256,128]{2,1,0:T(8,128)(2,1)}) custom-call(s32[3]{0:T(128)S(1)} %get-tuple-element.85.place, s32[1024]{0:T(1024)S(1)} %get-tuple-element.73.ent, s32[1024]{0:T(1024)S(1)} %get-tuple-element.74.slot, s32[1024]{0:T(1024)S(1)} %get-tuple-element.75.first, bf16[16,256,128]{2,1,0:T(8,128)(2,1)S(1)} %copy-done.10, ...), custom_call_target="tpu_custom_call" | custom-call | tf_op jit(solution)/shard_map/cond/branch_0_fun/pallas_call | solution.py:310
  151.8 2.4 %collective-permute-start.28 = (bf16[16,256,128]{2,1,0:T(8,128)(2,1)}, bf16[16,256,128]{2,1,0:T(8,128)(2,1)S(1)}, u32[]{:S(2)}, u32[]{:S(2)}) collective-permute-start(bf16[16,256,128]{2,1,0:T(8,128)(2,1)} %get-tuple-element.189), channel_id=1, source_target_pairs={{0,8},{8,0},{1,9},{9,1},{2,10},{10,2},{3,11},{11,3},{4,12},{12,4},... | collective-permute-start | bytes 3145736 | tf_op jit(solution)/shard_map/ppermute | solution.py:237
  154.2 2.5 %collective-permute-done.28 = bf16[16,256,128]{2,1,0:T(8,128)(2,1)S(1)} collective-permute-done((bf16[16,256,128]{2,1,0:T(8,128)(2,1)}, bf16[16,256,128]{2,1,0:T(8,128)(2,1)S(1)}, u32[]{:S(2)}, u32[]{:S(2)}) %collective-permute-start.28) | collective-permute-done | bytes 1048608 | tf_op jit(solution)/shard_map/ppermute | solution.py:237
  156.7 2.5 %add_convert_fusion = bf16[16,256,128]{2,1,0:T(8,128)(2,1)} fusion(bf16[16,256,128]{2,1,0:T(8,128)(2,1)S(1)} %collective-permute-done.28, bf16[16,256,128]{2,1,0:T(8,128)(2,1)} %get-tuple-element.188), kind=kLoop, calls=%fused_computation.4 | loop fusion | flops 2097152 | bytes 3145728 | tf_op jit(solution)/shard_map/convert_element_type | solution.py:354
  159.1 8.8 %all-to-all-start.9 = ((bf16[64,2,32,128]{3,2,1,0:T(8,128)(2,1)}), bf16[64,2,32,128]{3,2,1,0:T(8,128)(2,1)S(1)}, u32[]{:S(2)}, u32[]{:S(2)}) async-start(bf16[64,2,32,128]{3,2,1,0:T(8,128)(2,1)} %bitcast.24), calls=%async_computation.9 | async-start | bytes 2097152 | tf_op jit(solution)/shard_map/all_to_all | solution.py:245
  168.0 1.3 fusion.5
  169.3 1.4 copy_bitcast_fusion
  170.7 25.0 %all-to-all-done.9 = bf16[64,2,32,128]{3,2,1,0:T(8,128)(2,1)S(1)} async-done(((bf16[64,2,32,128]{3,2,1,0:T(8,128)(2,1)}), bf16[64,2,32,128]{3,2,1,0:T(8,128)(2,1)S(1)}, u32[]{:S(2)}, u32[]{:S(2)}) %all-to-all-start.9) | async-done | bytes 1048608 | tf_op jit(solution)/shard_map/all_to_all | solution.py:245
  (72 shorter events, 13.5 us)
Async XLA Ops:
  2.8 17.3 %copy-start.53 = (s32[128,8]{0,1:T(8,128)S(1)}, s32[128,8]{0,1:T(8,128)}, u32[]{:S(2)}) copy-start(s32[128,8]{0,1:T(8,128)} %param.15) | copy-start | bytes 12292
  2.8 21.3 %copy-start.54 = (s32[128,8]{0,1:T(8,128)S(1)}, s32[128,8]{0,1:T(8,128)}, u32[]{:S(2)}) copy-start(s32[128,8]{0,1:T(8,128)} %param.16) | copy-start | bytes 12292
  2.8 44.7 %all-to-all-start.8 = ((bf16[64,2,32,128]{3,2,1,0:T(8,128)(2,1)}), bf16[64,2,32,128]{3,2,1,0:T(8,128)(2,1)S(1)}, u32[]{:S(2)}, u32[]{:S(2)}) async-start(bf16[64,2,32,128]{3,2,1,0:T(8,128)(2,1)} %bitcast.15), calls=%async_computation.8 | async-start | bytes 2097152 | tf_op jit(solution)/shard_map/all_to_all | solution.py:245
  20.1 4.3 %copy-start.52 = (s32[16384]{0:T(1024)S(1)}, s32[16384]{0:T(1024)}, u32[]{:S(2)}) copy-start(s32[16384]{0:T(1024)} %param.17) | copy-start | bytes 196612
  20.1 27.4 %copy-start.47 = (bf16[32,64,128]{2,1,0:T(8,128)(2,1)S(1)}, bf16[32,64,128]{2,1,0:T(8,128)(2,1)}, u32[]{:S(2)}) copy-start(bf16[32,64,128]{2,1,0:T(8,128)(2,1)} %param.11) | copy-start | bytes 1572868
  20.1 27.4 %copy-start.50 = (bf16[32,64,128]{2,1,0:T(8,128)(2,1)S(1)}, bf16[32,64,128]{2,1,0:T(8,128)(2,1)}, u32[]{:S(2)}) copy-start(bf16[32,64,128]{2,1,0:T(8,128)(2,1)} %param.14) | copy-start | bytes 1572868
  47.5 13.9 %copy-start.43 = (bf16[16,256,128]{2,1,0:T(8,128)(2,1)}, bf16[16,256,128]{2,1,0:T(8,128)(2,1)S(1)}, u32[]{:S(2)}) copy-start(bf16[16,256,128]{2,1,0:T(8,128)(2,1)S(1)} %get-tuple-element.78.own_ref) | copy-start | bytes 3145732 | tf_op jit(solution)/shard_map/cond
  49.3 41.9 %all-to-all-start = ((bf16[8,2,8,32,128]{4,3,2,1,0:T(8,128)(2,1)}), bf16[8,2,8,32,128]{4,3,2,1,0:T(8,128)(2,1)S(1)}, u32[]{:S(2)}, u32[]{:S(2)}) async-start(bf16[8,2,8,32,128]{4,3,2,1,0:T(8,128)(2,1)} %maximum_bitcast_fusion), calls=%async_computation | async-start | bytes 2097152 | tf_op jit(solution)/shard_map/cond/branch_0_fun/all_to_all | solution.py:245
  54.7 6.8 %collective-permute-start = (bf16[16,256,128]{2,1,0:T(8,128)(2,1)S(1)}, bf16[16,256,128]{2,1,0:T(8,128)(2,1)S(1)}, u32[]{:S(2)}, u32[]{:S(2)}) collective-permute-start(bf16[16,256,128]{2,1,0:T(8,128)(2,1)S(1)} %get-tuple-element.78.own_ref), channel_id=1, source_target_pairs={{0,8},{8,0},{1,9},{9,1},{2,10},{10,2},{3,11},{11,3},{4,12},{12,4},... | collective-permute-start | bytes 3145736 | tf_op jit(solution)/shard_map/cond/branch_0_fun/ppermute | solution.py:237
  63.5 14.8 %collective-permute-start.1 = (bf16[7,256,128]{2,1,0:T(8,128)(2,1)S(1)}, bf16[7,256,128]{2,1,0:T(8,128)(2,1)S(1)}, u32[]{:S(2)}, u32[]{:S(2)}) collective-permute-start(bf16[7,256,128]{2,1,0:T(8,128)(2,1)S(1)} %get-tuple-element.82), channel_id=1, source_target_pairs={{0,16},{16,32},{32,48},{48,0},{1,17},{17,33},{33,49},{49,1},{2,18}... | collective-permute-start | bytes 1376264 | tf_op jit(solution)/shard_map/cond/branch_0_fun/ppermute | solution.py:237
  66.7 22.5 %collective-permute-start.2 = (bf16[7,256,128]{2,1,0:T(8,128)(2,1)S(1)}, bf16[7,256,128]{2,1,0:T(8,128)(2,1)S(1)}, u32[]{:S(2)}, u32[]{:S(2)}) collective-permute-start(bf16[7,256,128]{2,1,0:T(8,128)(2,1)S(1)} %get-tuple-element.83), channel_id=1, source_target_pairs={{0,32},{16,48},{32,0},{48,16},{1,33},{17,49},{33,1},{49,17},{2,34}... | collective-permute-start | bytes 1376264 | tf_op jit(solution)/shard_map/cond/branch_0_fun/ppermute | solution.py:237
  71.0 19.4 %collective-permute-start.3 = (bf16[7,256,128]{2,1,0:T(8,128)(2,1)S(1)}, bf16[7,256,128]{2,1,0:T(8,128)(2,1)S(1)}, u32[]{:S(2)}, u32[]{:S(2)}) collective-permute-start(bf16[7,256,128]{2,1,0:T(8,128)(2,1)S(1)} %get-tuple-element.84), channel_id=1, source_target_pairs={{0,48},{16,0},{32,16},{48,32},{1,49},{17,1},{33,17},{49,33},{2,50}... | collective-permute-start | bytes 1376264 | tf_op jit(solution)/shard_map/cond/branch_0_fun/ppermute | solution.py:237
  78.4 0.8 copy-start.32
  89.2 0.8 copy-start.36
  90.4 0.8 copy-start.40
  91.2 1.0 copy-start.33
  92.2 1.0 copy-start.37
  93.2 1.0 copy-start.41
  106.6 1.0 copy-start.9
  107.6 0.8 copy-start.34
  108.4 0.8 copy-start.38
  109.1 0.8 copy-start.42
  109.9 12.3 %copy-start.39 = (bf16[7,256,128]{2,1,0:T(8,128)(2,1)S(1)}, bf16[7,256,128]{2,1,0:T(8,128)(2,1)}, u32[]{:S(2)}) copy-start(bf16[7,256,128]{2,1,0:T(8,128)(2,1)} %copy-done.38) | copy-start | bytes 1376260 | tf_op jit(solution)/shard_map/cond
  109.9 15.8 %copy-start.35 = (bf16[7,256,128]{2,1,0:T(8,128)(2,1)S(1)}, bf16[7,256,128]{2,1,0:T(8,128)(2,1)}, u32[]{:S(2)}) copy-start(bf16[7,256,128]{2,1,0:T(8,128)(2,1)} %copy-done.34) | copy-start | bytes 1376260 | tf_op jit(solution)/shard_map/cond
  109.9 38.0 %copy-start.10 = (bf16[16,256,128]{2,1,0:T(8,128)(2,1)S(1)}, bf16[16,256,128]{2,1,0:T(8,128)(2,1)}, u32[]{:S(2)}) copy-start(bf16[16,256,128]{2,1,0:T(8,128)(2,1)} %copy-done.9) | copy-start | bytes 3145732 | tf_op jit(solution)/shard_map/cond
  109.9 38.0 %all-to-all-start.1 = ((bf16[8,2,8,32,128]{4,3,2,1,0:T(8,128)(2,1)}), bf16[8,2,8,32,128]{4,3,2,1,0:T(8,128)(2,1)}, u32[]{:S(2)}, u32[]{:S(2)}) async-start(bf16[8,2,8,32,128]{4,3,2,1,0:T(8,128)(2,1)} %get-tuple-element.91), calls=%async_computation.1 | async-start | bytes 2097152 | tf_op jit(solution)/shard_map/cond/branch_0_fun/all_to_all | solution.py:245
  117.0 15.5 %collective-permute-start.4 = (bf16[7,256,128]{2,1,0:T(8,128)(2,1)}, bf16[7,256,128]{2,1,0:T(8,128)(2,1)S(1)}, u32[]{:S(2)}, u32[]{:S(2)}) collective-permute-start(bf16[7,256,128]{2,1,0:T(8,128)(2,1)} %copy-done.42), channel_id=1, source_target_pairs={{0,48},{16,0},{32,16},{48,32},{1,49},{17,1},{33,17},{49,33},{2,50}... | collective-permute-start | bytes 1376264 | tf_op jit(solution)/shard_map/cond/branch_0_fun/ppermute | solution.py:237
  122.3 14.5 %collective-permute-start.5 = (bf16[7,256,128]{2,1,0:T(8,128)(2,1)S(1)}, bf16[7,256,128]{2,1,0:T(8,128)(2,1)S(1)}, u32[]{:S(2)}, u32[]{:S(2)}) collective-permute-start(bf16[7,256,128]{2,1,0:T(8,128)(2,1)S(1)} %copy-done.39), channel_id=1, source_target_pairs={{0,32},{16,48},{32,0},{48,16},{1,33},{17,49},{33,1},{49,17},{2,34}... | collective-permute-start | bytes 1376264 | tf_op jit(solution)/shard_map/cond/branch_0_fun/ppermute | solution.py:237
  125.7 22.2 %collective-permute-start.6 = (bf16[7,256,128]{2,1,0:T(8,128)(2,1)S(1)}, bf16[7,256,128]{2,1,0:T(8,128)(2,1)S(1)}, u32[]{:S(2)}, u32[]{:S(2)}) collective-permute-start(bf16[7,256,128]{2,1,0:T(8,128)(2,1)S(1)} %copy-done.35), channel_id=1, source_target_pairs={{0,16},{16,32},{32,48},{48,0},{1,17},{17,33},{33,49},{49,1},{2,18}... | collective-permute-start | bytes 1376264 | tf_op jit(solution)/shard_map/cond/branch_0_fun/ppermute | solution.py:237
  151.8 4.9 %collective-permute-start.28 = (bf16[16,256,128]{2,1,0:T(8,128)(2,1)}, bf16[16,256,128]{2,1,0:T(8,128)(2,1)S(1)}, u32[]{:S(2)}, u32[]{:S(2)}) collective-permute-start(bf16[16,256,128]{2,1,0:T(8,128)(2,1)} %get-tuple-element.189), channel_id=1, source_target_pairs={{0,8},{8,0},{1,9},{9,1},{2,10},{10,2},{3,11},{11,3},{4,12},{12,4},... | collective-permute-start | bytes 3145736 | tf_op jit(solution)/shard_map/ppermute | solution.py:237
  159.1 36.5 %all-to-all-start.9 = ((bf16[64,2,32,128]{3,2,1,0:T(8,128)(2,1)}), bf16[64,2,32,128]{3,2,1,0:T(8,128)(2,1)S(1)}, u32[]{:S(2)}, u32[]{:S(2)}) async-start(bf16[64,2,32,128]{3,2,1,0:T(8,128)(2,1)} %bitcast.24), calls=%async_computation.9 | async-start | bytes 2097152 | tf_op jit(solution)/shard_map/all_to_all | solution.py:245

commit v4 on v3

--- a/solution.py
+++ b/solution.py
@@ -21,58 +21,94 @@
 
 SMEM = pl.BlockSpec(memory_space=pltpu.SMEM)
 VMEM = pl.BlockSpec(memory_space=pltpu.VMEM)
-
-
-def owner_x(block):
-    return lax.rem(lax.shift_right_logical(block, 2), X)
-
-
-def owner_core(block):
-    return lax.rem(lax.shift_right_logical(block, 1), CORE)
-
-
-def slab_row(block):
-    return lax.shift_right_logical(block, 4) * 2 + lax.rem(block, 2)
-
-
-def gather_kernel(place, ent, slot, first, own_ref, oth_ref, s1, s2, s3):
+HBM = pl.BlockSpec(memory_space=pltpu.HBM)
+DMA = pltpu.SemaphoreType.DMA
+
+
+def fields(code):
+    bits, parts = (4, 1, 2, 4, 1), []
+    for bit in bits:
+        parts.append(code & ((1 << bit) - 1))
+        code = lax.shift_right_logical(code, bit)
+    return (*parts, code)
+
+
+def coded(kv_list):
+    ent = kv_list.reshape(CTX, ENTRIES)
+    order = jnp.arange(ENTRIES, dtype=jnp.int32)
+    equal = ent[:, :, None] == ent[:, None, :]
+    first = jnp.min(jnp.where(equal, order[None, None, :], ENTRIES), axis=2)
+    fresh = first == order[None, :]
+    column = lax.rem(ent // 4, X)
+    before = (
+        fresh[:, None, :]
+        & (column[:, :, None] == column[:, None, :])
+        & (order[None, None, :] < first[:, :, None])
+    )
+    slot = jnp.sum(before.astype(jnp.int32), axis=2)
+    home = lax.rem(jnp.arange(CTX, dtype=jnp.int32) // CORE, X)
+    most = jnp.max(jnp.where(column == home[:, None], 0, slot + 1))
+    row = ent // 16 * 2 + lax.rem(ent, 2)
+    core = lax.rem(ent // 2, CORE)
+    code = slot + 16 * (fresh.astype(jnp.int32) + 2 * first)
+    code = row + 16 * (core + CORE * (column + X * code))
+    return code.reshape(-1), most
+
+
+def neighbour_entries(place, code, k, what):
     z, x, core = place[0], place[1], place[2]
-    for k, out in ((1, s1), (2, s2), (3, s3)):
-        base = (z * (X * CORE) + lax.rem(x + k, X) * CORE + core) * ENTRIES
-
-        @pl.loop(0, ENTRIES)
-        def _(e):
-            block = ent[base + e]
-            row = slab_row(block)
-            sl = slot[base + e]
-            mine = (first[base + e] == e) & (owner_x(block) == x)
-            same_core = owner_core(block) == core
-
-            @pl.when(mine & same_core)
-            def _():
-                out[sl] = own_ref[row]
-
-            @pl.when(mine & jnp.logical_not(same_core))
-            def _():
-                out[sl] = oth_ref[row]
-
-
-def scatter_kernel(place, ent, slot, first, g0, g1, g2, g3, own_out, oth_out, acc):
-    z, x, core = place[0], place[1], place[2]
+    base = ((z * X + ((x + k) & (X - 1))) * CORE + core) * ENTRIES
+
+    @pl.loop(0, ENTRIES)
+    def _(e):
+        row, owner_core, owner_x, sl, fresh, _ = fields(code[base + e])
+
+        @pl.when((fresh == 1) & (owner_x == x))
+        def _():
+            what(e, row, owner_core == core, sl)
+
+
+def gather_kernel(place, code, own, oth, s1, s2, s3, sem):
+    def all_copies(act):
+        for k, out in ((1, s1), (2, s2), (3, s3)):
+
+            def one(e, row, same_core, sl, k=k, out=out):
+                for source, chosen in ((own, same_core), (oth, jnp.logical_not(same_core))):
+
+                    @pl.when(chosen)
+                    def _(source=source):
+                        done = sem.at[(k - 1) * ENTRIES + e]
+                        act(pltpu.make_async_copy(source.at[row], out.at[sl], done))
+
+            neighbour_entries(place, code, k, one)
+
+    all_copies(lambda copy: copy.start())
+    all_copies(lambda copy: copy.wait())
+
+
+def scatter_kernel(place, code, g0, g1, g2, g3, own_out, oth_out, stage, acc, sem):
+    buffers = ((0, g0), (1, g1), (2, g2), (3, g3))
+
+    def copy(k, buf, e, sl):
+        place_of = k * ENTRIES + e
+        return pltpu.make_async_copy(buf.at[sl], stage.at[place_of], sem.at[place_of])
+
+    for k, buf in buffers:
+
+        def start(e, row, same_core, sl, k=k, buf=buf):
+            copy(k, buf, e, sl).start()
+
+        neighbour_entries(place, code, k, start)
+
     acc[...] = jnp.zeros_like(acc)
-    for k, buf in ((0, g0), (1, g1), (2, g2), (3, g3)):
-        base = (z * (X * CORE) + lax.rem(x + k, X) * CORE + core) * ENTRIES
-
-        @pl.loop(0, ENTRIES)
-        def _(e):
-            block = ent[base + e]
-            mine = (first[base + e] == e) & (owner_x(block) == x)
-
-            @pl.when(mine)
-            def _():
-                away = jnp.where(owner_core(block) == core, 0, ENTRIES)
-                row = slab_row(block) + away
-                acc[row] += buf[slot[base + e]].astype(jnp.float32)
+    for k, buf in buffers:
+
+        def add(e, row, same_core, sl, k=k, buf=buf):
+            copy(k, buf, e, sl).wait()
+            to = row + jnp.where(same_core, 0, ENTRIES)
+            acc[to] += stage[k * ENTRIES + e].astype(jnp.float32)
+
+        neighbour_entries(place, code, k, add)
 
     own_out[...] = acc[:ENTRIES].astype(jnp.bfloat16)
     oth_out[...] = acc[ENTRIES:].astype(jnp.bfloat16)
@@ -96,48 +132,64 @@
 
 
 def attend_kernel(
-    place, ent, slot, first,
-    qd, own_ref, oth_ref, r1, r2, r3, mask,
-    out, g0, g1, g2, g3,
-    kc, vc, kt, vt, qs, dos, s_scr, p_scr, d_scr, dk, dv,
+    place, code, qd_in, own, oth, r1, r2, r3, mask_in,
+    out_to, g0, g1, g2, g3,
+    qd, tiles, mask, out, kc, vc, kt, vt, qs, dos, s_scr, p_scr, d_scr, dk, dv,
+    tile_sem, part_sem, out_sem, back_sem,
 ):
     z, x, core = place[0], place[1], place[2]
-    me = z * (X * CORE) + x * CORE + core
-    base = me * ENTRIES
+    base = ((z * X + x) * CORE + core) * ENTRIES
     scale = WIDTH**-0.5
     rows = 2 * BLOCK
     contract_last = (((1,), (1,)), ((), ()))
 
+    def query_copy(b):
+        half = pl.ds(b * 4, 4)
+        return pltpu.make_async_copy(qd_in.at[half], qd.at[half], part_sem.at[0, b])
+
+    def mask_copy(b):
+        half = pl.ds(b * LISTED, LISTED)
+        return pltpu.make_async_copy(mask_in.at[half], mask.at[half], part_sem.at[1, b])
+
+    def out_copy(b):
+        half = pl.ds(b * 4, 4)
+        return pltpu.make_async_copy(out.at[half], out_to.at[half], out_sem.at[b])
+
     @pl.loop(0, 2)
     def _(b):
+        query_copy(b).start()
+        mask_copy(b).start()
+
         @pl.loop(0, LISTED)
         def _(l):
-            e = base + b * LISTED + l
-            block = ent[e]
-            row = slab_row(block)
-            sl = slot[e]
-            away = lax.rem(x - owner_x(block) + X, X)
-            same_core = owner_core(block) == core
-            at = pl.ds(pl.multiple_of(l * BLOCK, BLOCK), BLOCK)
-
-            def take(tile):
-                tile = tile.reshape(4, 2, QUARTER, WIDTH)
-                kc[at, :] = tile[:, 0].reshape(BLOCK, WIDTH)
-                vc[at, :] = tile[:, 1].reshape(BLOCK, WIDTH)
-
-            @pl.when((away == 0) & same_core)
-            def _():
-                take(own_ref[row])
-
-            @pl.when((away == 0) & jnp.logical_not(same_core))
-            def _():
-                take(oth_ref[row])
-
-            for k, buf in ((1, r1), (2, r2), (3, r3)):
-
-                @pl.when(away == k)
-                def _():
-                    take(buf[sl])
+            e = b * LISTED + l
+            row, owner_core, owner_x, sl, _, _ = fields(code[base + e])
+            away = (x - owner_x) & (X - 1)
+            here = (away == 0) & (owner_core == core)
+            beside = (away == 0) & (owner_core != core)
+            sources = ((own, row, here), (oth, row, beside), (r1, sl, away == 1))
+            sources += ((r2, sl, away == 2), (r3, sl, away == 3))
+            for source, at, chosen in sources:
+
+                @pl.when(chosen)
+                def _(source=source, at=at):
+                    pltpu.make_async_copy(source.at[at], tiles.at[e], tile_sem.at[e]).start()
+
+    @pl.loop(0, 2)
+    def _(b):
+        query_copy(b).wait()
+        mask_copy(b).wait()
+
+        @pl.loop(0, LISTED)
+        def _(l):
+            e = b * LISTED + l
+            pltpu.make_async_copy(own.at[0], tiles.at[e], tile_sem.at[e]).wait()
+
+        for l in range(LISTED):
+            at = slice(l * BLOCK, (l + 1) * BLOCK)
+            tile = tiles[b * LISTED + l].reshape(4, 2, QUARTER, WIDTH)
+            kc[at, :] = tile[:, 0].reshape(BLOCK, WIDTH)
+            vc[at, :] = tile[:, 1].reshape(BLOCK, WIDTH)
 
         for l in range(LISTED):
             at = slice(l * BLOCK, (l + 1) * BLOCK)
@@ -205,27 +257,40 @@
         dk[here] = jnp.dot(d_scr[...], qs[...], preferred_element_type=jnp.float32).reshape(LISTED, BLOCK, WIDTH)
         dv[here] = jnp.dot(p_scr[...], dos[...], preferred_element_type=jnp.float32).reshape(LISTED, BLOCK, WIDTH)
 
+        out_copy(b).start()
+
     @pl.loop(LISTED, ENTRIES)
     def _(e):
-        f = first[base + e]
-
-        @pl.when(f != e)
+        *_, fresh, f = fields(code[base + e])
+
+        @pl.when(fresh == 0)
         def _():
             dk[f] += dk[e]
             dv[f] += dv[e]
 
+    def back_copies(e, act):
+        _, _, owner_x, sl, fresh, _ = fields(code[base + e])
+        away = (x - owner_x) & (X - 1)
+        for k, buf in ((0, g0), (1, g1), (2, g2), (3, g3)):
+
+            @pl.when((fresh == 1) & (away == k))
+            def _(buf=buf):
+                act(pltpu.make_async_copy(tiles.at[e], buf.at[sl], back_sem.at[e]))
+
     @pl.loop(0, ENTRIES)
     def _(e):
-        away = lax.rem(x - owner_x(ent[base + e]) + X, X)
-        sl = slot[base + e]
-        keep = first[base + e] == e
-        for k, buf in ((0, g0), (1, g1), (2, g2), (3, g3)):
-
-            @pl.when(keep & (away == k))
-            def _():
-                parts = [dk[e].reshape(4, 1, QUARTER, WIDTH), dv[e].reshape(4, 1, QUARTER, WIDTH)]
-                tile = jnp.concatenate(parts, axis=1).astype(jnp.bfloat16)
-                buf[sl] = tile.reshape(2 * BLOCK, WIDTH)
+        parts = [dk[e].reshape(4, 1, QUARTER, WIDTH), dv[e].reshape(4, 1, QUARTER, WIDTH)]
+        tile = jnp.concatenate(parts, axis=1).astype(jnp.bfloat16)
+        tiles[e] = tile.reshape(2 * BLOCK, WIDTH)
+        back_copies(e, lambda copy: copy.start())
+
+    @pl.loop(0, ENTRIES)
+    def _(e):
+        back_copies(e, lambda copy: copy.wait())
+
+    @pl.loop(0, 2)
+    def _(b):
+        out_copy(b).wait()
 
 
 def blocks(count):
@@ -257,13 +322,17 @@
 
 
 def attend(slots, *operands):
+    outs = jax.ShapeDtypeStruct((HEAD, 2, GROUP, QUARTER, WIDTH), jnp.bfloat16)
     return pl.pallas_call(
         attend_kernel,
-        out_shape=[jax.ShapeDtypeStruct((HEAD, 2, GROUP, QUARTER, WIDTH), jnp.bfloat16), blocks(ENTRIES)]
-        + [blocks(slots)] * 3,
-        in_specs=[SMEM] * 4 + [VMEM] * 7,
-        out_specs=[VMEM] * 5,
+        out_shape=[outs, blocks(ENTRIES)] + [blocks(slots)] * 3,
+        in_specs=[SMEM] * 2 + [HBM] * 7,
+        out_specs=[HBM] * 5,
         scratch_shapes=[
+            pltpu.VMEM((HEAD, 2, GROUP, QUARTER, WIDTH), jnp.bfloat16),
+            pltpu.VMEM((ENTRIES, 2 * BLOCK, WIDTH), jnp.bfloat16),
+            pltpu.VMEM((ENTRIES, BLOCK, BLOCK), jnp.float32),
+            pltpu.VMEM((HEAD, 2, GROUP, QUARTER, WIDTH), jnp.bfloat16),
             pltpu.VMEM((LISTED * BLOCK, WIDTH), jnp.bfloat16),
             pltpu.VMEM((LISTED * BLOCK, WIDTH), jnp.bfloat16),
             pltpu.VMEM((WIDTH, LISTED * BLOCK), jnp.bfloat16),
@@ -275,6 +344,10 @@
             pltpu.VMEM((LISTED * BLOCK, GROUP * BLOCK), jnp.bfloat16),
             pltpu.VMEM((ENTRIES, BLOCK, WIDTH), jnp.float32),
             pltpu.VMEM((ENTRIES, BLOCK, WIDTH), jnp.float32),
+            DMA((ENTRIES,)),
+            DMA((2, 2)),
+            DMA((2,)),
+            DMA((ENTRIES,)),
         ],
         compiler_params=params(24),
         cost_estimate=pl.CostEstimate(
@@ -284,15 +357,16 @@
 
 
 def between(slots, place, tables, own, queries, output_gradient, sess):
-    ent, kind, slot, first = tables
+    code, ent, kind = tables
     other = shift(own, "core", 1)
     sends = pl.pallas_call(
         gather_kernel,
         out_shape=[blocks(slots)] * 3,
-        in_specs=[SMEM] * 4 + [VMEM] * 2,
-        out_specs=[VMEM] * 3,
-        compiler_params=params(8),
-    )(place, ent, slot, first, own, other)
+        in_specs=[SMEM] * 2 + [HBM] * 2,
+        out_specs=[HBM] * 3,
+        scratch_shapes=[DMA((3 * ENTRIES,))],
+        compiler_params=params(4),
+    )(place, code, own, other)
     now, *sends = lax.optimization_barrier((place, *sends))
     fetched = [shift(sends[k - 1], "x", k) for k in (1, 2, 3)]
     mask = masks(now, ent, kind, sess)
@@ -301,7 +375,7 @@
     qd = exchange(qd.transpose(2, 0, 3, 1, 4), "head")
 
     out, g0, g1, g2, g3 = attend(
-        slots, place, ent, slot, first, qd, own, other, *fetched, mask
+        slots, place, code, qd, own, other, *fetched, mask
     )
 
     returned = [shift(g, "x", -k) for k, g in ((1, g1), (2, g2), (3, g3))]
@@ -310,11 +384,15 @@
     own_sum, other_sum = pl.pallas_call(
         scatter_kernel,
         out_shape=[blocks(ENTRIES)] * 2,
-        in_specs=[SMEM] * 4 + [VMEM] * 4,
+        in_specs=[SMEM] * 2 + [HBM] * 4,
         out_specs=[VMEM] * 2,
-        scratch_shapes=[pltpu.VMEM((2 * ENTRIES, 2 * BLOCK, WIDTH), jnp.float32)],
+        scratch_shapes=[
+            pltpu.VMEM((4 * ENTRIES, 2 * BLOCK, WIDTH), jnp.bfloat16),
+            pltpu.VMEM((2 * ENTRIES, 2 * BLOCK, WIDTH), jnp.float32),
+            DMA((4 * ENTRIES,)),
+        ],
         compiler_params=params(14),
-    )(place, ent, slot, first, g0, *returned)
+    )(place, code, g0, *returned)
     return out, own_sum, other_sum
 
 
@@ -322,21 +400,8 @@
     where = [lax.axis_index(axis) for axis in ("z", "x", "core")]
     place = jnp.stack(where).astype(jnp.int32)
 
-    ent = kv_list.reshape(CTX, ENTRIES)
-    order = jnp.arange(ENTRIES, dtype=jnp.int32)
-    equal = ent[:, :, None] == ent[:, None, :]
-    first = jnp.min(jnp.where(equal, order[None, None, :], ENTRIES), axis=2)
-    fresh = first == order[None, :]
-    column = owner_x(ent)
-    before = (
-        fresh[:, None, :]
-        & (column[:, :, None] == column[:, None, :])
-        & (order[None, None, :] < first[:, :, None])
-    )
-    slot = jnp.sum(before.astype(jnp.int32), axis=2)
-    home = lax.rem(jnp.arange(CTX, dtype=jnp.int32) // CORE, X)
-    most = jnp.max(jnp.where(column == home[:, None], 0, slot + 1))
-    tables = (ent.reshape(-1), kv_type.reshape(-1), slot.reshape(-1), first.reshape(-1))
+    code, most = coded(kv_list)
+    tables = (code, kv_list.reshape(-1), kv_type.reshape(-1))
     sess = session_id.astype(jnp.float32).reshape(-1, BLOCK)
 
     kv = jnp.stack([keys, values]).transpose(2, 0, 1, 3)

time: 199 us -> 200 us (level)
  local copies, waits for them, and re-layouts: 15.9 us -> 10.5 us
  Pallas kernels: 20.6 us -> 24.3 us
  waiting for transfers between devices: 85.6 us -> 87.7 us
    cond x28 -> x20, local copies, waits for them, and re-layouts: 8.68 us -> 3.32 us
    pallas_call x1, Pallas kernels: 3.81 us -> 6.49 us  [between(): pl.pallas_call(scatter_kernel, out_shape=[blocks(ENTRIES)] * 2, in_specs=...]
where the time goes in v4:
time: 200 us; the launch traced here: 199 us
  waiting for transfers between devices  87.7 us (44%)
  starting transfers between devices  66.9 us (33%)
  Pallas kernels  24.3 us (12%)
  local copies, waits for them, and re-layouts  10.5 us (5%)
  other arithmetic  5.6 us (3%)
  between operations  2.77 us (1%)
    all_to_all x4, waiting for transfers between devices, exchange(): return lax.all_to_all(array, axis, split_axis=0, concat_axis=0, tiled=True)  49 us
    ppermute x8, waiting for transfers between devices, shift(): lax.ppermute(array, axis, [(i, (i + by) % size) for i in range(size)])  38.7 us
    all_to_all x4, starting transfers between devices, exchange(): return lax.all_to_all(array, axis, split_axis=0, concat_axis=0, tiled=True)  38.3 us
    ppermute x8, starting transfers between devices, shift(): lax.ppermute(array, axis, [(i, (i + by) % size) for i in range(size)])  28.6 us
    pallas_call x1, Pallas kernels, attend(): pl.pallas_call(attend_kernel, out_shape=[outs, blocks(ENTRIES)] + [blocks...  13.1 us
    pallas_call x1, Pallas kernels, between(): pl.pallas_call(scatter_kernel, out_shape=[blocks(ENTRIES)] * 2, in_specs=...  6.49 us
  transfers between devices with their start and end apart: 12, of which 10 were waited for; matrix products, arithmetic and copies ran while one was open for 2% of the time, Pallas kernels for 2%

profile of v4, /device:TPU:1, one launch (start us, length us, event | category | flops | bytes accessed | tf_op | source)
XLA Modules:
  0.0 198.6 jit_solution(2209068843752972000)
XLA Ops:
  1.5 1.3 broadcast_in_dim.30
  2.8 17.3 %all-to-all-start.8 = ((bf16[64,2,32,128]{3,2,1,0:T(8,128)(2,1)}), bf16[64,2,32,128]{3,2,1,0:T(8,128)(2,1)S(1)}, u32[]{:S(2)}, u32[]{:S(2)}) async-start(bf16[64,2,32,128]{3,2,1,0:T(8,128)(2,1)} %bitcast.23), calls=%async_computation.8 | async-start | bytes 2097152 | tf_op jit(solution)/shard_map/all_to_all | solution.py:310
  23.8 23.7 %all-to-all-done.8 = bf16[64,2,32,128]{3,2,1,0:T(8,128)(2,1)S(1)} async-done(((bf16[64,2,32,128]{3,2,1,0:T(8,128)(2,1)}), bf16[64,2,32,128]{3,2,1,0:T(8,128)(2,1)S(1)}, u32[]{:S(2)}, u32[]{:S(2)}) %all-to-all-start.8) | async-done | bytes 1048608 | tf_op jit(solution)/shard_map/all_to_all | solution.py:310
  47.6 105.0 %conditional.1 = (bf16[8,2,8,32,128]{4,3,2,1,0:T(8,128)(2,1)}, bf16[16,256,128]{2,1,0:T(8,128)(2,1)}, bf16[16,256,128]{2,1,0:T(8,128)(2,1)}) conditional(s32[]{:T(128)} %clamp.3, (bf16[32,64,128]{2,1,0:T(8,128)(2,1)S(1)}, bf16[32,64,128]{2,1,0:T(8,128)(2,1)S(1)}, bf16[64,2,32,128]{3,2,1,0:T(8,128)(2,1)S(1)}, ...), branch_computations={%region_3.4_spmd, %region_4.5_spmd, %region_5.6_spmd, %region_6.7_... | conditional | flops 2686998528 | bytes 91357920 | solution.py:412
  48.3 1.1 maximum_bitcast_fusion
  49.4 5.4 %all-to-all-start = ((bf16[8,2,8,32,128]{4,3,2,1,0:T(8,128)(2,1)}), bf16[8,2,8,32,128]{4,3,2,1,0:T(8,128)(2,1)S(1)}, u32[]{:S(2)}, u32[]{:S(2)}) async-start(bf16[8,2,8,32,128]{4,3,2,1,0:T(8,128)(2,1)} %maximum_bitcast_fusion), calls=%async_computation | async-start | bytes 2097152 | tf_op jit(solution)/shard_map/cond/branch_0_fun/all_to_all | solution.py:310
  54.7 4.5 %collective-permute-start = (bf16[16,256,128]{2,1,0:T(8,128)(2,1)S(1)}, bf16[16,256,128]{2,1,0:T(8,128)(2,1)S(1)}, u32[]{:S(2)}, u32[]{:S(2)}) collective-permute-start(bf16[16,256,128]{2,1,0:T(8,128)(2,1)S(1)} %bitcast.44), channel_id=1, source_target_pairs={{0,8},{8,0},{1,9},{9,1},{2,10},{10,2},{3,11},{11,3},{4,12},{12,4},... | collective-permute-start | bytes 3145736 | tf_op jit(solution)/shard_map/cond/branch_0_fun/ppermute | solution.py:302
  59.7 1.9 collective-permute-done.oth
  61.6 2.4 %branch_0_fun.4 = (bf16[7,256,128]{2,1,0:T(8,128)(2,1)}, bf16[7,256,128]{2,1,0:T(8,128)(2,1)}, bf16[7,256,128]{2,1,0:T(8,128)(2,1)}) custom-call(s32[3]{0:T(128)S(1)} %get-tuple-element.75.place, s32[1024]{0:T(1024)S(1)} %fusion.7.code, bf16[16,256,128]{2,1,0:T(8,128)(2,1)S(1)} %bitcast.45, bf16[16,256,128]{2,1,0:T(8,128)(2,1)S(1)} %collective-permute-done.oth), custom_call_target="tpu_custom_call" | custom-call | tf_op jit(solution)/shard_map/cond/branch_0_fun/pallas_call | solution.py:362
  64.0 3.1 %collective-permute-start.1 = (bf16[7,256,128]{2,1,0:T(8,128)(2,1)}, bf16[7,256,128]{2,1,0:T(8,128)(2,1)}, u32[]{:S(2)}, u32[]{:S(2)}) collective-permute-start(bf16[7,256,128]{2,1,0:T(8,128)(2,1)} %get-tuple-element.72), channel_id=1, source_target_pairs={{0,16},{16,32},{32,48},{48,0},{1,17},{17,33},{33,49},{49,1},{2,18}... | collective-permute-start | bytes 1376264 | tf_op jit(solution)/shard_map/cond/branch_0_fun/ppermute | solution.py:302
  67.1 4.4 %collective-permute-start.2 = (bf16[7,256,128]{2,1,0:T(8,128)(2,1)}, bf16[7,256,128]{2,1,0:T(8,128)(2,1)}, u32[]{:S(2)}, u32[]{:S(2)}) collective-permute-start(bf16[7,256,128]{2,1,0:T(8,128)(2,1)} %get-tuple-element.73), channel_id=1, source_target_pairs={{0,32},{16,48},{32,0},{48,16},{1,33},{17,49},{33,1},{49,17},{2,34}... | collective-permute-start | bytes 1376264 | tf_op jit(solution)/shard_map/cond/branch_0_fun/ppermute | solution.py:302
  71.5 3.1 %collective-permute-start.3 = (bf16[7,256,128]{2,1,0:T(8,128)(2,1)}, bf16[7,256,128]{2,1,0:T(8,128)(2,1)}, u32[]{:S(2)}, u32[]{:S(2)}) collective-permute-start(bf16[7,256,128]{2,1,0:T(8,128)(2,1)} %get-tuple-element.74), channel_id=1, source_target_pairs={{0,48},{16,0},{32,16},{48,32},{1,49},{17,1},{33,17},{49,33},{2,50}... | collective-permute-start | bytes 1376264 | tf_op jit(solution)/shard_map/cond/branch_0_fun/ppermute | solution.py:302
  74.8 2.3 %branch_0_fun.5.mask_in = f32[16,128,128]{2,1,0:T(8,128)S(1)} custom-call(s32[3]{0:T(128)S(1)} %get-tuple-element.75.place, s32[1024]{0:T(1024)S(1)} %get-tuple-element.76.ent, s32[1024]{0:T(1024)S(1)} %reshape.180.kind, f32[128,128]{1,0:T(8,128)S(1)} %bitcast.65), custom_call_target="tpu_custom_call" | custom-call | flops 2097152 | bytes 1048576 | tf_op jit(solution)/shard_map/cond/branch_0_fun/pallas_call | solution.py:314
  77.1 2.0 %collective-permute-done.1.r1 = bf16[7,256,128]{2,1,0:T(8,128)(2,1)} collective-permute-done((bf16[7,256,128]{2,1,0:T(8,128)(2,1)}, bf16[7,256,128]{2,1,0:T(8,128)(2,1)}, u32[]{:S(2)}, u32[]{:S(2)}) %collective-permute-start.1) | collective-permute-done | bytes 458784 | tf_op jit(solution)/shard_map/cond/branch_0_fun/ppermute | solution.py:302
  79.2 10.8 %collective-permute-done.2.r2 = bf16[7,256,128]{2,1,0:T(8,128)(2,1)} collective-permute-done((bf16[7,256,128]{2,1,0:T(8,128)(2,1)}, bf16[7,256,128]{2,1,0:T(8,128)(2,1)}, u32[]{:S(2)}, u32[]{:S(2)}) %collective-permute-start.2) | collective-permute-done | bytes 458784 | tf_op jit(solution)/shard_map/cond/branch_0_fun/ppermute | solution.py:302
  90.0 1.2 collective-permute-done.3.r3
  91.2 13.1 %branch_0_fun.6 = (bf16[8,2,8,32,128]{4,3,2,1,0:T(8,128)(2,1)}, bf16[16,256,128]{2,1,0:T(8,128)(2,1)S(1)}, bf16[7,256,128]{2,1,0:T(8,128)(2,1)S(1)}, bf16[7,256,...) custom-call(s32[3]{0:T(128)S(1)} %get-tuple-element.75.place, s32[1024]{0:T(1024)S(1)} %fusion.7.code, ...), custom_call_target="tpu_custom_call" | custom-call | flops 2684354560 | bytes 8388608 | tf_op jit(solution)/shard_map/cond/branch_0_fun/pallas_call | solution.py:326
  107.6 7.1 %all-to-all-start.1 = ((bf16[8,2,8,32,128]{4,3,2,1,0:T(8,128)(2,1)}), bf16[8,2,8,32,128]{4,3,2,1,0:T(8,128)(2,1)}, u32[]{:S(2)}, u32[]{:S(2)}) async-start(bf16[8,2,8,32,128]{4,3,2,1,0:T(8,128)(2,1)} %get-tuple-element.82), calls=%async_computation.1 | async-start | bytes 2097152 | tf_op jit(solution)/shard_map/cond/branch_0_fun/all_to_all | solution.py:310
  114.7 5.2 %collective-permute-start.4 = (bf16[7,256,128]{2,1,0:T(8,128)(2,1)}, bf16[7,256,128]{2,1,0:T(8,128)(2,1)S(1)}, u32[]{:S(2)}, u32[]{:S(2)}) collective-permute-start(bf16[7,256,128]{2,1,0:T(8,128)(2,1)} %copy-done.32), channel_id=1, source_target_pairs={{0,48},{16,0},{32,16},{48,32},{1,49},{17,1},{33,17},{49,33},{2,50}... | collective-permute-start | bytes 1376264 | tf_op jit(solution)/shard_map/cond/branch_0_fun/ppermute | solution.py:302
  119.9 3.5 %collective-permute-start.5 = (bf16[7,256,128]{2,1,0:T(8,128)(2,1)S(1)}, bf16[7,256,128]{2,1,0:T(8,128)(2,1)S(1)}, u32[]{:S(2)}, u32[]{:S(2)}) collective-permute-start(bf16[7,256,128]{2,1,0:T(8,128)(2,1)S(1)} %copy-done.31), channel_id=1, source_target_pairs={{0,32},{16,48},{32,0},{48,16},{1,33},{17,49},{33,1},{49,17},{2,34}... | collective-permute-start | bytes 1376264 | tf_op jit(solution)/shard_map/cond/branch_0_fun/ppermute | solution.py:302
  123.4 1.9 collective-permute-start.6
  125.3 4.8 %collective-permute-done.4.g1 = bf16[7,256,128]{2,1,0:T(8,128)(2,1)S(1)} collective-permute-done((bf16[7,256,128]{2,1,0:T(8,128)(2,1)}, bf16[7,256,128]{2,1,0:T(8,128)(2,1)S(1)}, u32[]{:S(2)}, u32[]{:S(2)}) %collective-permute-start.4) | collective-permute-done | bytes 458784 | tf_op jit(solution)/shard_map/cond/branch_0_fun/ppermute | solution.py:302
  130.1 4.1 %collective-permute-done.5.g2 = bf16[7,256,128]{2,1,0:T(8,128)(2,1)S(1)} collective-permute-done((bf16[7,256,128]{2,1,0:T(8,128)(2,1)S(1)}, bf16[7,256,128]{2,1,0:T(8,128)(2,1)S(1)}, u32[]{:S(2)}, u32[]{:S(2)}) %collective-permute-start.5) | collective-permute-done | bytes 458784 | tf_op jit(solution)/shard_map/cond/branch_0_fun/ppermute | solution.py:302
  134.2 11.4 %collective-permute-done.6.g3 = bf16[7,256,128]{2,1,0:T(8,128)(2,1)S(1)} collective-permute-done((bf16[7,256,128]{2,1,0:T(8,128)(2,1)S(1)}, bf16[7,256,128]{2,1,0:T(8,128)(2,1)S(1)}, u32[]{:S(2)}, u32[]{:S(2)}) %collective-permute-start.6) | collective-permute-done | bytes 458784 | tf_op jit(solution)/shard_map/cond/branch_0_fun/ppermute | solution.py:302
  145.6 6.5 %branch_0_fun.7 = (bf16[16,256,128]{2,1,0:T(8,128)(2,1)}, bf16[16,256,128]{2,1,0:T(8,128)(2,1)}) custom-call(s32[3]{0:T(128)S(1)} %copy-done.45, s32[1024]{0:T(1024)S(1)} %fusion.7.code, bf16[16,256,128]{2,1,0:T(8,128)(2,1)S(1)} %copy-done.10, bf16[7,256,128]{2,1,0:T(8,128)(2,1)S(1)} %collective-permute-done.4.g1, ...), custom_call_target="tpu_custom_call" | custom-call | tf_op jit(solution)/shard_map/cond/branch_0_fun/pallas_call | solution.py:384
  152.6 3.0 %collective-permute-start.28 = (bf16[16,256,128]{2,1,0:T(8,128)(2,1)}, bf16[16,256,128]{2,1,0:T(8,128)(2,1)S(1)}, u32[]{:S(2)}, u32[]{:S(2)}) collective-permute-start(bf16[16,256,128]{2,1,0:T(8,128)(2,1)} %get-tuple-element.177), channel_id=1, source_target_pairs={{0,8},{8,0},{1,9},{9,1},{2,10},{10,2},{3,11},{11,3},{4,12},{12,4},... | collective-permute-start | bytes 3145736 | tf_op jit(solution)/shard_map/ppermute | solution.py:302
  155.6 2.5 %collective-permute-done.28 = bf16[16,256,128]{2,1,0:T(8,128)(2,1)S(1)} collective-permute-done((bf16[16,256,128]{2,1,0:T(8,128)(2,1)}, bf16[16,256,128]{2,1,0:T(8,128)(2,1)S(1)}, u32[]{:S(2)}, u32[]{:S(2)}) %collective-permute-start.28) | collective-permute-done | bytes 1048608 | tf_op jit(solution)/shard_map/ppermute | solution.py:302
  158.1 2.5 %add_convert_fusion = bf16[16,256,128]{2,1,0:T(8,128)(2,1)} fusion(bf16[16,256,128]{2,1,0:T(8,128)(2,1)S(1)} %collective-permute-done.28, bf16[16,256,128]{2,1,0:T(8,128)(2,1)} %get-tuple-element.176), kind=kLoop, calls=%fused_computation.68 | loop fusion | flops 2097152 | bytes 3145728 | tf_op jit(solution)/shard_map/convert_element_type | solution.py:419
  160.5 8.6 %all-to-all-start.9 = ((bf16[64,2,32,128]{3,2,1,0:T(8,128)(2,1)}), bf16[64,2,32,128]{3,2,1,0:T(8,128)(2,1)S(1)}, u32[]{:S(2)}, u32[]{:S(2)}) async-start(bf16[64,2,32,128]{3,2,1,0:T(8,128)(2,1)} %bitcast.30), calls=%async_computation.9 | async-start | bytes 2097152 | tf_op jit(solution)/shard_map/all_to_all | solution.py:310
  169.1 1.3 fusion.59
  170.4 1.4 copy_bitcast_fusion
  171.8 25.3 %all-to-all-done.9 = bf16[64,2,32,128]{3,2,1,0:T(8,128)(2,1)S(1)} async-done(((bf16[64,2,32,128]{3,2,1,0:T(8,128)(2,1)}), bf16[64,2,32,128]{3,2,1,0:T(8,128)(2,1)S(1)}, u32[]{:S(2)}, u32[]{:S(2)}) %all-to-all-start.9) | async-done | bytes 1048608 | tf_op jit(solution)/shard_map/all_to_all | solution.py:310
  (71 shorter events, 8.7 us)
Async XLA Ops:
  2.8 17.3 %copy-start.52 = (s32[128,8]{0,1:T(8,128)S(1)}, s32[128,8]{0,1:T(8,128)}, u32[]{:S(2)}) copy-start(s32[128,8]{0,1:T(8,128)} %param.15) | copy-start | bytes 12292
  2.8 20.9 %copy-start.51 = (s32[16384]{0:T(1024)S(1)}, s32[16384]{0:T(1024)}, u32[]{:S(2)}) copy-start(s32[16384]{0:T(1024)} %param.17) | copy-start | bytes 196612
  2.8 44.8 %copy-start.37 = (bf16[32,64,128]{2,1,0:T(8,128)(2,1)S(1)}, bf16[32,64,128]{2,1,0:T(8,128)(2,1)}, u32[]{:S(2)}) copy-start(bf16[32,64,128]{2,1,0:T(8,128)(2,1)} %param.11) | copy-start | bytes 1572868
  2.8 44.8 %copy-start.39 = (bf16[32,64,128]{2,1,0:T(8,128)(2,1)S(1)}, bf16[32,64,128]{2,1,0:T(8,128)(2,1)}, u32[]{:S(2)}) copy-start(bf16[32,64,128]{2,1,0:T(8,128)(2,1)} %param.14) | copy-start | bytes 1572868
  2.8 44.8 %copy-start.48 = (s32[128,8]{0,1:T(8,128)S(1)}, s32[128,8]{0,1:T(8,128)}, u32[]{:S(2)}) copy-start(s32[128,8]{0,1:T(8,128)} %param.16) | copy-start | bytes 12292
  2.8 44.7 %all-to-all-start.8 = ((bf16[64,2,32,128]{3,2,1,0:T(8,128)(2,1)}), bf16[64,2,32,128]{3,2,1,0:T(8,128)(2,1)S(1)}, u32[]{:S(2)}, u32[]{:S(2)}) async-start(bf16[64,2,32,128]{3,2,1,0:T(8,128)(2,1)} %bitcast.23), calls=%async_computation.8 | async-start | bytes 2097152 | tf_op jit(solution)/shard_map/all_to_all | solution.py:310
  47.6 14.0 %copy-start.33 = (bf16[64,2,32,128]{3,2,1,0:T(8,128)(2,1)}, bf16[64,2,32,128]{3,2,1,0:T(8,128)(2,1)S(1)}, u32[]{:S(2)}) copy-start(bf16[64,2,32,128]{3,2,1,0:T(8,128)(2,1)S(1)} %get-tuple-element.186) | copy-start | bytes 3145732 | tf_op jit(solution)/shard_map/cond
  47.6 43.6 %copy-start.44 = (s32[3]{0:T(128)}, s32[3]{0:T(128)S(1)}, u32[]{:S(2)}) copy-start(s32[3]{0:T(128)S(1)} %get-tuple-element.75.place) | copy-start | bytes 40 | tf_op jit(solution)/shard_map/cond
  49.4 41.8 %all-to-all-start = ((bf16[8,2,8,32,128]{4,3,2,1,0:T(8,128)(2,1)}), bf16[8,2,8,32,128]{4,3,2,1,0:T(8,128)(2,1)S(1)}, u32[]{:S(2)}, u32[]{:S(2)}) async-start(bf16[8,2,8,32,128]{4,3,2,1,0:T(8,128)(2,1)} %maximum_bitcast_fusion), calls=%async_computation | async-start | bytes 2097152 | tf_op jit(solution)/shard_map/cond/branch_0_fun/all_to_all | solution.py:310
  54.7 6.8 %collective-permute-start = (bf16[16,256,128]{2,1,0:T(8,128)(2,1)S(1)}, bf16[16,256,128]{2,1,0:T(8,128)(2,1)S(1)}, u32[]{:S(2)}, u32[]{:S(2)}) collective-permute-start(bf16[16,256,128]{2,1,0:T(8,128)(2,1)S(1)} %bitcast.44), channel_id=1, source_target_pairs={{0,8},{8,0},{1,9},{9,1},{2,10},{10,2},{3,11},{11,3},{4,12},{12,4},... | collective-permute-start | bytes 3145736 | tf_op jit(solution)/shard_map/cond/branch_0_fun/ppermute | solution.py:302
  64.0 15.2 %collective-permute-start.1 = (bf16[7,256,128]{2,1,0:T(8,128)(2,1)}, bf16[7,256,128]{2,1,0:T(8,128)(2,1)}, u32[]{:S(2)}, u32[]{:S(2)}) collective-permute-start(bf16[7,256,128]{2,1,0:T(8,128)(2,1)} %get-tuple-element.72), channel_id=1, source_target_pairs={{0,16},{16,32},{32,48},{48,0},{1,17},{17,33},{33,49},{49,1},{2,18}... | collective-permute-start | bytes 1376264 | tf_op jit(solution)/shard_map/cond/branch_0_fun/ppermute | solution.py:302
  67.1 22.8 %collective-permute-start.2 = (bf16[7,256,128]{2,1,0:T(8,128)(2,1)}, bf16[7,256,128]{2,1,0:T(8,128)(2,1)}, u32[]{:S(2)}, u32[]{:S(2)}) collective-permute-start(bf16[7,256,128]{2,1,0:T(8,128)(2,1)} %get-tuple-element.73), channel_id=1, source_target_pairs={{0,32},{16,48},{32,0},{48,16},{1,33},{17,49},{33,1},{49,17},{2,34}... | collective-permute-start | bytes 1376264 | tf_op jit(solution)/shard_map/cond/branch_0_fun/ppermute | solution.py:302
  71.5 19.7 %collective-permute-start.3 = (bf16[7,256,128]{2,1,0:T(8,128)(2,1)}, bf16[7,256,128]{2,1,0:T(8,128)(2,1)}, u32[]{:S(2)}, u32[]{:S(2)}) collective-permute-start(bf16[7,256,128]{2,1,0:T(8,128)(2,1)} %get-tuple-element.74), channel_id=1, source_target_pairs={{0,48},{16,0},{32,16},{48,32},{1,49},{17,1},{33,17},{49,33},{2,50}... | collective-permute-start | bytes 1376264 | tf_op jit(solution)/shard_map/cond/branch_0_fun/ppermute | solution.py:302
  104.3 1.0 copy-start.9
  105.3 0.8 copy-start.28
  106.1 0.8 copy-start.30
  106.8 0.8 copy-start.32
  107.6 12.2 %copy-start.31 = (bf16[7,256,128]{2,1,0:T(8,128)(2,1)S(1)}, bf16[7,256,128]{2,1,0:T(8,128)(2,1)}, u32[]{:S(2)}) copy-start(bf16[7,256,128]{2,1,0:T(8,128)(2,1)} %copy-done.30) | copy-start | bytes 1376260 | tf_op jit(solution)/shard_map/cond
  107.6 15.8 %copy-start.29 = (bf16[7,256,128]{2,1,0:T(8,128)(2,1)S(1)}, bf16[7,256,128]{2,1,0:T(8,128)(2,1)}, u32[]{:S(2)}) copy-start(bf16[7,256,128]{2,1,0:T(8,128)(2,1)} %copy-done.28) | copy-start | bytes 1376260 | tf_op jit(solution)/shard_map/cond
  107.6 37.9 %copy-start.10 = (bf16[16,256,128]{2,1,0:T(8,128)(2,1)S(1)}, bf16[16,256,128]{2,1,0:T(8,128)(2,1)}, u32[]{:S(2)}) copy-start(bf16[16,256,128]{2,1,0:T(8,128)(2,1)} %copy-done.9) | copy-start | bytes 3145732 | tf_op jit(solution)/shard_map/cond
  107.6 37.9 %copy-start.45 = (s32[3]{0:T(128)S(1)}, s32[3]{0:T(128)}, u32[]{:S(2)}) copy-start(s32[3]{0:T(128)} %copy-done.44) | copy-start | bytes 40 | tf_op jit(solution)/shard_map/cond
  107.6 37.9 %all-to-all-start.1 = ((bf16[8,2,8,32,128]{4,3,2,1,0:T(8,128)(2,1)}), bf16[8,2,8,32,128]{4,3,2,1,0:T(8,128)(2,1)}, u32[]{:S(2)}, u32[]{:S(2)}) async-start(bf16[8,2,8,32,128]{4,3,2,1,0:T(8,128)(2,1)} %get-tuple-element.82), calls=%async_computation.1 | async-start | bytes 2097152 | tf_op jit(solution)/shard_map/cond/branch_0_fun/all_to_all | solution.py:310
  114.7 15.4 %collective-permute-start.4 = (bf16[7,256,128]{2,1,0:T(8,128)(2,1)}, bf16[7,256,128]{2,1,0:T(8,128)(2,1)S(1)}, u32[]{:S(2)}, u32[]{:S(2)}) collective-permute-start(bf16[7,256,128]{2,1,0:T(8,128)(2,1)} %copy-done.32), channel_id=1, source_target_pairs={{0,48},{16,0},{32,16},{48,32},{1,49},{17,1},{33,17},{49,33},{2,50}... | collective-permute-start | bytes 1376264 | tf_op jit(solution)/shard_map/cond/branch_0_fun/ppermute | solution.py:302
  119.9 14.3 %collective-permute-start.5 = (bf16[7,256,128]{2,1,0:T(8,128)(2,1)S(1)}, bf16[7,256,128]{2,1,0:T(8,128)(2,1)S(1)}, u32[]{:S(2)}, u32[]{:S(2)}) collective-permute-start(bf16[7,256,128]{2,1,0:T(8,128)(2,1)S(1)} %copy-done.31), channel_id=1, source_target_pairs={{0,32},{16,48},{32,0},{48,16},{1,33},{17,49},{33,1},{49,17},{2,34}... | collective-permute-start | bytes 1376264 | tf_op jit(solution)/shard_map/cond/branch_0_fun/ppermute | solution.py:302
  123.4 22.2 %collective-permute-start.6 = (bf16[7,256,128]{2,1,0:T(8,128)(2,1)S(1)}, bf16[7,256,128]{2,1,0:T(8,128)(2,1)S(1)}, u32[]{:S(2)}, u32[]{:S(2)}) collective-permute-start(bf16[7,256,128]{2,1,0:T(8,128)(2,1)S(1)} %copy-done.29), channel_id=1, source_target_pairs={{0,16},{16,32},{32,48},{48,0},{1,17},{17,33},{33,49},{49,1},{2,18}... | collective-permute-start | bytes 1376264 | tf_op jit(solution)/shard_map/cond/branch_0_fun/ppermute | solution.py:302
  152.6 5.5 %collective-permute-start.28 = (bf16[16,256,128]{2,1,0:T(8,128)(2,1)}, bf16[16,256,128]{2,1,0:T(8,128)(2,1)S(1)}, u32[]{:S(2)}, u32[]{:S(2)}) collective-permute-start(bf16[16,256,128]{2,1,0:T(8,128)(2,1)} %get-tuple-element.177), channel_id=1, source_target_pairs={{0,8},{8,0},{1,9},{9,1},{2,10},{10,2},{3,11},{11,3},{4,12},{12,4},... | collective-permute-start | bytes 3145736 | tf_op jit(solution)/shard_map/ppermute | solution.py:302
  160.5 36.5 %all-to-all-start.9 = ((bf16[64,2,32,128]{3,2,1,0:T(8,128)(2,1)}), bf16[64,2,32,128]{3,2,1,0:T(8,128)(2,1)S(1)}, u32[]{:S(2)}, u32[]{:S(2)}) async-start(bf16[64,2,32,128]{3,2,1,0:T(8,128)(2,1)} %bitcast.30), calls=%async_computation.9 | async-start | bytes 2097152 | tf_op jit(solution)/shard_map/all_to_all | solution.py:310

commit v5 on v4

--- a/solution.py
+++ b/solution.py
@@ -69,44 +69,38 @@
 
 
 def gather_kernel(place, code, own, oth, s1, s2, s3, sem):
-    def all_copies(act):
-        for k, out in ((1, s1), (2, s2), (3, s3)):
-
-            def one(e, row, same_core, sl, k=k, out=out):
-                for source, chosen in ((own, same_core), (oth, jnp.logical_not(same_core))):
-
-                    @pl.when(chosen)
-                    def _(source=source):
-                        done = sem.at[(k - 1) * ENTRIES + e]
-                        act(pltpu.make_async_copy(source.at[row], out.at[sl], done))
-
-            neighbour_entries(place, code, k, one)
-
-    all_copies(lambda copy: copy.start())
-    all_copies(lambda copy: copy.wait())
-
-
-def scatter_kernel(place, code, g0, g1, g2, g3, own_out, oth_out, stage, acc, sem):
-    buffers = ((0, g0), (1, g1), (2, g2), (3, g3))
-
-    def copy(k, buf, e, sl):
-        place_of = k * ENTRIES + e
-        return pltpu.make_async_copy(buf.at[sl], stage.at[place_of], sem.at[place_of])
-
-    for k, buf in buffers:
-
-        def start(e, row, same_core, sl, k=k, buf=buf):
-            copy(k, buf, e, sl).start()
+    for k, out in ((1, s1), (2, s2), (3, s3)):
+
+        def start(e, row, same_core, sl, k=k, out=out):
+            for source, chosen in ((own, same_core), (oth, jnp.logical_not(same_core))):
+
+                @pl.when(chosen)
+                def _(source=source):
+                    copy = pltpu.make_async_copy(source.at[row], out.at[sl], sem.at[k, sl])
+                    copy.start()
 
         neighbour_entries(place, code, k, start)
 
+    for k, out in ((1, s1), (2, s2), (3, s3)):
+        z, x, core = place[0], place[1], place[2]
+        base = ((z * X + ((x + k) & (X - 1))) * CORE + core) * ENTRIES
+
+        def count(e, found, base=base):
+            _, _, owner_x, _, fresh, _ = fields(code[base + e])
+            return found + jnp.where((fresh == 1) & (owner_x == x), 1, 0)
+
+        @pl.loop(0, lax.fori_loop(0, ENTRIES, count, 0))
+        def _(sl, k=k, out=out):
+            pltpu.make_async_copy(own.at[0], out.at[sl], sem.at[k, sl]).wait()
+
+
+def scatter_kernel(place, code, g0, g1, g2, g3, own_out, oth_out, acc):
     acc[...] = jnp.zeros_like(acc)
-    for k, buf in buffers:
-
-        def add(e, row, same_core, sl, k=k, buf=buf):
-            copy(k, buf, e, sl).wait()
+    for k, buf in ((0, g0), (1, g1), (2, g2), (3, g3)):
+
+        def add(e, row, same_core, sl, buf=buf):
             to = row + jnp.where(same_core, 0, ENTRIES)
-            acc[to] += stage[k * ENTRIES + e].astype(jnp.float32)
+            acc[to] += buf[sl].astype(jnp.float32)
 
         neighbour_entries(place, code, k, add)
 
@@ -349,7 +343,7 @@
             DMA((2,)),
             DMA((ENTRIES,)),
         ],
-        compiler_params=params(24),
+        compiler_params=params(60),
         cost_estimate=pl.CostEstimate(
             flops=5 * 2 * 2048 * 1024 * 128, bytes_accessed=8 * MIB, transcendentals=2048 * 1024
         ),
@@ -364,7 +358,7 @@
         out_shape=[blocks(slots)] * 3,
         in_specs=[SMEM] * 2 + [HBM] * 2,
         out_specs=[HBM] * 3,
-        scratch_shapes=[DMA((3 * ENTRIES,))],
+        scratch_shapes=[DMA((X, ENTRIES))],
         compiler_params=params(4),
     )(place, code, own, other)
     now, *sends = lax.optimization_barrier((place, *sends))
@@ -384,16 +378,14 @@
     own_sum, other_sum = pl.pallas_call(
         scatter_kernel,
         out_shape=[blocks(ENTRIES)] * 2,
-        in_specs=[SMEM] * 2 + [HBM] * 4,
+        in_specs=[SMEM] * 2 + [VMEM] * 4,
         out_specs=[VMEM] * 2,
-        scratch_shapes=[
-            pltpu.VMEM((4 * ENTRIES, 2 * BLOCK, WIDTH), jnp.bfloat16),
-            pltpu.VMEM((2 * ENTRIES, 2 * BLOCK, WIDTH), jnp.float32),
-            DMA((4 * ENTRIES,)),
-        ],
+        scratch_shapes=[pltpu.VMEM((2 * ENTRIES, 2 * BLOCK, WIDTH), jnp.float32)],
         compiler_params=params(14),
     )(place, code, g0, *returned)
-    return out, own_sum, other_sum
+    from_core = shift(other_sum, "core", 1)
+    column_sum = (own_sum.astype(jnp.float32) + from_core.astype(jnp.float32)).astype(jnp.bfloat16)
+    return out, column_sum
 
 
 def per_device(queries, keys, values, output_gradient, kv_list, kv_type, session_id):
@@ -409,14 +401,12 @@
     own = exchange(kv.reshape(Z * HEAD, 2, QUARTER, WIDTH), ("z", "head"))
     own = own.reshape(ENTRIES, 2 * BLOCK, WIDTH)
 
-    out, own_sum, other_sum = lax.switch(
+    out, column_sum = lax.switch(
         sum((most > few).astype(jnp.int32) for few in SLOTS[:-1]),
         [functools.partial(between, slots) for slots in SLOTS],
         place, tables, own, queries, output_gradient, sess,
     )
 
-    from_core = shift(other_sum, "core", 1)
-    column_sum = (own_sum.astype(jnp.float32) + from_core.astype(jnp.float32)).astype(jnp.bfloat16)
     parts = exchange(column_sum.reshape(Z * HEAD, 2, QUARTER, WIDTH), ("z", "head"))
     parts = parts.reshape(Z, HEAD, 2, QUARTER, WIDTH)
     total = jnp.sum(parts.astype(jnp.float32), axis=0).astype(jnp.bfloat16)

time: 200 us -> 197 us (0.985)
  waiting for transfers between devices: 87.7 us -> 85.2 us
  Pallas kernels: 24.3 us -> 22 us
  other arithmetic: 5.6 us -> 7.82 us
    cond x20 -> x0, local copies, waits for them, and re-layouts: 3.32 us -> none
    pallas_call x1, Pallas kernels: 6.49 us -> 3.77 us  [between(): pl.pallas_call(scatter_kernel, out_shape=[blocks(ENTRIES)] * 2, in_specs=...]
    ppermute x8, starting transfers between devices: 28.6 us -> 26.4 us  [shift(): lax.ppermute(array, axis, [(i, (i + by) % size) for i in range(size)])]
    another operation x9 -> x7, local copies, waits for them, and re-layouts: 1.04 us -> 3.24 us
    convert_element_type x2, other arithmetic: 2.48 us -> 4.65 us  [the longest x1 3.12 us: between(): (own_sum.astype(jnp.float32) + from_core.astype(jnp.float32)).astype(jnp....]
  transfers between devices with their start and end apart: 12 -> 12, of which waited for: 10 -> 9; matrix products, arithmetic and copies ran while one was open for 2% -> 4% of each run, Pallas kernels for 2% -> 3%
where the time goes in v5:
time: 197 us; the launch traced here: 195 us
  waiting for transfers between devices  85.2 us (43%)
  starting transfers between devices  65.2 us (33%)
  Pallas kernels  22 us (11%)
  local copies, waits for them, and re-layouts  12.1 us (6%)
  other arithmetic  7.82 us (4%)
  between operations  2.79 us (1%)
    all_to_all x4, waiting for transfers between devices, exchange(): return lax.all_to_all(array, axis, split_axis=0, concat_axis=0, tiled=True)  47.8 us
    all_to_all x4, starting transfers between devices, exchange(): return lax.all_to_all(array, axis, split_axis=0, concat_axis=0, tiled=True)  38.8 us
    ppermute x8, waiting for transfers between devices, shift(): lax.ppermute(array, axis, [(i, (i + by) % size) for i in range(size)])  37.4 us
    ppermute x8, starting transfers between devices, shift(): lax.ppermute(array, axis, [(i, (i + by) % size) for i in range(size)])  26.4 us
    pallas_call x1, Pallas kernels, attend(): pl.pallas_call(attend_kernel, out_shape=[outs, blocks(ENTRIES)] + [blocks...  12.1 us
  transfers between devices with their start and end apart: 12, of which 9 were waited for; matrix products, arithmetic and copies ran while one was open for 4% of the time, Pallas kernels for 3%

profile of v5, /device:TPU:1, one launch (start us, length us, event | category | flops | bytes accessed | tf_op | source)
XLA Modules:
  0.0 195.3 jit_solution(14329240286494638260)
XLA Ops:
  1.6 1.2 broadcast_in_dim.30
  2.8 17.1 %all-to-all-start.8 = ((bf16[64,2,32,128]{3,2,1,0:T(8,128)(2,1)}), bf16[64,2,32,128]{3,2,1,0:T(8,128)(2,1)S(1)}, u32[]{:S(2)}, u32[]{:S(2)}) async-start(bf16[64,2,32,128]{3,2,1,0:T(8,128)(2,1)} %bitcast.23), calls=%async_computation.8 | async-start | bytes 2097152 | tf_op jit(solution)/shard_map/all_to_all | solution.py:304
  23.9 23.5 %all-to-all-done.8 = bf16[64,2,32,128]{3,2,1,0:T(8,128)(2,1)S(1)} async-done(((bf16[64,2,32,128]{3,2,1,0:T(8,128)(2,1)}), bf16[64,2,32,128]{3,2,1,0:T(8,128)(2,1)S(1)}, u32[]{:S(2)}, u32[]{:S(2)}) %all-to-all-start.8) | async-done | bytes 1048608 | tf_op jit(solution)/shard_map/all_to_all | solution.py:304
  47.4 106.4 %conditional.4 = (bf16[8,2,8,32,128]{4,3,2,1,0:T(8,128)(2,1)}, bf16[16,256,128]{2,1,0:T(8,128)(2,1)}, bf16[16,256,128]{2,1,0:T(8,128)(2,1)}, f32[16,256,128]{2,1,0:T(8,128)}) conditional(s32[]{:T(128)} %clamp.3, (s32[1024]{0:T(1024)S(1)}, pred[1024]{0:T(1024)(128)(4,1)S(1)}, s32[1024]{0:T(1024)S(1)}, ...), branch_computations={%region_3.4_spmd, %region_4.5_spmd, %region_5.6_spmd, %region_6.7_... | conditional | flops 2687532032 | bytes 75693784
  47.5 1.4 copy.87
  49.2 1.1 maximum_bitcast_fusion
  50.3 5.4 %all-to-all-start = ((bf16[8,2,8,32,128]{4,3,2,1,0:T(8,128)(2,1)}), bf16[8,2,8,32,128]{4,3,2,1,0:T(8,128)(2,1)}, u32[]{:S(2)}, u32[]{:S(2)}) async-start(bf16[8,2,8,32,128]{4,3,2,1,0:T(8,128)(2,1)} %maximum_bitcast_fusion), calls=%async_computation | async-start | bytes 2097152 | tf_op jit(solution)/shard_map/cond/branch_0_fun/all_to_all | solution.py:304
  55.7 4.6 %collective-permute-start = (bf16[16,256,128]{2,1,0:T(8,128)(2,1)S(1)}, bf16[16,256,128]{2,1,0:T(8,128)(2,1)S(1)}, u32[]{:S(2)}, u32[]{:S(2)}) collective-permute-start(bf16[16,256,128]{2,1,0:T(8,128)(2,1)S(1)} %bitcast.46), channel_id=1, source_target_pairs={{0,8},{8,0},{1,9},{9,1},{2,10},{10,2},{3,11},{11,3},{4,12},{12,4},... | collective-permute-start | bytes 3145736 | tf_op jit(solution)/shard_map/cond/branch_0_fun/ppermute | solution.py:296
  60.5 2.1 %collective-permute-done.oth = bf16[16,256,128]{2,1,0:T(8,128)(2,1)S(1)} collective-permute-done((bf16[16,256,128]{2,1,0:T(8,128)(2,1)S(1)}, bf16[16,256,128]{2,1,0:T(8,128)(2,1)S(1)}, u32[]{:S(2)}, u32[]{:S(2)}) %collective-permute-start) | collective-permute-done | bytes 1048608 | tf_op jit(solution)/shard_map/cond/branch_0_fun/ppermute | solution.py:296
  62.5 3.8 %branch_0_fun.4 = (bf16[7,256,128]{2,1,0:T(8,128)(2,1)S(1)}, bf16[7,256,128]{2,1,0:T(8,128)(2,1)S(1)}, bf16[7,256,128]{2,1,0:T(8,128)(2,1)S(1)}) custom-call(s32[3]{0:T(128)S(1)} %get-tuple-element.362.place, s32[1024]{0:T(1024)S(1)} %fusion.3.code, bf16[16,256,128]{2,1,0:T(8,128)(2,1)S(1)} %bitcast.47, bf16[16,256,128]{2,1,0:T(8,128)(2,1)S(1)} %collective-permute-done.oth), custom_call_target="tpu_custom_call" | custom-call | tf_op jit(solution)/shard_map/cond/branch_0_fun/pallas_call | solution.py:356
  66.3 2.4 %collective-permute-start.1 = (bf16[7,256,128]{2,1,0:T(8,128)(2,1)S(1)}, bf16[7,256,128]{2,1,0:T(8,128)(2,1)}, u32[]{:S(2)}, u32[]{:S(2)}) collective-permute-start(bf16[7,256,128]{2,1,0:T(8,128)(2,1)S(1)} %get-tuple-element.359), channel_id=1, source_target_pairs={{0,16},{16,32},{32,48},{48,0},{1,17},{17,33},{33,49},{49,1},{2,18}... | collective-permute-start | bytes 1376264 | tf_op jit(solution)/shard_map/cond/branch_0_fun/ppermute | solution.py:296
  68.8 5.3 %collective-permute-start.2 = (bf16[7,256,128]{2,1,0:T(8,128)(2,1)S(1)}, bf16[7,256,128]{2,1,0:T(8,128)(2,1)}, u32[]{:S(2)}, u32[]{:S(2)}) collective-permute-start(bf16[7,256,128]{2,1,0:T(8,128)(2,1)S(1)} %get-tuple-element.360), channel_id=1, source_target_pairs={{0,32},{16,48},{32,0},{48,16},{1,33},{17,49},{33,1},{49,17},{2,34}... | collective-permute-start | bytes 1376264 | tf_op jit(solution)/shard_map/cond/branch_0_fun/ppermute | solution.py:296
  74.1 2.0 %collective-permute-start.3 = (bf16[7,256,128]{2,1,0:T(8,128)(2,1)S(1)}, bf16[7,256,128]{2,1,0:T(8,128)(2,1)}, u32[]{:S(2)}, u32[]{:S(2)}) collective-permute-start(bf16[7,256,128]{2,1,0:T(8,128)(2,1)S(1)} %get-tuple-element.361), channel_id=1, source_target_pairs={{0,48},{16,0},{32,16},{48,32},{1,49},{17,1},{33,17},{49,33},{2,50}... | collective-permute-start | bytes 1376264 | tf_op jit(solution)/shard_map/cond/branch_0_fun/ppermute | solution.py:296
  76.1 1.4 copy.88
  78.5 2.3 %branch_0_fun.5.mask_in = f32[16,128,128]{2,1,0:T(8,128)S(1)} custom-call(s32[3]{0:T(128)} %copy-done.34, s32[1024]{0:T(1024)S(1)} %copy-done.27, s32[1024]{0:T(1024)S(1)} %reshape.181.kind, f32[128,128]{1,0:T(8,128)S(1)} %bitcast.67), custom_call_target="tpu_custom_call" | custom-call | flops 2097152 | bytes 1048576 | tf_op jit(solution)/shard_map/cond/branch_0_fun/pallas_call | solution.py:308
  81.8 11.3 %collective-permute-done.2.r2 = bf16[7,256,128]{2,1,0:T(8,128)(2,1)} collective-permute-done((bf16[7,256,128]{2,1,0:T(8,128)(2,1)S(1)}, bf16[7,256,128]{2,1,0:T(8,128)(2,1)}, u32[]{:S(2)}, u32[]{:S(2)}) %collective-permute-start.2) | collective-permute-done | bytes 458784 | tf_op jit(solution)/shard_map/cond/branch_0_fun/ppermute | solution.py:296
  93.4 12.1 %branch_0_fun.6 = (bf16[8,2,8,32,128]{4,3,2,1,0:T(8,128)(2,1)}, bf16[16,256,128]{2,1,0:T(8,128)(2,1)}, bf16[7,256,128]{2,1,0:T(8,128)(2,1)}, bf16[7,256,128]{2,1,0:T(8,128)(2,1)}, bf16[7,256,128]{2,1,0:T(8,128)(2,1)}) custom-call(s32[3]{0:T(128)} %copy-done.34, s32[1024]{0:T(1024)} %copy-done.14, bf16[8,2,8,32,128]{4,3,2,1,0:T(8,128)(2,1)} %all-to-all-done.qd_in, ...), custom_call_target="tpu_custom_call" | custom-call | flops 2684354560 | bytes 8388608 | tf_op jit(solution)/shard_map/cond/branch_0_fun/pallas_call | solution.py:320
  105.6 7.1 %all-to-all-start.1 = ((bf16[8,2,8,32,128]{4,3,2,1,0:T(8,128)(2,1)}), bf16[8,2,8,32,128]{4,3,2,1,0:T(8,128)(2,1)}, u32[]{:S(2)}, u32[]{:S(2)}) async-start(bf16[8,2,8,32,128]{4,3,2,1,0:T(8,128)(2,1)} %get-tuple-element.369), calls=%async_computation.1 | async-start | bytes 2097152 | tf_op jit(solution)/shard_map/cond/branch_0_fun/all_to_all | solution.py:304
  112.6 5.3 %collective-permute-start.4 = (bf16[7,256,128]{2,1,0:T(8,128)(2,1)}, bf16[7,256,128]{2,1,0:T(8,128)(2,1)S(1)}, u32[]{:S(2)}, u32[]{:S(2)}) collective-permute-start(bf16[7,256,128]{2,1,0:T(8,128)(2,1)} %get-tuple-element.366), channel_id=1, source_target_pairs={{0,48},{16,0},{32,16},{48,32},{1,49},{17,1},{33,17},{49,33},{2,50}... | collective-permute-start | bytes 1376264 | tf_op jit(solution)/shard_map/cond/branch_0_fun/ppermute | solution.py:296
  118.0 2.5 %collective-permute-start.5 = (bf16[7,256,128]{2,1,0:T(8,128)(2,1)S(1)}, bf16[7,256,128]{2,1,0:T(8,128)(2,1)S(1)}, u32[]{:S(2)}, u32[]{:S(2)}) collective-permute-start(bf16[7,256,128]{2,1,0:T(8,128)(2,1)S(1)} %copy-done.45), channel_id=1, source_target_pairs={{0,32},{16,48},{32,0},{48,16},{1,33},{17,49},{33,1},{49,17},{2,34}... | collective-permute-start | bytes 1376264 | tf_op jit(solution)/shard_map/cond/branch_0_fun/ppermute | solution.py:296
  120.5 1.9 collective-permute-start.6
  122.4 6.2 %collective-permute-done.4.g1 = bf16[7,256,128]{2,1,0:T(8,128)(2,1)S(1)} collective-permute-done((bf16[7,256,128]{2,1,0:T(8,128)(2,1)}, bf16[7,256,128]{2,1,0:T(8,128)(2,1)S(1)}, u32[]{:S(2)}, u32[]{:S(2)}) %collective-permute-start.4) | collective-permute-done | bytes 458784 | tf_op jit(solution)/shard_map/cond/branch_0_fun/ppermute | solution.py:296
  128.6 3.9 %collective-permute-done.5.g2 = bf16[7,256,128]{2,1,0:T(8,128)(2,1)S(1)} collective-permute-done((bf16[7,256,128]{2,1,0:T(8,128)(2,1)S(1)}, bf16[7,256,128]{2,1,0:T(8,128)(2,1)S(1)}, u32[]{:S(2)}, u32[]{:S(2)}) %collective-permute-start.5) | collective-permute-done | bytes 458784 | tf_op jit(solution)/shard_map/cond/branch_0_fun/ppermute | solution.py:296
  132.5 11.2 %collective-permute-done.6.g3 = bf16[7,256,128]{2,1,0:T(8,128)(2,1)S(1)} collective-permute-done((bf16[7,256,128]{2,1,0:T(8,128)(2,1)S(1)}, bf16[7,256,128]{2,1,0:T(8,128)(2,1)S(1)}, u32[]{:S(2)}, u32[]{:S(2)}) %collective-permute-start.6) | collective-permute-done | bytes 458784 | tf_op jit(solution)/shard_map/cond/branch_0_fun/ppermute | solution.py:296
  143.7 3.8 %branch_0_fun.7 = (bf16[16,256,128]{2,1,0:T(8,128)(2,1)}, bf16[16,256,128]{2,1,0:T(8,128)(2,1)}) custom-call(s32[3]{0:T(128)S(1)} %copy-done.35, s32[1024]{0:T(1024)S(1)} %copy-done.15, bf16[16,256,128]{2,1,0:T(8,128)(2,1)S(1)} %copy-done.11, bf16[7,256,128]{2,1,0:T(8,128)(2,1)S(1)} %collective-permute-done.4.g1, ...), custom_call_target="tpu_custom_call" | custom-call | tf_op jit(solution)/shard_map/cond/branch_0_fun/pallas_call | solution.py:378
  147.5 2.4 %collective-permute-start.7 = (bf16[16,256,128]{2,1,0:T(8,128)(2,1)}, bf16[16,256,128]{2,1,0:T(8,128)(2,1)S(1)}, u32[]{:S(2)}, u32[]{:S(2)}) collective-permute-start(bf16[16,256,128]{2,1,0:T(8,128)(2,1)} %get-tuple-element.1007), channel_id=1, source_target_pairs={{0,8},{8,0},{1,9},{9,1},{2,10},{10,2},{3,11},{11,3},{4,12},{12,4},... | collective-permute-start | bytes 3145736 | tf_op jit(solution)/shard_map/cond/branch_0_fun/ppermute | solution.py:296
  149.8 2.5 %collective-permute-done.7 = bf16[16,256,128]{2,1,0:T(8,128)(2,1)S(1)} collective-permute-done((bf16[16,256,128]{2,1,0:T(8,128)(2,1)}, bf16[16,256,128]{2,1,0:T(8,128)(2,1)S(1)}, u32[]{:S(2)}, u32[]{:S(2)}) %collective-permute-start.7) | collective-permute-done | bytes 1048608 | tf_op jit(solution)/shard_map/cond/branch_0_fun/ppermute | solution.py:296
  152.3 1.5 convert_element_type.61
  153.8 3.1 %add_convert_fusion = bf16[16,256,128]{2,1,0:T(8,128)(2,1)} fusion(f32[16,256,128]{2,1,0:T(8,128)} %get-tuple-element.910, bf16[16,256,128]{2,1,0:T(8,128)(2,1)} %get-tuple-element.511), kind=kLoop, calls=%fused_computation.76 | loop fusion | flops 1572864 | bytes 4194304 | tf_op jit(solution)/shard_map/cond/branch_0_fun/convert_element_type | solution.py:387
  157.0 9.2 %all-to-all-start.9 = ((bf16[64,2,32,128]{3,2,1,0:T(8,128)(2,1)}), bf16[64,2,32,128]{3,2,1,0:T(8,128)(2,1)S(1)}, u32[]{:S(2)}, u32[]{:S(2)}) async-start(bf16[64,2,32,128]{3,2,1,0:T(8,128)(2,1)} %bitcast.30), calls=%async_computation.9 | async-start | bytes 2097152 | tf_op jit(solution)/shard_map/all_to_all | solution.py:304
  166.2 1.3 fusion.58
  169.5 24.3 %all-to-all-done.9 = bf16[64,2,32,128]{3,2,1,0:T(8,128)(2,1)S(1)} async-done(((bf16[64,2,32,128]{3,2,1,0:T(8,128)(2,1)}), bf16[64,2,32,128]{3,2,1,0:T(8,128)(2,1)S(1)}, u32[]{:S(2)}, u32[]{:S(2)}) %all-to-all-start.9) | async-done | bytes 1048608 | tf_op jit(solution)/shard_map/all_to_all | solution.py:304
  (75 shorter events, 9.2 us)
Async XLA Ops:
  0.6 19.3 %copy-start.40 = (s32[128,8]{0,1:T(8,128)S(1)}, s32[128,8]{0,1:T(8,128)}, u32[]{:S(2)}) copy-start(s32[128,8]{0,1:T(8,128)} %param.15) | copy-start | bytes 12292
  1.6 22.2 %copy-start.39 = (s32[16384]{0:T(1024)S(1)}, s32[16384]{0:T(1024)}, u32[]{:S(2)}) copy-start(s32[16384]{0:T(1024)} %param.17) | copy-start | bytes 196612
  1.6 45.9 %copy-start.24 = (bf16[32,64,128]{2,1,0:T(8,128)(2,1)S(1)}, bf16[32,64,128]{2,1,0:T(8,128)(2,1)}, u32[]{:S(2)}) copy-start(bf16[32,64,128]{2,1,0:T(8,128)(2,1)} %param.11) | copy-start | bytes 1572868
  2.8 44.6 %all-to-all-start.8 = ((bf16[64,2,32,128]{3,2,1,0:T(8,128)(2,1)}), bf16[64,2,32,128]{3,2,1,0:T(8,128)(2,1)S(1)}, u32[]{:S(2)}, u32[]{:S(2)}) async-start(bf16[64,2,32,128]{3,2,1,0:T(8,128)(2,1)} %bitcast.23), calls=%async_computation.8 | async-start | bytes 2097152 | tf_op jit(solution)/shard_map/all_to_all | solution.py:304
  47.5 8.2 %copy-start.26 = (s32[1024]{0:T(1024)}, s32[1024]{0:T(1024)S(1)}, u32[]{:S(2)}) copy-start(s32[1024]{0:T(1024)S(1)} %get-tuple-element.363.ent) | copy-start | bytes 12292
  47.5 15.0 %copy-start.34 = (s32[3]{0:T(128)}, s32[3]{0:T(128)S(1)}, u32[]{:S(2)}) copy-start(s32[3]{0:T(128)S(1)} %get-tuple-element.362.place) | copy-start | bytes 40
  50.3 43.1 %all-to-all-start = ((bf16[8,2,8,32,128]{4,3,2,1,0:T(8,128)(2,1)}), bf16[8,2,8,32,128]{4,3,2,1,0:T(8,128)(2,1)}, u32[]{:S(2)}, u32[]{:S(2)}) async-start(bf16[8,2,8,32,128]{4,3,2,1,0:T(8,128)(2,1)} %maximum_bitcast_fusion), calls=%async_computation | async-start | bytes 2097152 | tf_op jit(solution)/shard_map/cond/branch_0_fun/all_to_all | solution.py:304
  55.7 6.8 %collective-permute-start = (bf16[16,256,128]{2,1,0:T(8,128)(2,1)S(1)}, bf16[16,256,128]{2,1,0:T(8,128)(2,1)S(1)}, u32[]{:S(2)}, u32[]{:S(2)}) collective-permute-start(bf16[16,256,128]{2,1,0:T(8,128)(2,1)S(1)} %bitcast.46), channel_id=1, source_target_pairs={{0,8},{8,0},{1,9},{9,1},{2,10},{10,2},{3,11},{11,3},{4,12},{12,4},... | collective-permute-start | bytes 3145736 | tf_op jit(solution)/shard_map/cond/branch_0_fun/ppermute | solution.py:296
  60.4 33.0 %copy-start.14 = (s32[1024]{0:T(1024)}, s32[1024]{0:T(1024)S(1)}, u32[]{:S(2)}) copy-start(s32[1024]{0:T(1024)S(1)} %fusion.3.code) | copy-start | bytes 12292
  60.4 18.0 %copy-start.27 = (s32[1024]{0:T(1024)S(1)}, s32[1024]{0:T(1024)}, u32[]{:S(2)}) copy-start(s32[1024]{0:T(1024)} %copy-done.26) | copy-start | bytes 12292
  62.5 30.9 %copy-start.2 = (bf16[16,256,128]{2,1,0:T(8,128)(2,1)}, bf16[16,256,128]{2,1,0:T(8,128)(2,1)S(1)}, u32[]{:S(2)}) copy-start(bf16[16,256,128]{2,1,0:T(8,128)(2,1)S(1)} %collective-permute-done.oth) | copy-start | bytes 3145732
  66.3 15.5 %collective-permute-start.1 = (bf16[7,256,128]{2,1,0:T(8,128)(2,1)S(1)}, bf16[7,256,128]{2,1,0:T(8,128)(2,1)}, u32[]{:S(2)}, u32[]{:S(2)}) collective-permute-start(bf16[7,256,128]{2,1,0:T(8,128)(2,1)S(1)} %get-tuple-element.359), channel_id=1, source_target_pairs={{0,16},{16,32},{32,48},{48,0},{1,17},{17,33},{33,49},{49,1},{2,18}... | collective-permute-start | bytes 1376264 | tf_op jit(solution)/shard_map/cond/branch_0_fun/ppermute | solution.py:296
  68.8 24.3 %collective-permute-start.2 = (bf16[7,256,128]{2,1,0:T(8,128)(2,1)S(1)}, bf16[7,256,128]{2,1,0:T(8,128)(2,1)}, u32[]{:S(2)}, u32[]{:S(2)}) collective-permute-start(bf16[7,256,128]{2,1,0:T(8,128)(2,1)S(1)} %get-tuple-element.360), channel_id=1, source_target_pairs={{0,32},{16,48},{32,0},{48,16},{1,33},{17,49},{33,1},{49,17},{2,34}... | collective-permute-start | bytes 1376264 | tf_op jit(solution)/shard_map/cond/branch_0_fun/ppermute | solution.py:296
  74.1 19.3 %collective-permute-start.3 = (bf16[7,256,128]{2,1,0:T(8,128)(2,1)S(1)}, bf16[7,256,128]{2,1,0:T(8,128)(2,1)}, u32[]{:S(2)}, u32[]{:S(2)}) collective-permute-start(bf16[7,256,128]{2,1,0:T(8,128)(2,1)S(1)} %get-tuple-element.361), channel_id=1, source_target_pairs={{0,48},{16,0},{32,16},{48,32},{1,49},{17,1},{33,17},{49,33},{2,50}... | collective-permute-start | bytes 1376264 | tf_op jit(solution)/shard_map/cond/branch_0_fun/ppermute | solution.py:296
  80.8 1.0 copy-start.7
  105.5 12.4 %copy-start.45 = (bf16[7,256,128]{2,1,0:T(8,128)(2,1)S(1)}, bf16[7,256,128]{2,1,0:T(8,128)(2,1)}, u32[]{:S(2)}) copy-start(bf16[7,256,128]{2,1,0:T(8,128)(2,1)} %get-tuple-element.367) | copy-start | bytes 1376260
  105.5 15.0 %copy-start.44 = (bf16[7,256,128]{2,1,0:T(8,128)(2,1)S(1)}, bf16[7,256,128]{2,1,0:T(8,128)(2,1)}, u32[]{:S(2)}) copy-start(bf16[7,256,128]{2,1,0:T(8,128)(2,1)} %get-tuple-element.368) | copy-start | bytes 1376260
  105.6 38.1 %copy-start.11 = (bf16[16,256,128]{2,1,0:T(8,128)(2,1)S(1)}, bf16[16,256,128]{2,1,0:T(8,128)(2,1)}, u32[]{:S(2)}) copy-start(bf16[16,256,128]{2,1,0:T(8,128)(2,1)} %get-tuple-element.371.g0) | copy-start | bytes 3145732
  105.6 38.1 %copy-start.15 = (s32[1024]{0:T(1024)S(1)}, s32[1024]{0:T(1024)}, u32[]{:S(2)}) copy-start(s32[1024]{0:T(1024)} %copy-done.14) | copy-start | bytes 12292
  105.6 38.1 %copy-start.35 = (s32[3]{0:T(128)S(1)}, s32[3]{0:T(128)}, u32[]{:S(2)}) copy-start(s32[3]{0:T(128)} %copy-done.34) | copy-start | bytes 40
  105.6 38.1 %all-to-all-start.1 = ((bf16[8,2,8,32,128]{4,3,2,1,0:T(8,128)(2,1)}), bf16[8,2,8,32,128]{4,3,2,1,0:T(8,128)(2,1)}, u32[]{:S(2)}, u32[]{:S(2)}) async-start(bf16[8,2,8,32,128]{4,3,2,1,0:T(8,128)(2,1)} %get-tuple-element.369), calls=%async_computation.1 | async-start | bytes 2097152 | tf_op jit(solution)/shard_map/cond/branch_0_fun/all_to_all | solution.py:304
  112.6 16.0 %collective-permute-start.4 = (bf16[7,256,128]{2,1,0:T(8,128)(2,1)}, bf16[7,256,128]{2,1,0:T(8,128)(2,1)S(1)}, u32[]{:S(2)}, u32[]{:S(2)}) collective-permute-start(bf16[7,256,128]{2,1,0:T(8,128)(2,1)} %get-tuple-element.366), channel_id=1, source_target_pairs={{0,48},{16,0},{32,16},{48,32},{1,49},{17,1},{33,17},{49,33},{2,50}... | collective-permute-start | bytes 1376264 | tf_op jit(solution)/shard_map/cond/branch_0_fun/ppermute | solution.py:296
  118.0 14.5 %collective-permute-start.5 = (bf16[7,256,128]{2,1,0:T(8,128)(2,1)S(1)}, bf16[7,256,128]{2,1,0:T(8,128)(2,1)S(1)}, u32[]{:S(2)}, u32[]{:S(2)}) collective-permute-start(bf16[7,256,128]{2,1,0:T(8,128)(2,1)S(1)} %copy-done.45), channel_id=1, source_target_pairs={{0,32},{16,48},{32,0},{48,16},{1,33},{17,49},{33,1},{49,17},{2,34}... | collective-permute-start | bytes 1376264 | tf_op jit(solution)/shard_map/cond/branch_0_fun/ppermute | solution.py:296
  120.5 23.1 %collective-permute-start.6 = (bf16[7,256,128]{2,1,0:T(8,128)(2,1)S(1)}, bf16[7,256,128]{2,1,0:T(8,128)(2,1)S(1)}, u32[]{:S(2)}, u32[]{:S(2)}) collective-permute-start(bf16[7,256,128]{2,1,0:T(8,128)(2,1)S(1)} %copy-done.44), channel_id=1, source_target_pairs={{0,16},{16,32},{32,48},{48,0},{1,17},{17,33},{33,49},{49,1},{2,18}... | collective-permute-start | bytes 1376264 | tf_op jit(solution)/shard_map/cond/branch_0_fun/ppermute | solution.py:296
  147.5 4.8 %collective-permute-start.7 = (bf16[16,256,128]{2,1,0:T(8,128)(2,1)}, bf16[16,256,128]{2,1,0:T(8,128)(2,1)S(1)}, u32[]{:S(2)}, u32[]{:S(2)}) collective-permute-start(bf16[16,256,128]{2,1,0:T(8,128)(2,1)} %get-tuple-element.1007), channel_id=1, source_target_pairs={{0,8},{8,0},{1,9},{9,1},{2,10},{10,2},{3,11},{11,3},{4,12},{12,4},... | collective-permute-start | bytes 3145736 | tf_op jit(solution)/shard_map/cond/branch_0_fun/ppermute | solution.py:296
  157.0 36.9 %all-to-all-start.9 = ((bf16[64,2,32,128]{3,2,1,0:T(8,128)(2,1)}), bf16[64,2,32,128]{3,2,1,0:T(8,128)(2,1)S(1)}, u32[]{:S(2)}, u32[]{:S(2)}) async-start(bf16[64,2,32,128]{3,2,1,0:T(8,128)(2,1)} %bitcast.30), calls=%async_computation.9 | async-start | bytes 2097152 | tf_op jit(solution)/shard_map/all_to_all | solution.py:304

commit v6 on v5

--- a/solution.py
+++ b/solution.py
@@ -116,7 +116,7 @@
     @pl.loop(0, ENTRIES)
     def _(e):
         index = me * 2 + e // LISTED
-        block, t = ent[me * ENTRIES + e], kind[me * ENTRIES + e]
+        block, t = ent[e % LISTED, index], kind[e % LISTED, index]
         sess_q = sess[pl.ds(index, 1), :]
         sess_k = jnp.broadcast_to(sess[pl.ds(block, 1), :], (BLOCK, BLOCK)).T
         needs = jnp.where((t == 0) | (t == 2), 1.0, 0.0)
@@ -304,6 +304,42 @@
     return lax.all_to_all(array, axis, split_axis=0, concat_axis=0, tiled=True)
 
 
+def gather(slots, *operands):
+    return pl.pallas_call(
+        gather_kernel,
+        out_shape=[blocks(slots)] * 3,
+        in_specs=[SMEM] * 2 + [HBM] * 2,
+        out_specs=[HBM] * 3,
+        scratch_shapes=[DMA((X, ENTRIES))],
+        compiler_params=params(4),
+    )(*operands)
+
+
+def scatter(*operands):
+    return pl.pallas_call(
+        scatter_kernel,
+        out_shape=[blocks(ENTRIES)] * 2,
+        in_specs=[SMEM] * 2 + [VMEM] * 4,
+        out_specs=[VMEM] * 2,
+        scratch_shapes=[pltpu.VMEM((2 * ENTRIES, 2 * BLOCK, WIDTH), jnp.float32)],
+        compiler_params=params(14),
+    )(*operands)
+
+
+def add_kernel(left, right, total):
+    total[...] = (left[...].astype(jnp.float32) + right[...].astype(jnp.float32)).astype(jnp.bfloat16)
+
+
+def add(*operands):
+    return pl.pallas_call(
+        add_kernel,
+        out_shape=blocks(ENTRIES),
+        in_specs=[VMEM] * 2,
+        out_specs=VMEM,
+        compiler_params=params(8),
+    )(*operands)
+
+
 def masks(*operands):
     return pl.pallas_call(
         mask_kernel,
@@ -353,14 +389,7 @@
 def between(slots, place, tables, own, queries, output_gradient, sess):
     code, ent, kind = tables
     other = shift(own, "core", 1)
-    sends = pl.pallas_call(
-        gather_kernel,
-        out_shape=[blocks(slots)] * 3,
-        in_specs=[SMEM] * 2 + [HBM] * 2,
-        out_specs=[HBM] * 3,
-        scratch_shapes=[DMA((X, ENTRIES))],
-        compiler_params=params(4),
-    )(place, code, own, other)
+    sends = gather(slots, place, code, own, other)
     now, *sends = lax.optimization_barrier((place, *sends))
     fetched = [shift(sends[k - 1], "x", k) for k in (1, 2, 3)]
     mask = masks(now, ent, kind, sess)
@@ -375,16 +404,9 @@
     returned = [shift(g, "x", -k) for k, g in ((1, g1), (2, g2), (3, g3))]
     out = exchange(out, "head")
     *returned, out = lax.optimization_barrier((*returned, out))
-    own_sum, other_sum = pl.pallas_call(
-        scatter_kernel,
-        out_shape=[blocks(ENTRIES)] * 2,
-        in_specs=[SMEM] * 2 + [VMEM] * 4,
-        out_specs=[VMEM] * 2,
-        scratch_shapes=[pltpu.VMEM((2 * ENTRIES, 2 * BLOCK, WIDTH), jnp.float32)],
-        compiler_params=params(14),
-    )(place, code, g0, *returned)
+    own_sum, other_sum = scatter(place, code, g0, *returned)
     from_core = shift(other_sum, "core", 1)
-    column_sum = (own_sum.astype(jnp.float32) + from_core.astype(jnp.float32)).astype(jnp.bfloat16)
+    column_sum = add(own_sum, from_core)
     return out, column_sum
 
 
@@ -393,7 +415,6 @@
     place = jnp.stack(where).astype(jnp.int32)
 
     code, most = coded(kv_list)
-    tables = (code, kv_list.reshape(-1), kv_type.reshape(-1))
     sess = session_id.astype(jnp.float32).reshape(-1, BLOCK)
 
     kv = jnp.stack([keys, values]).transpose(2, 0, 1, 3)
@@ -401,6 +422,8 @@
     own = exchange(kv.reshape(Z * HEAD, 2, QUARTER, WIDTH), ("z", "head"))
     own = own.reshape(ENTRIES, 2 * BLOCK, WIDTH)
 
+    own, code, most, sess = lax.optimization_barrier((own, code, most, sess))
+    tables = (code, kv_list.T, kv_type.T)
     out, column_sum = lax.switch(
         sum((most > few).astype(jnp.int32) for few in SLOTS[:-1]),
         [functools.partial(between, slots) for slots in SLOTS],

time: 197 us -> 194 us (0.985)
  other arithmetic: 7.82 us -> 3.12 us
  waiting for transfers between devices: 85.2 us -> 88.9 us
    convert_element_type x3 -> x0, other arithmetic: 4.66 us -> none  [the longest x1 3.12 us: between(): (own_sum.astype(jnp.float32) + from_core.astype(jnp.float32)).astype(jnp....]
    cond x0 -> x16, local copies, waits for them, and re-layouts: none -> 2.77 us
    all_to_all x4, waiting for transfers between devices: 47.8 us -> 50.4 us  [exchange(): return lax.all_to_all(array, axis, split_axis=0, concat_axis=0, tiled=True)]
    another operation x7 -> x2, local copies, waits for them, and re-layouts: 3.24 us -> 0.69 us
    slice x3 -> x1, local copies, waits for them, and re-layouts: 3.3 us -> 1.3 us  [per_device(): return (out[0], out[1], total[0], total[1])]
    pallas_call x2 -> x3, Pallas kernels: 7.58 us -> 7.6 us  [the longest x1 3.91 us: gather(): pl.pallas_call(gather_kernel, out_shape=[blocks(slots)] * 3, in_specs=[SM...]
  transfers between devices with their start and end apart: 12 -> 12, of which waited for: 9 -> 10; matrix products, arithmetic and copies ran while one was open for 4% -> 2% of each run, Pallas kernels for 3% -> 3%
where the time goes in v6:
time: 194 us; the launch traced here: 192 us
  waiting for transfers between devices  88.9 us (46%)
  starting transfers between devices  64.9 us (33%)
  Pallas kernels  22.1 us (11%)
  local copies, waits for them, and re-layouts  10.3 us (5%)
  other arithmetic  3.12 us (2%)
  between operations  2.72 us (1%)
    all_to_all x4, waiting for transfers between devices, exchange(): return lax.all_to_all(array, axis, split_axis=0, concat_axis=0, tiled=True)  50.4 us
    ppermute x8, waiting for transfers between devices, shift(): lax.ppermute(array, axis, [(i, (i + by) % size) for i in range(size)])  38.5 us
    all_to_all x4, starting transfers between devices, exchange(): return lax.all_to_all(array, axis, split_axis=0, concat_axis=0, tiled=True)  38.3 us
    ppermute x8, starting transfers between devices, shift(): lax.ppermute(array, axis, [(i, (i + by) % size) for i in range(size)])  26.6 us
    pallas_call x1, Pallas kernels, attend(): pl.pallas_call(attend_kernel, out_shape=[outs, blocks(ENTRIES)] + [blocks...  12 us
    pallas_call x1, Pallas kernels, gather(): pl.pallas_call(gather_kernel, out_shape=[blocks(slots)] * 3, in_specs=[SM...  3.91 us
  transfers between devices with their start and end apart: 12, of which 10 were waited for; matrix products, arithmetic and copies ran while one was open for 2% of the time, Pallas kernels for 3%

profile of v6, /device:TPU:1, one launch (start us, length us, event | category | flops | bytes accessed | tf_op | source)
XLA Modules:
  0.0 192.2 jit_solution(6573052603191987165)
XLA Ops:
  1.5 1.2 broadcast_in_dim.18
  2.8 17.3 %all-to-all-start.8 = ((bf16[64,2,32,128]{3,2,1,0:T(8,128)(2,1)}), bf16[64,2,32,128]{3,2,1,0:T(8,128)(2,1)S(1)}, u32[]{:S(2)}, u32[]{:S(2)}) async-start(bf16[64,2,32,128]{3,2,1,0:T(8,128)(2,1)} %bitcast.15), calls=%async_computation.8 | async-start | bytes 2097152 | tf_op jit(solution)/shard_map/all_to_all | solution.py:304
  22.1 25.4 %all-to-all-done.8 = bf16[64,2,32,128]{3,2,1,0:T(8,128)(2,1)S(1)} async-done(((bf16[64,2,32,128]{3,2,1,0:T(8,128)(2,1)}), bf16[64,2,32,128]{3,2,1,0:T(8,128)(2,1)S(1)}, u32[]{:S(2)}, u32[]{:S(2)}) %all-to-all-start.8) | async-done | bytes 1048608 | tf_op jit(solution)/shard_map/all_to_all | solution.py:304
  50.1 104.3 %conditional.1 = (bf16[8,2,8,32,128]{4,3,2,1,0:T(8,128)(2,1)}, bf16[16,256,128]{2,1,0:T(8,128)(2,1)}) conditional(s32[]{:T(128)} %clamp.3, (bf16[32,64,128]{2,1,0:T(8,128)(2,1)S(1)}, bf16[32,64,128]{2,1,0:T(8,128)(2,1)S(1)}, bf16[16,256,128]{2,1,0:T(8,128)(2,1)S(1)}, s32[3]{0:T(128)S(1)}, s32[1024]{0:T(1024)S(1)}, ...), branch_computations={%region_3.4_spmd, %region_4.5_spmd, %region_5.6_spmd, %region_6.7_... | conditional | flops 2686976000 | bytes 83362512 | solution.py:427
  50.8 1.1 maximum_bitcast_fusion
  51.9 5.4 %all-to-all-start = ((bf16[8,2,8,32,128]{4,3,2,1,0:T(8,128)(2,1)}), bf16[8,2,8,32,128]{4,3,2,1,0:T(8,128)(2,1)S(1)}, u32[]{:S(2)}, u32[]{:S(2)}) async-start(bf16[8,2,8,32,128]{4,3,2,1,0:T(8,128)(2,1)} %maximum_bitcast_fusion), calls=%async_computation | async-start | bytes 2097152 | tf_op jit(solution)/shard_map/cond/branch_0_fun/all_to_all | solution.py:304
  57.2 4.5 %collective-permute-start = (bf16[16,256,128]{2,1,0:T(8,128)(2,1)S(1)}, bf16[16,256,128]{2,1,0:T(8,128)(2,1)S(1)}, u32[]{:S(2)}, u32[]{:S(2)}) collective-permute-start(bf16[16,256,128]{2,1,0:T(8,128)(2,1)S(1)} %get-tuple-element.68.own), channel_id=1, source_target_pairs={{0,8},{8,0},{1,9},{9,1},{2,10},{10,2},{3,11},{11,3},{4,12},{12,4},... | collective-permute-start | bytes 3145736 | tf_op jit(solution)/shard_map/cond/branch_0_fun/ppermute | solution.py:296
  61.8 2.3 %collective-permute-done.oth = bf16[16,256,128]{2,1,0:T(8,128)(2,1)S(1)} collective-permute-done((bf16[16,256,128]{2,1,0:T(8,128)(2,1)S(1)}, bf16[16,256,128]{2,1,0:T(8,128)(2,1)S(1)}, u32[]{:S(2)}, u32[]{:S(2)}) %collective-permute-start) | collective-permute-done | bytes 1048608 | tf_op jit(solution)/shard_map/cond/branch_0_fun/ppermute | solution.py:296
  64.1 3.9 %branch_0_fun.5 = (bf16[7,256,128]{2,1,0:T(8,128)(2,1)S(1)}, bf16[7,256,128]{2,1,0:T(8,128)(2,1)S(1)}, bf16[7,256,128]{2,1,0:T(8,128)(2,1)S(1)}) custom-call(s32[3]{0:T(128)S(1)} %get-tuple-element.75.place, s32[1024]{0:T(1024)S(1)} %get-tuple-element.65.code, bf16[16,256,128]{2,1,0:T(8,128)(2,1)S(1)} %get-tuple-element.68.own, ...), custom_call_target="tpu_custom_call" | custom-call | tf_op jit(solution)/shard_map/cond/branch_0_fun/pallas_call | solution.py:308
  68.0 2.8 %collective-permute-start.1 = (bf16[7,256,128]{2,1,0:T(8,128)(2,1)S(1)}, bf16[7,256,128]{2,1,0:T(8,128)(2,1)S(1)}, u32[]{:S(2)}, u32[]{:S(2)}) collective-permute-start(bf16[7,256,128]{2,1,0:T(8,128)(2,1)S(1)} %get-tuple-element.72), channel_id=1, source_target_pairs={{0,16},{16,32},{32,48},{48,0},{1,17},{17,33},{33,49},{49,1},{2,18}... | collective-permute-start | bytes 1376264 | tf_op jit(solution)/shard_map/cond/branch_0_fun/ppermute | solution.py:296
  70.8 4.2 %collective-permute-start.2 = (bf16[7,256,128]{2,1,0:T(8,128)(2,1)S(1)}, bf16[7,256,128]{2,1,0:T(8,128)(2,1)S(1)}, u32[]{:S(2)}, u32[]{:S(2)}) collective-permute-start(bf16[7,256,128]{2,1,0:T(8,128)(2,1)S(1)} %get-tuple-element.73), channel_id=1, source_target_pairs={{0,32},{16,48},{32,0},{48,16},{1,33},{17,49},{33,1},{49,17},{2,34}... | collective-permute-start | bytes 1376264 | tf_op jit(solution)/shard_map/cond/branch_0_fun/ppermute | solution.py:296
  75.0 3.0 %collective-permute-start.3 = (bf16[7,256,128]{2,1,0:T(8,128)(2,1)S(1)}, bf16[7,256,128]{2,1,0:T(8,128)(2,1)}, u32[]{:S(2)}, u32[]{:S(2)}) collective-permute-start(bf16[7,256,128]{2,1,0:T(8,128)(2,1)S(1)} %get-tuple-element.74), channel_id=1, source_target_pairs={{0,48},{16,0},{32,16},{48,32},{1,49},{17,1},{33,17},{49,33},{2,50}... | collective-permute-start | bytes 1376264 | tf_op jit(solution)/shard_map/cond/branch_0_fun/ppermute | solution.py:296
  78.0 2.5 %branch_0_fun.6.mask_in = f32[16,128,128]{2,1,0:T(8,128)S(1)} custom-call(s32[3]{0:T(128)S(1)} %get-tuple-element.75.place, s32[8,128]{1,0:T(8,128)S(1)} %get-tuple-element.76.ent, s32[8,128]{1,0:T(8,128)S(1)} %get-tuple-element.77.kind, f32[128,128]{1,0:T(8,128)S(1)} %get-tuple-element.78.sess), custom_call_target="tpu_custom_call" | custom-call | flops 2097152 | bytes 1048576 | tf_op jit(solution)/shard_map/cond/branch_0_fun/pallas_call | solution.py:344
  81.4 1.8 collective-permute-done.1.r1
  83.2 9.7 %collective-permute-done.2.r2 = bf16[7,256,128]{2,1,0:T(8,128)(2,1)S(1)} collective-permute-done((bf16[7,256,128]{2,1,0:T(8,128)(2,1)S(1)}, bf16[7,256,128]{2,1,0:T(8,128)(2,1)S(1)}, u32[]{:S(2)}, u32[]{:S(2)}) %collective-permute-start.2) | collective-permute-done | bytes 458784 | tf_op jit(solution)/shard_map/cond/branch_0_fun/ppermute | solution.py:296
  93.7 1.6 collective-permute-done.3.r3
  96.3 12.0 %branch_0_fun.7 = (bf16[8,2,8,32,128]{4,3,2,1,0:T(8,128)(2,1)}, bf16[16,256,128]{2,1,0:T(8,128)(2,1)}, bf16[7,256,128]{2,1,0:T(8,128)(2,1)}, bf16[7,256,128]{2,1,0:T(8,128)(2,1)}, bf16[7,256,128]{2,1,0:T(8,128)(2,1)}) custom-call(s32[3]{0:T(128)S(1)} %get-tuple-element.75.place, s32[1024]{0:T(1024)S(1)} %get-tuple-element.65.code, ...), custom_call_target="tpu_custom_call" | custom-call | flops 2684354560 | bytes 8388608 | tf_op jit(solution)/shard_map/cond/branch_0_fun/pallas_call | solution.py:356
  108.4 7.1 %all-to-all-start.1 = ((bf16[8,2,8,32,128]{4,3,2,1,0:T(8,128)(2,1)}), bf16[8,2,8,32,128]{4,3,2,1,0:T(8,128)(2,1)}, u32[]{:S(2)}, u32[]{:S(2)}) async-start(bf16[8,2,8,32,128]{4,3,2,1,0:T(8,128)(2,1)} %get-tuple-element.82), calls=%async_computation.1 | async-start | bytes 2097152 | tf_op jit(solution)/shard_map/cond/branch_0_fun/all_to_all | solution.py:304
  115.5 4.9 %collective-permute-start.4 = (bf16[7,256,128]{2,1,0:T(8,128)(2,1)}, bf16[7,256,128]{2,1,0:T(8,128)(2,1)S(1)}, u32[]{:S(2)}, u32[]{:S(2)}) collective-permute-start(bf16[7,256,128]{2,1,0:T(8,128)(2,1)} %get-tuple-element.79), channel_id=1, source_target_pairs={{0,48},{16,0},{32,16},{48,32},{1,49},{17,1},{33,17},{49,33},{2,50}... | collective-permute-start | bytes 1376264 | tf_op jit(solution)/shard_map/cond/branch_0_fun/ppermute | solution.py:296
  120.4 2.9 %collective-permute-start.5 = (bf16[7,256,128]{2,1,0:T(8,128)(2,1)S(1)}, bf16[7,256,128]{2,1,0:T(8,128)(2,1)S(1)}, u32[]{:S(2)}, u32[]{:S(2)}) collective-permute-start(bf16[7,256,128]{2,1,0:T(8,128)(2,1)S(1)} %copy-done.36), channel_id=1, source_target_pairs={{0,32},{16,48},{32,0},{48,16},{1,33},{17,49},{33,1},{49,17},{2,34}... | collective-permute-start | bytes 1376264 | tf_op jit(solution)/shard_map/cond/branch_0_fun/ppermute | solution.py:296
  123.3 1.9 collective-permute-start.6
  125.2 4.8 %collective-permute-done.4.g1 = bf16[7,256,128]{2,1,0:T(8,128)(2,1)S(1)} collective-permute-done((bf16[7,256,128]{2,1,0:T(8,128)(2,1)}, bf16[7,256,128]{2,1,0:T(8,128)(2,1)S(1)}, u32[]{:S(2)}, u32[]{:S(2)}) %collective-permute-start.4) | collective-permute-done | bytes 458784 | tf_op jit(solution)/shard_map/cond/branch_0_fun/ppermute | solution.py:296
  130.1 4.7 %collective-permute-done.5.g2 = bf16[7,256,128]{2,1,0:T(8,128)(2,1)S(1)} collective-permute-done((bf16[7,256,128]{2,1,0:T(8,128)(2,1)S(1)}, bf16[7,256,128]{2,1,0:T(8,128)(2,1)S(1)}, u32[]{:S(2)}, u32[]{:S(2)}) %collective-permute-start.5) | collective-permute-done | bytes 458784 | tf_op jit(solution)/shard_map/cond/branch_0_fun/ppermute | solution.py:296
  134.8 11.3 %collective-permute-done.6.g3 = bf16[7,256,128]{2,1,0:T(8,128)(2,1)S(1)} collective-permute-done((bf16[7,256,128]{2,1,0:T(8,128)(2,1)S(1)}, bf16[7,256,128]{2,1,0:T(8,128)(2,1)S(1)}, u32[]{:S(2)}, u32[]{:S(2)}) %collective-permute-start.6) | collective-permute-done | bytes 458784 | tf_op jit(solution)/shard_map/cond/branch_0_fun/ppermute | solution.py:296
  146.1 2.5 %branch_0_fun.8 = (bf16[16,256,128]{2,1,0:T(8,128)(2,1)S(1)}, bf16[16,256,128]{2,1,0:T(8,128)(2,1)S(1)}) custom-call(s32[3]{0:T(128)S(1)} %get-tuple-element.75.place, s32[1024]{0:T(1024)S(1)} %get-tuple-element.65.code, bf16[16,256,128]{2,1,0:T(8,128)(2,1)S(1)} %copy-done.11, bf16[7,256,128]{2,1,0:T(8,128)(2,1)S(1)} %collective-permute-done.4.g1, ...), custom_call_target="tpu_custom_call" | custom-call | tf_op jit(solution)/shard_map/cond/branch_0_fun/pallas_call | solution.py:319
  148.6 2.4 %collective-permute-start.7 = (bf16[16,256,128]{2,1,0:T(8,128)(2,1)S(1)}, bf16[16,256,128]{2,1,0:T(8,128)(2,1)S(1)}, u32[]{:S(2)}, u32[]{:S(2)}) collective-permute-start(bf16[16,256,128]{2,1,0:T(8,128)(2,1)S(1)} %get-tuple-element.89), channel_id=1, source_target_pairs={{0,8},{8,0},{1,9},{9,1},{2,10},{10,2},{3,11},{11,3},{4,12},{12,4},... | collective-permute-start | bytes 3145736 | tf_op jit(solution)/shard_map/cond/branch_0_fun/ppermute | solution.py:296
  150.9 2.3 %collective-permute-done.7.right = bf16[16,256,128]{2,1,0:T(8,128)(2,1)S(1)} collective-permute-done((bf16[16,256,128]{2,1,0:T(8,128)(2,1)S(1)}, bf16[16,256,128]{2,1,0:T(8,128)(2,1)S(1)}, u32[]{:S(2)}, u32[]{:S(2)}) %collective-permute-start.7) | collective-permute-done | bytes 1048608 | tf_op jit(solution)/shard_map/cond/branch_0_fun/ppermute | solution.py:296
  153.2 1.2 branch_0_fun.9
  154.5 8.6 %all-to-all-start.9 = ((bf16[64,2,32,128]{3,2,1,0:T(8,128)(2,1)}), bf16[64,2,32,128]{3,2,1,0:T(8,128)(2,1)S(1)}, u32[]{:S(2)}, u32[]{:S(2)}) async-start(bf16[64,2,32,128]{3,2,1,0:T(8,128)(2,1)} %bitcast.26), calls=%async_computation.9 | async-start | bytes 2097152 | tf_op jit(solution)/shard_map/all_to_all | solution.py:304
  163.1 1.3 fusion.23
  164.4 1.4 copy_bitcast_fusion
  165.8 25.0 %all-to-all-done.9 = bf16[64,2,32,128]{3,2,1,0:T(8,128)(2,1)S(1)} async-done(((bf16[64,2,32,128]{3,2,1,0:T(8,128)(2,1)}), bf16[64,2,32,128]{3,2,1,0:T(8,128)(2,1)S(1)}, u32[]{:S(2)}, u32[]{:S(2)}) %all-to-all-start.9) | async-done | bytes 1048608 | tf_op jit(solution)/shard_map/all_to_all | solution.py:304
  (56 shorter events, 8.5 us)
Async XLA Ops:
  2.8 17.3 %copy-start.25 = (s32[128,8]{0,1:T(8,128)S(1)}, s32[128,8]{0,1:T(8,128)}, u32[]{:S(2)}) copy-start(s32[128,8]{0,1:T(8,128)} %param.15) | copy-start | bytes 12292
  2.8 46.7 %copy-start.19 = (bf16[32,64,128]{2,1,0:T(8,128)(2,1)S(1)}, bf16[32,64,128]{2,1,0:T(8,128)(2,1)}, u32[]{:S(2)}) copy-start(bf16[32,64,128]{2,1,0:T(8,128)(2,1)} %param.14) | copy-start | bytes 1572868
  2.8 44.7 %all-to-all-start.8 = ((bf16[64,2,32,128]{3,2,1,0:T(8,128)(2,1)}), bf16[64,2,32,128]{3,2,1,0:T(8,128)(2,1)S(1)}, u32[]{:S(2)}, u32[]{:S(2)}) async-start(bf16[64,2,32,128]{3,2,1,0:T(8,128)(2,1)} %bitcast.15), calls=%async_computation.8 | async-start | bytes 2097152 | tf_op jit(solution)/shard_map/all_to_all | solution.py:304
  20.0 29.4 %copy-start.16 = (bf16[32,64,128]{2,1,0:T(8,128)(2,1)S(1)}, bf16[32,64,128]{2,1,0:T(8,128)(2,1)}, u32[]{:S(2)}) copy-start(bf16[32,64,128]{2,1,0:T(8,128)(2,1)} %param.11) | copy-start | bytes 1572868
  21.2 0.8 copy-start.27
  49.4 0.7 copy-start.26
  51.9 43.4 %all-to-all-start = ((bf16[8,2,8,32,128]{4,3,2,1,0:T(8,128)(2,1)}), bf16[8,2,8,32,128]{4,3,2,1,0:T(8,128)(2,1)S(1)}, u32[]{:S(2)}, u32[]{:S(2)}) async-start(bf16[8,2,8,32,128]{4,3,2,1,0:T(8,128)(2,1)} %maximum_bitcast_fusion), calls=%async_computation | async-start | bytes 2097152 | tf_op jit(solution)/shard_map/cond/branch_0_fun/all_to_all | solution.py:304
  57.2 6.8 %collective-permute-start = (bf16[16,256,128]{2,1,0:T(8,128)(2,1)S(1)}, bf16[16,256,128]{2,1,0:T(8,128)(2,1)S(1)}, u32[]{:S(2)}, u32[]{:S(2)}) collective-permute-start(bf16[16,256,128]{2,1,0:T(8,128)(2,1)S(1)} %get-tuple-element.68.own), channel_id=1, source_target_pairs={{0,8},{8,0},{1,9},{9,1},{2,10},{10,2},{3,11},{11,3},{4,12},{12,4},... | collective-permute-start | bytes 3145736 | tf_op jit(solution)/shard_map/cond/branch_0_fun/ppermute | solution.py:296
  64.1 3.9 %copy-start.2 = (bf16[16,256,128]{2,1,0:T(8,128)(2,1)}, bf16[16,256,128]{2,1,0:T(8,128)(2,1)S(1)}, u32[]{:S(2)}) copy-start(bf16[16,256,128]{2,1,0:T(8,128)(2,1)S(1)} %collective-permute-done.oth) | copy-start | bytes 3145732 | tf_op jit(solution)/shard_map/cond
  68.0 15.3 %collective-permute-start.1 = (bf16[7,256,128]{2,1,0:T(8,128)(2,1)S(1)}, bf16[7,256,128]{2,1,0:T(8,128)(2,1)S(1)}, u32[]{:S(2)}, u32[]{:S(2)}) collective-permute-start(bf16[7,256,128]{2,1,0:T(8,128)(2,1)S(1)} %get-tuple-element.72), channel_id=1, source_target_pairs={{0,16},{16,32},{32,48},{48,0},{1,17},{17,33},{33,49},{49,1},{2,18}... | collective-permute-start | bytes 1376264 | tf_op jit(solution)/shard_map/cond/branch_0_fun/ppermute | solution.py:296
  70.8 22.1 %collective-permute-start.2 = (bf16[7,256,128]{2,1,0:T(8,128)(2,1)S(1)}, bf16[7,256,128]{2,1,0:T(8,128)(2,1)S(1)}, u32[]{:S(2)}, u32[]{:S(2)}) collective-permute-start(bf16[7,256,128]{2,1,0:T(8,128)(2,1)S(1)} %get-tuple-element.73), channel_id=1, source_target_pairs={{0,32},{16,48},{32,0},{48,16},{1,33},{17,49},{33,1},{49,17},{2,34}... | collective-permute-start | bytes 1376264 | tf_op jit(solution)/shard_map/cond/branch_0_fun/ppermute | solution.py:296
  75.0 20.3 %collective-permute-start.3 = (bf16[7,256,128]{2,1,0:T(8,128)(2,1)S(1)}, bf16[7,256,128]{2,1,0:T(8,128)(2,1)}, u32[]{:S(2)}, u32[]{:S(2)}) collective-permute-start(bf16[7,256,128]{2,1,0:T(8,128)(2,1)S(1)} %get-tuple-element.74), channel_id=1, source_target_pairs={{0,48},{16,0},{32,16},{48,32},{1,49},{17,1},{33,17},{49,33},{2,50}... | collective-permute-start | bytes 1376264 | tf_op jit(solution)/shard_map/cond/branch_0_fun/ppermute | solution.py:296
  80.4 1.0 copy-start.7
  83.2 12.1 %copy-start.33 = (bf16[7,256,128]{2,1,0:T(8,128)(2,1)}, bf16[7,256,128]{2,1,0:T(8,128)(2,1)S(1)}, u32[]{:S(2)}) copy-start(bf16[7,256,128]{2,1,0:T(8,128)(2,1)S(1)} %collective-permute-done.1.r1) | copy-start | bytes 1376260 | tf_op jit(solution)/shard_map/cond
  92.9 0.8 copy-start.35
  95.3 1.0 copy-start.22
  108.4 12.0 %copy-start.36 = (bf16[7,256,128]{2,1,0:T(8,128)(2,1)S(1)}, bf16[7,256,128]{2,1,0:T(8,128)(2,1)}, u32[]{:S(2)}) copy-start(bf16[7,256,128]{2,1,0:T(8,128)(2,1)} %get-tuple-element.80) | copy-start | bytes 1376260 | tf_op jit(solution)/shard_map/cond
  108.4 14.9 %copy-start.34 = (bf16[7,256,128]{2,1,0:T(8,128)(2,1)S(1)}, bf16[7,256,128]{2,1,0:T(8,128)(2,1)}, u32[]{:S(2)}) copy-start(bf16[7,256,128]{2,1,0:T(8,128)(2,1)} %get-tuple-element.81) | copy-start | bytes 1376260 | tf_op jit(solution)/shard_map/cond
  108.4 37.7 %copy-start.11 = (bf16[16,256,128]{2,1,0:T(8,128)(2,1)S(1)}, bf16[16,256,128]{2,1,0:T(8,128)(2,1)}, u32[]{:S(2)}) copy-start(bf16[16,256,128]{2,1,0:T(8,128)(2,1)} %get-tuple-element.84.g0) | copy-start | bytes 3145732 | tf_op jit(solution)/shard_map/cond
  108.4 37.7 %all-to-all-start.1 = ((bf16[8,2,8,32,128]{4,3,2,1,0:T(8,128)(2,1)}), bf16[8,2,8,32,128]{4,3,2,1,0:T(8,128)(2,1)}, u32[]{:S(2)}, u32[]{:S(2)}) async-start(bf16[8,2,8,32,128]{4,3,2,1,0:T(8,128)(2,1)} %get-tuple-element.82), calls=%async_computation.1 | async-start | bytes 2097152 | tf_op jit(solution)/shard_map/cond/branch_0_fun/all_to_all | solution.py:304
  115.5 14.6 %collective-permute-start.4 = (bf16[7,256,128]{2,1,0:T(8,128)(2,1)}, bf16[7,256,128]{2,1,0:T(8,128)(2,1)S(1)}, u32[]{:S(2)}, u32[]{:S(2)}) collective-permute-start(bf16[7,256,128]{2,1,0:T(8,128)(2,1)} %get-tuple-element.79), channel_id=1, source_target_pairs={{0,48},{16,0},{32,16},{48,32},{1,49},{17,1},{33,17},{49,33},{2,50}... | collective-permute-start | bytes 1376264 | tf_op jit(solution)/shard_map/cond/branch_0_fun/ppermute | solution.py:296
  120.4 14.4 %collective-permute-start.5 = (bf16[7,256,128]{2,1,0:T(8,128)(2,1)S(1)}, bf16[7,256,128]{2,1,0:T(8,128)(2,1)S(1)}, u32[]{:S(2)}, u32[]{:S(2)}) collective-permute-start(bf16[7,256,128]{2,1,0:T(8,128)(2,1)S(1)} %copy-done.36), channel_id=1, source_target_pairs={{0,32},{16,48},{32,0},{48,16},{1,33},{17,49},{33,1},{49,17},{2,34}... | collective-permute-start | bytes 1376264 | tf_op jit(solution)/shard_map/cond/branch_0_fun/ppermute | solution.py:296
  123.3 22.8 %collective-permute-start.6 = (bf16[7,256,128]{2,1,0:T(8,128)(2,1)S(1)}, bf16[7,256,128]{2,1,0:T(8,128)(2,1)S(1)}, u32[]{:S(2)}, u32[]{:S(2)}) collective-permute-start(bf16[7,256,128]{2,1,0:T(8,128)(2,1)S(1)} %copy-done.34), channel_id=1, source_target_pairs={{0,16},{16,32},{32,48},{48,0},{1,17},{17,33},{33,49},{49,1},{2,18}... | collective-permute-start | bytes 1376264 | tf_op jit(solution)/shard_map/cond/branch_0_fun/ppermute | solution.py:296
  148.6 4.6 %collective-permute-start.7 = (bf16[16,256,128]{2,1,0:T(8,128)(2,1)S(1)}, bf16[16,256,128]{2,1,0:T(8,128)(2,1)S(1)}, u32[]{:S(2)}, u32[]{:S(2)}) collective-permute-start(bf16[16,256,128]{2,1,0:T(8,128)(2,1)S(1)} %get-tuple-element.89), channel_id=1, source_target_pairs={{0,8},{8,0},{1,9},{9,1},{2,10},{10,2},{3,11},{11,3},{4,12},{12,4},... | collective-permute-start | bytes 3145736 | tf_op jit(solution)/shard_map/cond/branch_0_fun/ppermute | solution.py:296
  154.5 36.3 %all-to-all-start.9 = ((bf16[64,2,32,128]{3,2,1,0:T(8,128)(2,1)}), bf16[64,2,32,128]{3,2,1,0:T(8,128)(2,1)S(1)}, u32[]{:S(2)}, u32[]{:S(2)}) async-start(bf16[64,2,32,128]{3,2,1,0:T(8,128)(2,1)} %bitcast.26), calls=%async_computation.9 | async-start | bytes 2097152 | tf_op jit(solution)/shard_map/all_to_all | solution.py:304

commit v7 on v6

--- a/solution.py
+++ b/solution.py
@@ -386,17 +386,9 @@
     )(*operands)
 
 
-def between(slots, place, tables, own, queries, output_gradient, sess):
-    code, ent, kind = tables
-    other = shift(own, "core", 1)
+def between(slots, place, code, own, other, qd, mask):
     sends = gather(slots, place, code, own, other)
-    now, *sends = lax.optimization_barrier((place, *sends))
     fetched = [shift(sends[k - 1], "x", k) for k in (1, 2, 3)]
-    mask = masks(now, ent, kind, sess)
-
-    qd = jnp.stack([queries, output_gradient]).reshape(2, QUARTER, HEAD, GROUP, WIDTH)
-    qd = exchange(qd.transpose(2, 0, 3, 1, 4), "head")
-
     out, g0, g1, g2, g3 = attend(
         slots, place, code, qd, own, other, *fetched, mask
     )
@@ -417,17 +409,25 @@
     code, most = coded(kv_list)
     sess = session_id.astype(jnp.float32).reshape(-1, BLOCK)
 
-    kv = jnp.stack([keys, values]).transpose(2, 0, 1, 3)
-    kv = jnp.broadcast_to(kv, (Z, HEAD, 2, QUARTER, WIDTH))
-    own = exchange(kv.reshape(Z * HEAD, 2, QUARTER, WIDTH), ("z", "head"))
-    own = own.reshape(ENTRIES, 2 * BLOCK, WIDTH)
-
-    own, code, most, sess = lax.optimization_barrier((own, code, most, sess))
-    tables = (code, kv_list.T, kv_type.T)
+    code, most = lax.optimization_barrier((code, most))
+
+    kv = exchange(jnp.stack([keys, values]).transpose(2, 0, 1, 3), "head")
+    kv = kv.reshape(2, 2 * BLOCK, WIDTH)
+    kv, queries, output_gradient, sess = lax.optimization_barrier(
+        (kv, queries, output_gradient, sess)
+    )
+    own = lax.all_gather(kv, "z", axis=0, tiled=True)
+
+    qd = jnp.stack([queries, output_gradient]).reshape(2, QUARTER, HEAD, GROUP, WIDTH)
+    qd = exchange(qd.transpose(2, 0, 3, 1, 4), "head")
+    mask = masks(place, kv_list.T, kv_type.T, sess)
+    own, qd, mask = lax.optimization_barrier((own, qd, mask))
+    other = shift(own, "core", 1)
+
     out, column_sum = lax.switch(
         sum((most > few).astype(jnp.int32) for few in SLOTS[:-1]),
         [functools.partial(between, slots) for slots in SLOTS],
-        place, tables, own, queries, output_gradient, sess,
+        place, code, own, other, qd, mask,
     )
 
     parts = exchange(column_sum.reshape(Z * HEAD, 2, QUARTER, WIDTH), ("z", "head"))

time: 194 us -> 211 us (1.088)
  between operations: 2.72 us -> 16.2 us
  waiting for transfers between devices: 88.9 us -> 99.9 us
  starting transfers between devices: 64.9 us -> 57.9 us
    all_gather x0 -> x1, waiting for transfers between devices: none -> 27.7 us  [per_device(): own = lax.all_gather(kv, 'z', axis=0, tiled=True)]
    all_to_all x4, waiting for transfers between devices: 50.4 us -> 32.3 us  [exchange(): return lax.all_to_all(array, axis, split_axis=0, concat_axis=0, tiled=True)]
    all_to_all x4, starting transfers between devices: 38.3 us -> 28.2 us  [exchange(): return lax.all_to_all(array, axis, split_axis=0, concat_axis=0, tiled=True)]
    ppermute x8, starting transfers between devices: 26.6 us -> 29.7 us  [shift(): lax.ppermute(array, axis, [(i, (i + by) % size) for i in range(size)])]
    unnamed x13 -> x17, local copies, waits for them, and re-layouts: 2.19 us -> 4.38 us
  transfers between devices with their start and end apart: 12 -> 13, of which waited for: 10 -> 10; matrix products, arithmetic and copies ran while one was open for 2% -> 3% of each run, Pallas kernels for 3% -> 2%
where the time goes in v7:
time: 211 us; the launch traced here: 209 us
  waiting for transfers between devices  99.9 us (47%)
  starting transfers between devices  57.9 us (27%)
  Pallas kernels  21.3 us (10%)
  between operations  16.2 us (8%)
  local copies, waits for them, and re-layouts  10.9 us (5%)
  other arithmetic  2.91 us (1%)
    ppermute x8, waiting for transfers between devices, shift(): lax.ppermute(array, axis, [(i, (i + by) % size) for i in range(size)])  39.9 us
    all_to_all x4, waiting for transfers between devices, exchange(): return lax.all_to_all(array, axis, split_axis=0, concat_axis=0, tiled=True)  32.3 us
    ppermute x8, starting transfers between devices, shift(): lax.ppermute(array, axis, [(i, (i + by) % size) for i in range(size)])  29.7 us
    all_to_all x4, starting transfers between devices, exchange(): return lax.all_to_all(array, axis, split_axis=0, concat_axis=0, tiled=True)  28.2 us
    all_gather x1, waiting for transfers between devices, per_device(): own = lax.all_gather(kv, 'z', axis=0, tiled=True)  27.7 us
    pallas_call x1, Pallas kernels, attend(): pl.pallas_call(attend_kernel, out_shape=[outs, blocks(ENTRIES)] + [blocks...  12 us
    unnamed x17, local copies, waits for them, and re-layouts  4.38 us
  transfers between devices with their start and end apart: 13, of which 10 were waited for; matrix products, arithmetic and copies ran while one was open for 3% of the time, Pallas kernels for 2%

profile of v7, /device:TPU:1, one launch (start us, length us, event | category | flops | bytes accessed | tf_op | source)
XLA Modules:
  0.0 209.4 jit_solution(2957787809719109782)
XLA Ops:
  8.8 7.8 %all-to-all-start.4 = ((bf16[8,2,32,128]{3,2,1,0:T(8,128)(2,1)}), bf16[8,2,32,128]{3,2,1,0:T(8,128)(2,1)S(1)}, u32[]{:S(2)}, u32[]{:S(2)}) async-start(bf16[8,2,32,128]{3,2,1,0:T(8,128)(2,1)} %maximum_bitcast_fusion.1), calls=%async_computation.4 | async-start | bytes 262144 | tf_op jit(solution)/shard_map/all_to_all | solution.py:304
  16.6 8.0 %all-to-all-done.4 = bf16[8,2,32,128]{3,2,1,0:T(8,128)(2,1)S(1)} async-done(((bf16[8,2,32,128]{3,2,1,0:T(8,128)(2,1)}), bf16[8,2,32,128]{3,2,1,0:T(8,128)(2,1)S(1)}, u32[]{:S(2)}, u32[]{:S(2)}) %all-to-all-start.4) | async-done | bytes 131104 | tf_op jit(solution)/shard_map/all_to_all | solution.py:304
  26.7 1.1 maximum_bitcast_fusion
  27.8 3.7 %all-to-all-start.5 = ((bf16[8,2,8,32,128]{4,3,2,1,0:T(8,128)(2,1)}), bf16[8,2,8,32,128]{4,3,2,1,0:T(8,128)(2,1)S(1)}, u32[]{:S(2)}, u32[]{:S(2)}) async-start(bf16[8,2,8,32,128]{4,3,2,1,0:T(8,128)(2,1)} %maximum_bitcast_fusion), calls=%async_computation.5 | async-start | bytes 2097152 | tf_op jit(solution)/shard_map/all_to_all | solution.py:304
  32.8 3.4 %shard_map.102 = f32[16,128,128]{2,1,0:T(8,128)} custom-call(s32[3]{0:T(128)S(1)} %pad_add_fusion.place, s32[8,128]{1,0:T(8,128)S(1)} %bitcast.32, s32[8,128]{1,0:T(8,128)S(1)} %bitcast.33, f32[128,128]{1,0:T(8,128)S(1)} %convert_bitcast_fusion.sess), custom_call_target="tpu_custom_call" | custom-call | flops 2097152 | bytes 1048576 | tf_op jit(solution)/shard_map/pallas_call | solution.py:344
  36.3 27.7 %all-gather.2.cloned.1.call-done = bf16[16,256,128]{2,1,0:T(8,128)(2,1)} async-done(((bf16[2,256,128]{2,1,0:T(8,128)(2,1)}), bf16[16,256,128]{2,1,0:T(8,128)(2,1)}) %all-gather.2.cloned.1.call-update) | async-done | bytes 1048592 | tf_op jit(solution)/shard_map/all_gather | solution.py:419
  63.9 6.9 %collective-permute-start.28 = (bf16[16,256,128]{2,1,0:T(8,128)(2,1)}, bf16[16,256,128]{2,1,0:T(8,128)(2,1)S(1)}, u32[]{:S(2)}, u32[]{:S(2)}) collective-permute-start(bf16[16,256,128]{2,1,0:T(8,128)(2,1)} %all-gather.2.cloned.1.call-done), channel_id=1, source_target_pairs={{0,8},{8,0},{1,9},{9,1},{2,10},{10,2},{3,11},{11,3},{4,12},{12,4},... | collective-permute-start | bytes 3145736 | tf_op jit(solution)/shard_map/ppermute | solution.py:296
  74.0 88.1 %conditional.1 = (bf16[8,2,8,32,128]{4,3,2,1,0:T(8,128)(2,1)}, bf16[16,256,128]{2,1,0:T(8,128)(2,1)S(1)}) conditional(s32[]{:T(128)} %clamp.3, (s32[3]{0:T(128)S(1)}, s32[1024]{0:T(1024)S(1)}, bf16[16,256,128]{2,1,0:T(8,128)(2,1)}, bf16[16,256,128]{2,1,0:T(8,128)(2,1)S(1)}, bf16[8,2,8,32,128]{4,3,2,1,0:T(8,128)(2,1)S(1)}, ...), branch_computations={%region_3.4_spmd, %region_4.5_spmd, %region_5.6_spmd, %region_6.7_... | conditional | flops 2684354560 | bytes 64487948 | solution.py:427
  74.0 3.3 %branch_0_fun.4 = (bf16[7,256,128]{2,1,0:T(8,128)(2,1)S(1)}, bf16[7,256,128]{2,1,0:T(8,128)(2,1)S(1)}, bf16[7,256,128]{2,1,0:T(8,128)(2,1)S(1)}) custom-call(s32[3]{0:T(128)S(1)} %get-tuple-element.48.place, s32[1024]{0:T(1024)S(1)} %get-tuple-element.49.code, bf16[16,256,128]{2,1,0:T(8,128)(2,1)} %get-tuple-element.51.own, ...), custom_call_target="tpu_custom_call" | custom-call | tf_op jit(solution)/shard_map/cond/branch_0_fun/pallas_call | solution.py:308
  77.3 2.9 %collective-permute-start = (bf16[7,256,128]{2,1,0:T(8,128)(2,1)S(1)}, bf16[7,256,128]{2,1,0:T(8,128)(2,1)S(1)}, u32[]{:S(2)}, u32[]{:S(2)}) collective-permute-start(bf16[7,256,128]{2,1,0:T(8,128)(2,1)S(1)} %get-tuple-element.53), channel_id=1, source_target_pairs={{0,16},{16,32},{32,48},{48,0},{1,17},{17,33},{33,49},{49,1},{2,18}... | collective-permute-start | bytes 1376264 | tf_op jit(solution)/shard_map/cond/branch_0_fun/ppermute | solution.py:296
  80.2 4.2 %collective-permute-start.1 = (bf16[7,256,128]{2,1,0:T(8,128)(2,1)S(1)}, bf16[7,256,128]{2,1,0:T(8,128)(2,1)S(1)}, u32[]{:S(2)}, u32[]{:S(2)}) collective-permute-start(bf16[7,256,128]{2,1,0:T(8,128)(2,1)S(1)} %get-tuple-element.54), channel_id=1, source_target_pairs={{0,32},{16,48},{32,0},{48,16},{1,33},{17,49},{33,1},{49,17},{2,34}... | collective-permute-start | bytes 1376264 | tf_op jit(solution)/shard_map/cond/branch_0_fun/ppermute | solution.py:296
  84.4 3.4 %collective-permute-start.2 = (bf16[7,256,128]{2,1,0:T(8,128)(2,1)S(1)}, bf16[7,256,128]{2,1,0:T(8,128)(2,1)S(1)}, u32[]{:S(2)}, u32[]{:S(2)}) collective-permute-start(bf16[7,256,128]{2,1,0:T(8,128)(2,1)S(1)} %get-tuple-element.55), channel_id=1, source_target_pairs={{0,48},{16,0},{32,16},{48,32},{1,49},{17,1},{33,17},{49,33},{2,50}... | collective-permute-start | bytes 1376264 | tf_op jit(solution)/shard_map/cond/branch_0_fun/ppermute | solution.py:296
  87.8 5.0 %collective-permute-done.r1 = bf16[7,256,128]{2,1,0:T(8,128)(2,1)S(1)} collective-permute-done((bf16[7,256,128]{2,1,0:T(8,128)(2,1)S(1)}, bf16[7,256,128]{2,1,0:T(8,128)(2,1)S(1)}, u32[]{:S(2)}, u32[]{:S(2)}) %collective-permute-start) | collective-permute-done | bytes 458784 | tf_op jit(solution)/shard_map/cond/branch_0_fun/ppermute | solution.py:296
  92.8 10.3 %collective-permute-done.1.r2 = bf16[7,256,128]{2,1,0:T(8,128)(2,1)S(1)} collective-permute-done((bf16[7,256,128]{2,1,0:T(8,128)(2,1)S(1)}, bf16[7,256,128]{2,1,0:T(8,128)(2,1)S(1)}, u32[]{:S(2)}, u32[]{:S(2)}) %collective-permute-start.1) | collective-permute-done | bytes 458784 | tf_op jit(solution)/shard_map/cond/branch_0_fun/ppermute | solution.py:296
  103.1 1.9 collective-permute-done.2.r3
  105.8 12.0 %branch_0_fun.5 = (bf16[8,2,8,32,128]{4,3,2,1,0:T(8,128)(2,1)}, bf16[16,256,128]{2,1,0:T(8,128)(2,1)}, bf16[7,256,128]{2,1,0:T(8,128)(2,1)}, bf16[7,256,128]{2,1,0:T(8,128)(2,1)}, bf16[7,256,128]{2,1,0:T(8,128)(2,1)}) custom-call(s32[3]{0:T(128)S(1)} %get-tuple-element.48.place, s32[1024]{0:T(1024)S(1)} %get-tuple-element.49.code, ...), custom_call_target="tpu_custom_call" | custom-call | flops 2684354560 | bytes 8388608 | tf_op jit(solution)/shard_map/cond/branch_0_fun/pallas_call | solution.py:356
  117.8 6.4 %all-to-all-start = ((bf16[8,2,8,32,128]{4,3,2,1,0:T(8,128)(2,1)}), bf16[8,2,8,32,128]{4,3,2,1,0:T(8,128)(2,1)}, u32[]{:S(2)}, u32[]{:S(2)}) async-start(bf16[8,2,8,32,128]{4,3,2,1,0:T(8,128)(2,1)} %get-tuple-element.60), calls=%async_computation | async-start | bytes 2097152 | tf_op jit(solution)/shard_map/cond/branch_0_fun/all_to_all | solution.py:304
  124.2 4.4 %collective-permute-start.3 = (bf16[7,256,128]{2,1,0:T(8,128)(2,1)}, bf16[7,256,128]{2,1,0:T(8,128)(2,1)S(1)}, u32[]{:S(2)}, u32[]{:S(2)}) collective-permute-start(bf16[7,256,128]{2,1,0:T(8,128)(2,1)} %get-tuple-element.57), channel_id=1, source_target_pairs={{0,48},{16,0},{32,16},{48,32},{1,49},{17,1},{33,17},{49,33},{2,50}... | collective-permute-start | bytes 1376264 | tf_op jit(solution)/shard_map/cond/branch_0_fun/ppermute | solution.py:296
  128.6 3.5 %collective-permute-start.4 = (bf16[7,256,128]{2,1,0:T(8,128)(2,1)}, bf16[7,256,128]{2,1,0:T(8,128)(2,1)S(1)}, u32[]{:S(2)}, u32[]{:S(2)}) collective-permute-start(bf16[7,256,128]{2,1,0:T(8,128)(2,1)} %get-tuple-element.58), channel_id=1, source_target_pairs={{0,32},{16,48},{32,0},{48,16},{1,33},{17,49},{33,1},{49,17},{2,34}... | collective-permute-start | bytes 1376264 | tf_op jit(solution)/shard_map/cond/branch_0_fun/ppermute | solution.py:296
  132.1 1.9 collective-permute-start.5
  134.0 5.0 %collective-permute-done.3.g1 = bf16[7,256,128]{2,1,0:T(8,128)(2,1)S(1)} collective-permute-done((bf16[7,256,128]{2,1,0:T(8,128)(2,1)}, bf16[7,256,128]{2,1,0:T(8,128)(2,1)S(1)}, u32[]{:S(2)}, u32[]{:S(2)}) %collective-permute-start.3) | collective-permute-done | bytes 458784 | tf_op jit(solution)/shard_map/cond/branch_0_fun/ppermute | solution.py:296
  139.0 4.2 %collective-permute-done.4.g2 = bf16[7,256,128]{2,1,0:T(8,128)(2,1)S(1)} collective-permute-done((bf16[7,256,128]{2,1,0:T(8,128)(2,1)}, bf16[7,256,128]{2,1,0:T(8,128)(2,1)S(1)}, u32[]{:S(2)}, u32[]{:S(2)}) %collective-permute-start.4) | collective-permute-done | bytes 458784 | tf_op jit(solution)/shard_map/cond/branch_0_fun/ppermute | solution.py:296
  143.3 11.2 %collective-permute-done.5.g3 = bf16[7,256,128]{2,1,0:T(8,128)(2,1)S(1)} collective-permute-done((bf16[7,256,128]{2,1,0:T(8,128)(2,1)S(1)}, bf16[7,256,128]{2,1,0:T(8,128)(2,1)S(1)}, u32[]{:S(2)}, u32[]{:S(2)}) %collective-permute-start.5) | collective-permute-done | bytes 458784 | tf_op jit(solution)/shard_map/cond/branch_0_fun/ppermute | solution.py:296
  154.5 2.4 %branch_0_fun.6 = (bf16[16,256,128]{2,1,0:T(8,128)(2,1)S(1)}, bf16[16,256,128]{2,1,0:T(8,128)(2,1)S(1)}) custom-call(s32[3]{0:T(128)S(1)} %get-tuple-element.48.place, s32[1024]{0:T(1024)S(1)} %get-tuple-element.49.code, bf16[16,256,128]{2,1,0:T(8,128)(2,1)S(1)} %copy-done.3, bf16[7,256,128]{2,1,0:T(8,128)(2,1)S(1)} %collective-permute-done.3.g1, ...), custom_call_target="tpu_custom_call" | custom-call | tf_op jit(solution)/shard_map/cond/branch_0_fun/pallas_call | solution.py:319
  156.9 2.4 %collective-permute-start.6 = (bf16[16,256,128]{2,1,0:T(8,128)(2,1)S(1)}, bf16[16,256,128]{2,1,0:T(8,128)(2,1)S(1)}, u32[]{:S(2)}, u32[]{:S(2)}) collective-permute-start(bf16[16,256,128]{2,1,0:T(8,128)(2,1)S(1)} %get-tuple-element.67), channel_id=1, source_target_pairs={{0,8},{8,0},{1,9},{9,1},{2,10},{10,2},{3,11},{11,3},{4,12},{12,4},... | collective-permute-start | bytes 3145736 | tf_op jit(solution)/shard_map/cond/branch_0_fun/ppermute | solution.py:296
  159.3 2.3 %collective-permute-done.6.right = bf16[16,256,128]{2,1,0:T(8,128)(2,1)S(1)} collective-permute-done((bf16[16,256,128]{2,1,0:T(8,128)(2,1)S(1)}, bf16[16,256,128]{2,1,0:T(8,128)(2,1)S(1)}, u32[]{:S(2)}, u32[]{:S(2)}) %collective-permute-start.6) | collective-permute-done | bytes 1048608 | tf_op jit(solution)/shard_map/cond/branch_0_fun/ppermute | solution.py:296
  162.1 1.0 copy-done.12
  163.1 10.3 %all-to-all-start.6 = ((bf16[64,2,32,128]{3,2,1,0:T(8,128)(2,1)}), bf16[64,2,32,128]{3,2,1,0:T(8,128)(2,1)S(1)}, u32[]{:S(2)}, u32[]{:S(2)}) async-start(bf16[64,2,32,128]{3,2,1,0:T(8,128)(2,1)} %bitcast.34), calls=%async_computation.6 | async-start | bytes 2097152 | tf_op jit(solution)/shard_map/all_to_all | solution.py:304
  173.4 1.3 fusion.23
  174.7 1.0 copy.67
  175.7 1.0 copy.68
  176.7 24.3 %all-to-all-done.6 = bf16[64,2,32,128]{3,2,1,0:T(8,128)(2,1)S(1)} async-done(((bf16[64,2,32,128]{3,2,1,0:T(8,128)(2,1)}), bf16[64,2,32,128]{3,2,1,0:T(8,128)(2,1)S(1)}, u32[]{:S(2)}, u32[]{:S(2)}) %all-to-all-start.6) | async-done | bytes 1048608 | tf_op jit(solution)/shard_map/all_to_all | solution.py:304
  (59 shorter events, 8.8 us)
Async XLA Ops:
  7.2 18.1 %copy-start.13 = (bf16[32,64,128]{2,1,0:T(8,128)(2,1)S(1)}, bf16[32,64,128]{2,1,0:T(8,128)(2,1)}, u32[]{:S(2)}) copy-start(bf16[32,64,128]{2,1,0:T(8,128)(2,1)} %param.11) | copy-start | bytes 1572868
  8.8 7.8 %copy-start.16 = (s32[16384]{0:T(1024)S(1)}, s32[16384]{0:T(1024)}, u32[]{:S(2)}) copy-start(s32[16384]{0:T(1024)} %param.17) | copy-start | bytes 196612
  8.8 15.8 %all-to-all-start.4 = ((bf16[8,2,32,128]{3,2,1,0:T(8,128)(2,1)}), bf16[8,2,32,128]{3,2,1,0:T(8,128)(2,1)S(1)}, u32[]{:S(2)}, u32[]{:S(2)}) async-start(bf16[8,2,32,128]{3,2,1,0:T(8,128)(2,1)} %maximum_bitcast_fusion.1), calls=%async_computation.4 | async-start | bytes 262144 | tf_op jit(solution)/shard_map/all_to_all | solution.py:304
  16.6 47.3 %all-gather.2.cloned.1.call-start = ((), (), s32[]{:S(2)}) async-start(), calls=%async_computation.7 | async-start | bytes 1179648 | tf_op jit(solution)/shard_map/all_gather | solution.py:419
  24.6 0.7 copy-start.15
  25.3 1.0 copy-start.14
  27.8 3.7 %copy-start.6 = (s32[128,8]{0,1:T(8,128)S(1)}, s32[128,8]{0,1:T(8,128)}, u32[]{:S(2)}) copy-start(s32[128,8]{0,1:T(8,128)} %param.15) | copy-start | bytes 12292
  27.8 36.2 %all-to-all-start.5 = ((bf16[8,2,8,32,128]{4,3,2,1,0:T(8,128)(2,1)}), bf16[8,2,8,32,128]{4,3,2,1,0:T(8,128)(2,1)S(1)}, u32[]{:S(2)}, u32[]{:S(2)}) async-start(bf16[8,2,8,32,128]{4,3,2,1,0:T(8,128)(2,1)} %maximum_bitcast_fusion), calls=%async_computation.5 | async-start | bytes 2097152 | tf_op jit(solution)/shard_map/all_to_all | solution.py:304
  32.1 0.7 copy-start.7
  63.9 10.0 %collective-permute-start.28 = (bf16[16,256,128]{2,1,0:T(8,128)(2,1)}, bf16[16,256,128]{2,1,0:T(8,128)(2,1)S(1)}, u32[]{:S(2)}, u32[]{:S(2)}) collective-permute-start(bf16[16,256,128]{2,1,0:T(8,128)(2,1)} %all-gather.2.cloned.1.call-done), channel_id=1, source_target_pairs={{0,8},{8,0},{1,9},{9,1},{2,10},{10,2},{3,11},{11,3},{4,12},{12,4},... | collective-permute-start | bytes 3145736 | tf_op jit(solution)/shard_map/ppermute | solution.py:296
  74.0 31.8 %copy-start.8 = (bf16[16,256,128]{2,1,0:T(8,128)(2,1)S(1)}, bf16[16,256,128]{2,1,0:T(8,128)(2,1)}, u32[]{:S(2)}) copy-start(bf16[16,256,128]{2,1,0:T(8,128)(2,1)} %get-tuple-element.51.own) | copy-start | bytes 3145732 | tf_op jit(solution)/shard_map/cond
  77.3 15.5 %collective-permute-start = (bf16[7,256,128]{2,1,0:T(8,128)(2,1)S(1)}, bf16[7,256,128]{2,1,0:T(8,128)(2,1)S(1)}, u32[]{:S(2)}, u32[]{:S(2)}) collective-permute-start(bf16[7,256,128]{2,1,0:T(8,128)(2,1)S(1)} %get-tuple-element.53), channel_id=1, source_target_pairs={{0,16},{16,32},{32,48},{48,0},{1,17},{17,33},{33,49},{49,1},{2,18}... | collective-permute-start | bytes 1376264 | tf_op jit(solution)/shard_map/cond/branch_0_fun/ppermute | solution.py:296
  80.2 22.9 %collective-permute-start.1 = (bf16[7,256,128]{2,1,0:T(8,128)(2,1)S(1)}, bf16[7,256,128]{2,1,0:T(8,128)(2,1)S(1)}, u32[]{:S(2)}, u32[]{:S(2)}) collective-permute-start(bf16[7,256,128]{2,1,0:T(8,128)(2,1)S(1)} %get-tuple-element.54), channel_id=1, source_target_pairs={{0,32},{16,48},{32,0},{48,16},{1,33},{17,49},{33,1},{49,17},{2,34}... | collective-permute-start | bytes 1376264 | tf_op jit(solution)/shard_map/cond/branch_0_fun/ppermute | solution.py:296
  84.4 20.6 %collective-permute-start.2 = (bf16[7,256,128]{2,1,0:T(8,128)(2,1)S(1)}, bf16[7,256,128]{2,1,0:T(8,128)(2,1)S(1)}, u32[]{:S(2)}, u32[]{:S(2)}) collective-permute-start(bf16[7,256,128]{2,1,0:T(8,128)(2,1)S(1)} %get-tuple-element.55), channel_id=1, source_target_pairs={{0,48},{16,0},{32,16},{48,32},{1,49},{17,1},{33,17},{49,33},{2,50}... | collective-permute-start | bytes 1376264 | tf_op jit(solution)/shard_map/cond/branch_0_fun/ppermute | solution.py:296
  92.8 13.0 %copy-start.28 = (bf16[7,256,128]{2,1,0:T(8,128)(2,1)}, bf16[7,256,128]{2,1,0:T(8,128)(2,1)S(1)}, u32[]{:S(2)}) copy-start(bf16[7,256,128]{2,1,0:T(8,128)(2,1)S(1)} %collective-permute-done.r1) | copy-start | bytes 1376260 | tf_op jit(solution)/shard_map/cond
  103.1 1.9 copy-start.29
  105.0 0.8 copy-start.30
  117.8 14.3 %copy-start.27 = (bf16[7,256,128]{2,1,0:T(8,128)(2,1)S(1)}, bf16[7,256,128]{2,1,0:T(8,128)(2,1)}, u32[]{:S(2)}) copy-start(bf16[7,256,128]{2,1,0:T(8,128)(2,1)} %get-tuple-element.59) | copy-start | bytes 1376260 | tf_op jit(solution)/shard_map/cond
  117.8 36.7 %copy-start.3 = (bf16[16,256,128]{2,1,0:T(8,128)(2,1)S(1)}, bf16[16,256,128]{2,1,0:T(8,128)(2,1)}, u32[]{:S(2)}) copy-start(bf16[16,256,128]{2,1,0:T(8,128)(2,1)} %get-tuple-element.62.g0) | copy-start | bytes 3145732 | tf_op jit(solution)/shard_map/cond
  117.8 36.7 %all-to-all-start = ((bf16[8,2,8,32,128]{4,3,2,1,0:T(8,128)(2,1)}), bf16[8,2,8,32,128]{4,3,2,1,0:T(8,128)(2,1)}, u32[]{:S(2)}, u32[]{:S(2)}) async-start(bf16[8,2,8,32,128]{4,3,2,1,0:T(8,128)(2,1)} %get-tuple-element.60), calls=%async_computation | async-start | bytes 2097152 | tf_op jit(solution)/shard_map/cond/branch_0_fun/all_to_all | solution.py:304
  124.2 14.8 %collective-permute-start.3 = (bf16[7,256,128]{2,1,0:T(8,128)(2,1)}, bf16[7,256,128]{2,1,0:T(8,128)(2,1)S(1)}, u32[]{:S(2)}, u32[]{:S(2)}) collective-permute-start(bf16[7,256,128]{2,1,0:T(8,128)(2,1)} %get-tuple-element.57), channel_id=1, source_target_pairs={{0,48},{16,0},{32,16},{48,32},{1,49},{17,1},{33,17},{49,33},{2,50}... | collective-permute-start | bytes 1376264 | tf_op jit(solution)/shard_map/cond/branch_0_fun/ppermute | solution.py:296
  128.6 14.7 %collective-permute-start.4 = (bf16[7,256,128]{2,1,0:T(8,128)(2,1)}, bf16[7,256,128]{2,1,0:T(8,128)(2,1)S(1)}, u32[]{:S(2)}, u32[]{:S(2)}) collective-permute-start(bf16[7,256,128]{2,1,0:T(8,128)(2,1)} %get-tuple-element.58), channel_id=1, source_target_pairs={{0,32},{16,48},{32,0},{48,16},{1,33},{17,49},{33,1},{49,17},{2,34}... | collective-permute-start | bytes 1376264 | tf_op jit(solution)/shard_map/cond/branch_0_fun/ppermute | solution.py:296
  132.1 22.4 %collective-permute-start.5 = (bf16[7,256,128]{2,1,0:T(8,128)(2,1)S(1)}, bf16[7,256,128]{2,1,0:T(8,128)(2,1)S(1)}, u32[]{:S(2)}, u32[]{:S(2)}) collective-permute-start(bf16[7,256,128]{2,1,0:T(8,128)(2,1)S(1)} %copy-done.27), channel_id=1, source_target_pairs={{0,16},{16,32},{32,48},{48,0},{1,17},{17,33},{33,49},{49,1},{2,18}... | collective-permute-start | bytes 1376264 | tf_op jit(solution)/shard_map/cond/branch_0_fun/ppermute | solution.py:296
  156.9 4.7 %collective-permute-start.6 = (bf16[16,256,128]{2,1,0:T(8,128)(2,1)S(1)}, bf16[16,256,128]{2,1,0:T(8,128)(2,1)S(1)}, u32[]{:S(2)}, u32[]{:S(2)}) collective-permute-start(bf16[16,256,128]{2,1,0:T(8,128)(2,1)S(1)} %get-tuple-element.67), channel_id=1, source_target_pairs={{0,8},{8,0},{1,9},{9,1},{2,10},{10,2},{3,11},{11,3},{4,12},{12,4},... | collective-permute-start | bytes 3145736 | tf_op jit(solution)/shard_map/cond/branch_0_fun/ppermute | solution.py:296
  162.1 1.0 copy-start.12
  163.1 38.0 %all-to-all-start.6 = ((bf16[64,2,32,128]{3,2,1,0:T(8,128)(2,1)}), bf16[64,2,32,128]{3,2,1,0:T(8,128)(2,1)S(1)}, u32[]{:S(2)}, u32[]{:S(2)}) async-start(bf16[64,2,32,128]{3,2,1,0:T(8,128)(2,1)} %bitcast.34), calls=%async_computation.6 | async-start | bytes 2097152 | tf_op jit(solution)/shard_map/all_to_all | solution.py:304
Sparse Core Ops, SparseCore 0:
  25.4 38.4 all-gather.1

commit v8 on v6

--- a/solution.py
+++ b/solution.py
@@ -69,29 +69,21 @@
 
 
 def gather_kernel(place, code, own, oth, s1, s2, s3, sem):
-    for k, out in ((1, s1), (2, s2), (3, s3)):
-
-        def start(e, row, same_core, sl, k=k, out=out):
-            for source, chosen in ((own, same_core), (oth, jnp.logical_not(same_core))):
-
-                @pl.when(chosen)
-                def _(source=source):
-                    copy = pltpu.make_async_copy(source.at[row], out.at[sl], sem.at[k, sl])
-                    copy.start()
-
-        neighbour_entries(place, code, k, start)
-
-    for k, out in ((1, s1), (2, s2), (3, s3)):
-        z, x, core = place[0], place[1], place[2]
-        base = ((z * X + ((x + k) & (X - 1))) * CORE + core) * ENTRIES
-
-        def count(e, found, base=base):
-            _, _, owner_x, _, fresh, _ = fields(code[base + e])
-            return found + jnp.where((fresh == 1) & (owner_x == x), 1, 0)
-
-        @pl.loop(0, lax.fori_loop(0, ENTRIES, count, 0))
-        def _(sl, k=k, out=out):
-            pltpu.make_async_copy(own.at[0], out.at[sl], sem.at[k, sl]).wait()
+    def all_copies(act):
+        for k, out in ((1, s1), (2, s2), (3, s3)):
+
+            def one(e, row, same_core, sl, k=k, out=out):
+                for source, chosen in ((own, same_core), (oth, jnp.logical_not(same_core))):
+
+                    @pl.when(chosen)
+                    def _(source=source):
+                        done = sem.at[(k - 1) * ENTRIES + e]
+                        act(pltpu.make_async_copy(source.at[row], out.at[sl], done))
+
+            neighbour_entries(place, code, k, one)
+
+    all_copies(lambda copy: copy.start())
+    all_copies(lambda copy: copy.wait())
 
 
 def scatter_kernel(place, code, g0, g1, g2, g3, own_out, oth_out, acc):
@@ -310,7 +302,7 @@
         out_shape=[blocks(slots)] * 3,
         in_specs=[SMEM] * 2 + [HBM] * 2,
         out_specs=[HBM] * 3,
-        scratch_shapes=[DMA((X, ENTRIES))],
+        scratch_shapes=[DMA((3 * ENTRIES,))],
         compiler_params=params(4),
     )(*operands)
 
@@ -386,17 +378,11 @@
     )(*operands)
 
 
-def between(slots, place, tables, own, queries, output_gradient, sess):
-    code, ent, kind = tables
+def between(slots, place, code, own, qd, mask):
     other = shift(own, "core", 1)
     sends = gather(slots, place, code, own, other)
-    now, *sends = lax.optimization_barrier((place, *sends))
     fetched = [shift(sends[k - 1], "x", k) for k in (1, 2, 3)]
-    mask = masks(now, ent, kind, sess)
-
-    qd = jnp.stack([queries, output_gradient]).reshape(2, QUARTER, HEAD, GROUP, WIDTH)
-    qd = exchange(qd.transpose(2, 0, 3, 1, 4), "head")
-
+    qd = exchange(qd, "head")
     out, g0, g1, g2, g3 = attend(
         slots, place, code, qd, own, other, *fetched, mask
     )
@@ -417,17 +403,22 @@
     code, most = coded(kv_list)
     sess = session_id.astype(jnp.float32).reshape(-1, BLOCK)
 
+    code, most = lax.optimization_barrier((code, most))
+
     kv = jnp.stack([keys, values]).transpose(2, 0, 1, 3)
     kv = jnp.broadcast_to(kv, (Z, HEAD, 2, QUARTER, WIDTH))
     own = exchange(kv.reshape(Z * HEAD, 2, QUARTER, WIDTH), ("z", "head"))
     own = own.reshape(ENTRIES, 2 * BLOCK, WIDTH)
 
-    own, code, most, sess = lax.optimization_barrier((own, code, most, sess))
-    tables = (code, kv_list.T, kv_type.T)
+    qd = jnp.stack([queries, output_gradient]).reshape(2, QUARTER, HEAD, GROUP, WIDTH)
+    qd = qd.transpose(2, 0, 3, 1, 4)
+    mask = masks(place, kv_list.T, kv_type.T, sess)
+    qd, mask = lax.optimization_barrier((qd, mask))
+
     out, column_sum = lax.switch(
         sum((most > few).astype(jnp.int32) for few in SLOTS[:-1]),
         [functools.partial(between, slots) for slots in SLOTS],
-        place, tables, own, queries, output_gradient, sess,
+        place, code, own, qd, mask,
     )
 
     parts = exchange(column_sum.reshape(Z * HEAD, 2, QUARTER, WIDTH), ("z", "head"))

time: 194 us -> 196 us (1.010)
    ppermute x8, waiting for transfers between devices: 38.5 us -> 47.3 us  [shift(): lax.ppermute(array, axis, [(i, (i + by) % size) for i in range(size)])]
    all_to_all x4, waiting for transfers between devices: 50.4 us -> 42.5 us  [exchange(): return lax.all_to_all(array, axis, split_axis=0, concat_axis=0, tiled=True)]
    unnamed x13 -> x17, local copies, waits for them, and re-layouts: 2.19 us -> 4.83 us
  transfers between devices with their start and end apart: 12 -> 12, of which waited for: 10 -> 9; matrix products, arithmetic and copies ran while one was open for 2% -> 3% of each run, Pallas kernels for 3% -> 3%
where the time goes in v8:
time: 196 us; the launch traced here: 194 us
  waiting for transfers between devices  89.8 us (46%)
  starting transfers between devices  66 us (34%)
  Pallas kernels  20.6 us (11%)
  local copies, waits for them, and re-layouts  11.4 us (6%)
  other arithmetic  3.08 us (2%)
  between operations  2.75 us (1%)
    ppermute x8, waiting for transfers between devices, shift(): lax.ppermute(array, axis, [(i, (i + by) % size) for i in range(size)])  47.3 us
    all_to_all x4, waiting for transfers between devices, exchange(): return lax.all_to_all(array, axis, split_axis=0, concat_axis=0, tiled=True)  42.5 us
    all_to_all x4, starting transfers between devices, exchange(): return lax.all_to_all(array, axis, split_axis=0, concat_axis=0, tiled=True)  38.6 us
    ppermute x8, starting transfers between devices, shift(): lax.ppermute(array, axis, [(i, (i + by) % size) for i in range(size)])  27.4 us
    pallas_call x1, Pallas kernels, attend(): pl.pallas_call(attend_kernel, out_shape=[outs, blocks(ENTRIES)] + [blocks...  11.9 us
    unnamed x17, local copies, waits for them, and re-layouts  4.83 us
  transfers between devices with their start and end apart: 12, of which 9 were waited for; matrix products, arithmetic and copies ran while one was open for 3% of the time, Pallas kernels for 3%

profile of v8, /device:TPU:1, one launch (start us, length us, event | category | flops | bytes accessed | tf_op | source)
XLA Modules:
  0.0 194.0 jit_solution(13767205798725473924)
XLA Ops:
  1.5 1.2 broadcast_in_dim.30
  2.8 17.3 %all-to-all-start.8 = ((bf16[64,2,32,128]{3,2,1,0:T(8,128)(2,1)}), bf16[64,2,32,128]{3,2,1,0:T(8,128)(2,1)S(1)}, u32[]{:S(2)}, u32[]{:S(2)}) async-start(bf16[64,2,32,128]{3,2,1,0:T(8,128)(2,1)} %bitcast.12), calls=%async_computation.8 | async-start | bytes 2097152 | tf_op jit(solution)/shard_map/all_to_all | solution.py:296
  26.4 2.5 %shard_map.102 = f32[16,128,128]{2,1,0:T(8,128)S(1)} custom-call(s32[3]{0:T(128)S(1)} %pad_add_fusion.place, s32[8,128]{1,0:T(8,128)S(1)} %bitcast.29, s32[8,128]{1,0:T(8,128)S(1)} %bitcast.30, f32[128,128]{1,0:T(8,128)S(1)} %convert_bitcast_fusion.sess), custom_call_target="tpu_custom_call" | custom-call | flops 2097152 | bytes 1048576 | tf_op jit(solution)/shard_map/pallas_call | solution.py:336
  28.9 1.0 maximum_bitcast_fusion
  29.9 17.6 %all-to-all-done.8 = bf16[64,2,32,128]{3,2,1,0:T(8,128)(2,1)S(1)} async-done(((bf16[64,2,32,128]{3,2,1,0:T(8,128)(2,1)}), bf16[64,2,32,128]{3,2,1,0:T(8,128)(2,1)S(1)}, u32[]{:S(2)}, u32[]{:S(2)}) %all-to-all-start.8) | async-done | bytes 1048608 | tf_op jit(solution)/shard_map/all_to_all | solution.py:296
  47.5 107.5 %conditional.1 = (bf16[8,2,8,32,128]{4,3,2,1,0:T(8,128)(2,1)}, bf16[16,256,128]{2,1,0:T(8,128)(2,1)S(1)}) conditional(s32[]{:T(128)} %clamp.3, (bf16[8,2,8,32,128]{4,3,2,1,0:T(8,128)(2,1)}, bf16[16,256,128]{2,1,0:T(8,128)(2,1)S(1)}, s32[3]{0:T(128)S(1)}, s32[1024]{0:T(1024)S(1)}, ...), branch_computations={%region_3.4_spmd, %region_4.5_spmd, %region_5.6_spmd, %region_6.7_... | conditional | flops 2684354560 | bytes 72876624 | solution.py:418
  47.5 5.4 %all-to-all-start.2 = ((bf16[8,2,8,32,128]{4,3,2,1,0:T(8,128)(2,1)}), bf16[8,2,8,32,128]{4,3,2,1,0:T(8,128)(2,1)S(1)}, u32[]{:S(2)}, u32[]{:S(2)}) async-start(bf16[8,2,8,32,128]{4,3,2,1,0:T(8,128)(2,1)} %get-tuple-element.61), calls=%async_computation.2 | async-start | bytes 2097152 | tf_op jit(solution)/shard_map/cond/branch_1_fun/all_to_all | solution.py:296
  52.9 4.5 %collective-permute-start.8 = (bf16[16,256,128]{2,1,0:T(8,128)(2,1)S(1)}, bf16[16,256,128]{2,1,0:T(8,128)(2,1)S(1)}, u32[]{:S(2)}, u32[]{:S(2)}) collective-permute-start(bf16[16,256,128]{2,1,0:T(8,128)(2,1)S(1)} %get-tuple-element.62.own), channel_id=1, source_target_pairs={{0,8},{8,0},{1,9},{9,1},{2,10},{10,2},{3,11},{11,3},{4,12},{12,4},... | collective-permute-start | bytes 3145736 | tf_op jit(solution)/shard_map/cond/branch_1_fun/ppermute | solution.py:288
  57.4 2.3 %collective-permute-done.8.oth = bf16[16,256,128]{2,1,0:T(8,128)(2,1)S(1)} collective-permute-done((bf16[16,256,128]{2,1,0:T(8,128)(2,1)S(1)}, bf16[16,256,128]{2,1,0:T(8,128)(2,1)S(1)}, u32[]{:S(2)}, u32[]{:S(2)}) %collective-permute-start.8) | collective-permute-done | bytes 1048608 | tf_op jit(solution)/shard_map/cond/branch_1_fun/ppermute | solution.py:288
  59.7 3.6 %branch_1_fun.4 = (bf16[8,256,128]{2,1,0:T(8,128)(2,1)S(1)}, bf16[8,256,128]{2,1,0:T(8,128)(2,1)S(1)}, bf16[8,256,128]{2,1,0:T(8,128)(2,1)S(1)}) custom-call(s32[3]{0:T(128)S(1)} %get-tuple-element.59.place, s32[1024]{0:T(1024)S(1)} %get-tuple-element.60.code, bf16[16,256,128]{2,1,0:T(8,128)(2,1)S(1)} %get-tuple-element.62.own, ...), custom_call_target="tpu_custom_call" | custom-call | tf_op jit(solution)/shard_map/cond/branch_1_fun/pallas_call | solution.py:300
  63.3 2.8 %collective-permute-start.9 = (bf16[8,256,128]{2,1,0:T(8,128)(2,1)S(1)}, bf16[8,256,128]{2,1,0:T(8,128)(2,1)S(1)}, u32[]{:S(2)}, u32[]{:S(2)}) collective-permute-start(bf16[8,256,128]{2,1,0:T(8,128)(2,1)S(1)} %get-tuple-element.63), channel_id=1, source_target_pairs={{0,16},{16,32},{32,48},{48,0},{1,17},{17,33},{33,49},{49,1},{2,18}... | collective-permute-start | bytes 1572872 | tf_op jit(solution)/shard_map/cond/branch_1_fun/ppermute | solution.py:288
  66.1 5.1 %collective-permute-start.10 = (bf16[8,256,128]{2,1,0:T(8,128)(2,1)S(1)}, bf16[8,256,128]{2,1,0:T(8,128)(2,1)S(1)}, u32[]{:S(2)}, u32[]{:S(2)}) collective-permute-start(bf16[8,256,128]{2,1,0:T(8,128)(2,1)S(1)} %get-tuple-element.64), channel_id=1, source_target_pairs={{0,32},{16,48},{32,0},{48,16},{1,33},{17,49},{33,1},{49,17},{2,34}... | collective-permute-start | bytes 1572872 | tf_op jit(solution)/shard_map/cond/branch_1_fun/ppermute | solution.py:288
  71.2 2.6 %collective-permute-start.11 = (bf16[8,256,128]{2,1,0:T(8,128)(2,1)S(1)}, bf16[8,256,128]{2,1,0:T(8,128)(2,1)}, u32[]{:S(2)}, u32[]{:S(2)}) collective-permute-start(bf16[8,256,128]{2,1,0:T(8,128)(2,1)S(1)} %get-tuple-element.65), channel_id=1, source_target_pairs={{0,48},{16,0},{32,16},{48,32},{1,49},{17,1},{33,17},{49,33},{2,50}... | collective-permute-start | bytes 1572872 | tf_op jit(solution)/shard_map/cond/branch_1_fun/ppermute | solution.py:288
  73.8 5.8 %collective-permute-done.9.r1 = bf16[8,256,128]{2,1,0:T(8,128)(2,1)S(1)} collective-permute-done((bf16[8,256,128]{2,1,0:T(8,128)(2,1)S(1)}, bf16[8,256,128]{2,1,0:T(8,128)(2,1)S(1)}, u32[]{:S(2)}, u32[]{:S(2)}) %collective-permute-start.9) | collective-permute-done | bytes 524320 | tf_op jit(solution)/shard_map/cond/branch_1_fun/ppermute | solution.py:288
  79.6 13.0 %collective-permute-done.10.r2 = bf16[8,256,128]{2,1,0:T(8,128)(2,1)S(1)} collective-permute-done((bf16[8,256,128]{2,1,0:T(8,128)(2,1)S(1)}, bf16[8,256,128]{2,1,0:T(8,128)(2,1)S(1)}, u32[]{:S(2)}, u32[]{:S(2)}) %collective-permute-start.10) | collective-permute-done | bytes 524320 | tf_op jit(solution)/shard_map/cond/branch_1_fun/ppermute | solution.py:288
  93.5 1.0 copy-done.16
  94.5 11.9 %branch_1_fun.5 = (bf16[8,2,8,32,128]{4,3,2,1,0:T(8,128)(2,1)}, bf16[16,256,128]{2,1,0:T(8,128)(2,1)}, bf16[8,256,128]{2,1,0:T(8,128)(2,1)}, bf16[8,256,128]{2,1,0:T(8,128)(2,1)}, bf16[8,256,128]{2,1,0:T(8,128)(2,1)}) custom-call(s32[3]{0:T(128)S(1)} %get-tuple-element.59.place, s32[1024]{0:T(1024)S(1)} %get-tuple-element.60.code, ...), custom_call_target="tpu_custom_call" | custom-call | flops 2684354560 | bytes 8388608 | tf_op jit(solution)/shard_map/cond/branch_1_fun/pallas_call | solution.py:348
  106.4 7.1 %all-to-all-start.3 = ((bf16[8,2,8,32,128]{4,3,2,1,0:T(8,128)(2,1)}), bf16[8,2,8,32,128]{4,3,2,1,0:T(8,128)(2,1)}, u32[]{:S(2)}, u32[]{:S(2)}) async-start(bf16[8,2,8,32,128]{4,3,2,1,0:T(8,128)(2,1)} %get-tuple-element.70), calls=%async_computation.3 | async-start | bytes 2097152 | tf_op jit(solution)/shard_map/cond/branch_1_fun/all_to_all | solution.py:296
  113.4 5.3 %collective-permute-start.12 = (bf16[8,256,128]{2,1,0:T(8,128)(2,1)}, bf16[8,256,128]{2,1,0:T(8,128)(2,1)S(1)}, u32[]{:S(2)}, u32[]{:S(2)}) collective-permute-start(bf16[8,256,128]{2,1,0:T(8,128)(2,1)} %get-tuple-element.67), channel_id=1, source_target_pairs={{0,48},{16,0},{32,16},{48,32},{1,49},{17,1},{33,17},{49,33},{2,50}... | collective-permute-start | bytes 1572872 | tf_op jit(solution)/shard_map/cond/branch_1_fun/ppermute | solution.py:288
  118.7 2.8 %collective-permute-start.13 = (bf16[8,256,128]{2,1,0:T(8,128)(2,1)}, bf16[8,256,128]{2,1,0:T(8,128)(2,1)S(1)}, u32[]{:S(2)}, u32[]{:S(2)}) collective-permute-start(bf16[8,256,128]{2,1,0:T(8,128)(2,1)} %get-tuple-element.68), channel_id=1, source_target_pairs={{0,32},{16,48},{32,0},{48,16},{1,33},{17,49},{33,1},{49,17},{2,34}... | collective-permute-start | bytes 1572872 | tf_op jit(solution)/shard_map/cond/branch_1_fun/ppermute | solution.py:288
  121.6 1.9 collective-permute-start.14
  123.5 6.7 %collective-permute-done.12.g1 = bf16[8,256,128]{2,1,0:T(8,128)(2,1)S(1)} collective-permute-done((bf16[8,256,128]{2,1,0:T(8,128)(2,1)}, bf16[8,256,128]{2,1,0:T(8,128)(2,1)S(1)}, u32[]{:S(2)}, u32[]{:S(2)}) %collective-permute-start.12) | collective-permute-done | bytes 524320 | tf_op jit(solution)/shard_map/cond/branch_1_fun/ppermute | solution.py:288
  130.2 4.7 %collective-permute-done.13.g2 = bf16[8,256,128]{2,1,0:T(8,128)(2,1)S(1)} collective-permute-done((bf16[8,256,128]{2,1,0:T(8,128)(2,1)}, bf16[8,256,128]{2,1,0:T(8,128)(2,1)S(1)}, u32[]{:S(2)}, u32[]{:S(2)}) %collective-permute-start.13) | collective-permute-done | bytes 524320 | tf_op jit(solution)/shard_map/cond/branch_1_fun/ppermute | solution.py:288
  134.9 12.5 %collective-permute-done.14.g3 = bf16[8,256,128]{2,1,0:T(8,128)(2,1)S(1)} collective-permute-done((bf16[8,256,128]{2,1,0:T(8,128)(2,1)S(1)}, bf16[8,256,128]{2,1,0:T(8,128)(2,1)S(1)}, u32[]{:S(2)}, u32[]{:S(2)}) %collective-permute-start.14) | collective-permute-done | bytes 524320 | tf_op jit(solution)/shard_map/cond/branch_1_fun/ppermute | solution.py:288
  147.4 2.4 %branch_1_fun.6 = (bf16[16,256,128]{2,1,0:T(8,128)(2,1)S(1)}, bf16[16,256,128]{2,1,0:T(8,128)(2,1)S(1)}) custom-call(s32[3]{0:T(128)S(1)} %get-tuple-element.59.place, s32[1024]{0:T(1024)S(1)} %get-tuple-element.60.code, bf16[16,256,128]{2,1,0:T(8,128)(2,1)S(1)} %copy-done.5, bf16[8,256,128]{2,1,0:T(8,128)(2,1)S(1)} %collective-permute-done.12.g1, ...), custom_call_target="tpu_custom_call" | custom-call | tf_op jit(solution)/shard_map/cond/branch_1_fun/pallas_call | solution.py:311
  149.8 2.4 %collective-permute-start.15 = (bf16[16,256,128]{2,1,0:T(8,128)(2,1)S(1)}, bf16[16,256,128]{2,1,0:T(8,128)(2,1)S(1)}, u32[]{:S(2)}, u32[]{:S(2)}) collective-permute-start(bf16[16,256,128]{2,1,0:T(8,128)(2,1)S(1)} %get-tuple-element.77), channel_id=1, source_target_pairs={{0,8},{8,0},{1,9},{9,1},{2,10},{10,2},{3,11},{11,3},{4,12},{12,4},... | collective-permute-start | bytes 3145736 | tf_op jit(solution)/shard_map/cond/branch_1_fun/ppermute | solution.py:288
  152.3 2.3 %collective-permute-done.15.right = bf16[16,256,128]{2,1,0:T(8,128)(2,1)S(1)} collective-permute-done((bf16[16,256,128]{2,1,0:T(8,128)(2,1)S(1)}, bf16[16,256,128]{2,1,0:T(8,128)(2,1)S(1)}, u32[]{:S(2)}, u32[]{:S(2)}) %collective-permute-start.15) | collective-permute-done | bytes 1048608 | tf_op jit(solution)/shard_map/cond/branch_1_fun/ppermute | solution.py:288
  155.0 0.9 copy-done.13
  156.0 8.9 %all-to-all-start.9 = ((bf16[64,2,32,128]{3,2,1,0:T(8,128)(2,1)}), bf16[64,2,32,128]{3,2,1,0:T(8,128)(2,1)S(1)}, u32[]{:S(2)}, u32[]{:S(2)}) async-start(bf16[64,2,32,128]{3,2,1,0:T(8,128)(2,1)} %bitcast.35), calls=%async_computation.9 | async-start | bytes 2097152 | tf_op jit(solution)/shard_map/all_to_all | solution.py:296
  164.8 1.3 fusion.23
  166.1 1.4 copy_bitcast_fusion
  167.5 25.0 %all-to-all-done.9 = bf16[64,2,32,128]{3,2,1,0:T(8,128)(2,1)S(1)} async-done(((bf16[64,2,32,128]{3,2,1,0:T(8,128)(2,1)}), bf16[64,2,32,128]{3,2,1,0:T(8,128)(2,1)S(1)}, u32[]{:S(2)}, u32[]{:S(2)}) %all-to-all-start.9) | async-done | bytes 1048608 | tf_op jit(solution)/shard_map/all_to_all | solution.py:296
  (54 shorter events, 7.8 us)
Async XLA Ops:
  2.8 17.3 %copy-start.10 = (s32[128,8]{0,1:T(8,128)S(1)}, s32[128,8]{0,1:T(8,128)}, u32[]{:S(2)}) copy-start(s32[128,8]{0,1:T(8,128)} %param.15) | copy-start | bytes 12292
  2.8 44.7 %all-to-all-start.8 = ((bf16[64,2,32,128]{3,2,1,0:T(8,128)(2,1)}), bf16[64,2,32,128]{3,2,1,0:T(8,128)(2,1)S(1)}, u32[]{:S(2)}, u32[]{:S(2)}) async-start(bf16[64,2,32,128]{3,2,1,0:T(8,128)(2,1)} %bitcast.12), calls=%async_computation.8 | async-start | bytes 2097152 | tf_op jit(solution)/shard_map/all_to_all | solution.py:296
  20.1 3.8 %copy-start.18 = (bf16[32,64,128]{2,1,0:T(8,128)(2,1)S(1)}, bf16[32,64,128]{2,1,0:T(8,128)(2,1)}, u32[]{:S(2)}) copy-start(bf16[32,64,128]{2,1,0:T(8,128)(2,1)} %param.11) | copy-start | bytes 1572868
  23.9 1.0 copy-start.19
  24.9 0.8 copy-start.20
  25.7 0.7 copy-start.11
  47.5 45.9 %all-to-all-start.2 = ((bf16[8,2,8,32,128]{4,3,2,1,0:T(8,128)(2,1)}), bf16[8,2,8,32,128]{4,3,2,1,0:T(8,128)(2,1)S(1)}, u32[]{:S(2)}, u32[]{:S(2)}) async-start(bf16[8,2,8,32,128]{4,3,2,1,0:T(8,128)(2,1)} %get-tuple-element.61), calls=%async_computation.2 | async-start | bytes 2097152 | tf_op jit(solution)/shard_map/cond/branch_1_fun/all_to_all | solution.py:296
  52.9 6.8 %collective-permute-start.8 = (bf16[16,256,128]{2,1,0:T(8,128)(2,1)S(1)}, bf16[16,256,128]{2,1,0:T(8,128)(2,1)S(1)}, u32[]{:S(2)}, u32[]{:S(2)}) collective-permute-start(bf16[16,256,128]{2,1,0:T(8,128)(2,1)S(1)} %get-tuple-element.62.own), channel_id=1, source_target_pairs={{0,8},{8,0},{1,9},{9,1},{2,10},{10,2},{3,11},{11,3},{4,12},{12,4},... | collective-permute-start | bytes 3145736 | tf_op jit(solution)/shard_map/cond/branch_1_fun/ppermute | solution.py:288
  59.7 3.6 %copy-start.3 = (bf16[16,256,128]{2,1,0:T(8,128)(2,1)}, bf16[16,256,128]{2,1,0:T(8,128)(2,1)S(1)}, u32[]{:S(2)}) copy-start(bf16[16,256,128]{2,1,0:T(8,128)(2,1)S(1)} %collective-permute-done.8.oth) | copy-start | bytes 3145732 | tf_op jit(solution)/shard_map/cond
  63.3 16.3 %collective-permute-start.9 = (bf16[8,256,128]{2,1,0:T(8,128)(2,1)S(1)}, bf16[8,256,128]{2,1,0:T(8,128)(2,1)S(1)}, u32[]{:S(2)}, u32[]{:S(2)}) collective-permute-start(bf16[8,256,128]{2,1,0:T(8,128)(2,1)S(1)} %get-tuple-element.63), channel_id=1, source_target_pairs={{0,16},{16,32},{32,48},{48,0},{1,17},{17,33},{33,49},{49,1},{2,18}... | collective-permute-start | bytes 1572872 | tf_op jit(solution)/shard_map/cond/branch_1_fun/ppermute | solution.py:288
  66.1 26.6 %collective-permute-start.10 = (bf16[8,256,128]{2,1,0:T(8,128)(2,1)S(1)}, bf16[8,256,128]{2,1,0:T(8,128)(2,1)S(1)}, u32[]{:S(2)}, u32[]{:S(2)}) collective-permute-start(bf16[8,256,128]{2,1,0:T(8,128)(2,1)S(1)} %get-tuple-element.64), channel_id=1, source_target_pairs={{0,32},{16,48},{32,0},{48,16},{1,33},{17,49},{33,1},{49,17},{2,34}... | collective-permute-start | bytes 1572872 | tf_op jit(solution)/shard_map/cond/branch_1_fun/ppermute | solution.py:288
  71.2 22.3 %collective-permute-start.11 = (bf16[8,256,128]{2,1,0:T(8,128)(2,1)S(1)}, bf16[8,256,128]{2,1,0:T(8,128)(2,1)}, u32[]{:S(2)}, u32[]{:S(2)}) collective-permute-start(bf16[8,256,128]{2,1,0:T(8,128)(2,1)S(1)} %get-tuple-element.65), channel_id=1, source_target_pairs={{0,48},{16,0},{32,16},{48,32},{1,49},{17,1},{33,17},{49,33},{2,50}... | collective-permute-start | bytes 1572872 | tf_op jit(solution)/shard_map/cond/branch_1_fun/ppermute | solution.py:288
  79.6 13.0 %copy-start.24 = (bf16[8,256,128]{2,1,0:T(8,128)(2,1)}, bf16[8,256,128]{2,1,0:T(8,128)(2,1)S(1)}, u32[]{:S(2)}) copy-start(bf16[8,256,128]{2,1,0:T(8,128)(2,1)S(1)} %collective-permute-done.9.r1) | copy-start | bytes 1572868 | tf_op jit(solution)/shard_map/cond
  92.7 0.8 copy-start.26
  93.5 1.0 copy-start.16
  106.3 15.2 %copy-start.25 = (bf16[8,256,128]{2,1,0:T(8,128)(2,1)S(1)}, bf16[8,256,128]{2,1,0:T(8,128)(2,1)}, u32[]{:S(2)}) copy-start(bf16[8,256,128]{2,1,0:T(8,128)(2,1)} %get-tuple-element.69) | copy-start | bytes 1572868 | tf_op jit(solution)/shard_map/cond
  106.4 41.0 %copy-start.5 = (bf16[16,256,128]{2,1,0:T(8,128)(2,1)S(1)}, bf16[16,256,128]{2,1,0:T(8,128)(2,1)}, u32[]{:S(2)}) copy-start(bf16[16,256,128]{2,1,0:T(8,128)(2,1)} %get-tuple-element.72.g0) | copy-start | bytes 3145732 | tf_op jit(solution)/shard_map/cond
  106.4 41.0 %all-to-all-start.3 = ((bf16[8,2,8,32,128]{4,3,2,1,0:T(8,128)(2,1)}), bf16[8,2,8,32,128]{4,3,2,1,0:T(8,128)(2,1)}, u32[]{:S(2)}, u32[]{:S(2)}) async-start(bf16[8,2,8,32,128]{4,3,2,1,0:T(8,128)(2,1)} %get-tuple-element.70), calls=%async_computation.3 | async-start | bytes 2097152 | tf_op jit(solution)/shard_map/cond/branch_1_fun/all_to_all | solution.py:296
  113.4 16.8 %collective-permute-start.12 = (bf16[8,256,128]{2,1,0:T(8,128)(2,1)}, bf16[8,256,128]{2,1,0:T(8,128)(2,1)S(1)}, u32[]{:S(2)}, u32[]{:S(2)}) collective-permute-start(bf16[8,256,128]{2,1,0:T(8,128)(2,1)} %get-tuple-element.67), channel_id=1, source_target_pairs={{0,48},{16,0},{32,16},{48,32},{1,49},{17,1},{33,17},{49,33},{2,50}... | collective-permute-start | bytes 1572872 | tf_op jit(solution)/shard_map/cond/branch_1_fun/ppermute | solution.py:288
  118.7 16.2 %collective-permute-start.13 = (bf16[8,256,128]{2,1,0:T(8,128)(2,1)}, bf16[8,256,128]{2,1,0:T(8,128)(2,1)S(1)}, u32[]{:S(2)}, u32[]{:S(2)}) collective-permute-start(bf16[8,256,128]{2,1,0:T(8,128)(2,1)} %get-tuple-element.68), channel_id=1, source_target_pairs={{0,32},{16,48},{32,0},{48,16},{1,33},{17,49},{33,1},{49,17},{2,34}... | collective-permute-start | bytes 1572872 | tf_op jit(solution)/shard_map/cond/branch_1_fun/ppermute | solution.py:288
  121.6 25.8 %collective-permute-start.14 = (bf16[8,256,128]{2,1,0:T(8,128)(2,1)S(1)}, bf16[8,256,128]{2,1,0:T(8,128)(2,1)S(1)}, u32[]{:S(2)}, u32[]{:S(2)}) collective-permute-start(bf16[8,256,128]{2,1,0:T(8,128)(2,1)S(1)} %copy-done.25), channel_id=1, source_target_pairs={{0,16},{16,32},{32,48},{48,0},{1,17},{17,33},{33,49},{49,1},{2,18}... | collective-permute-start | bytes 1572872 | tf_op jit(solution)/shard_map/cond/branch_1_fun/ppermute | solution.py:288
  149.8 4.7 %collective-permute-start.15 = (bf16[16,256,128]{2,1,0:T(8,128)(2,1)S(1)}, bf16[16,256,128]{2,1,0:T(8,128)(2,1)S(1)}, u32[]{:S(2)}, u32[]{:S(2)}) collective-permute-start(bf16[16,256,128]{2,1,0:T(8,128)(2,1)S(1)} %get-tuple-element.77), channel_id=1, source_target_pairs={{0,8},{8,0},{1,9},{9,1},{2,10},{10,2},{3,11},{11,3},{4,12},{12,4},... | collective-permute-start | bytes 3145736 | tf_op jit(solution)/shard_map/cond/branch_1_fun/ppermute | solution.py:288
  155.0 0.9 copy-start.13
  156.0 36.5 %all-to-all-start.9 = ((bf16[64,2,32,128]{3,2,1,0:T(8,128)(2,1)}), bf16[64,2,32,128]{3,2,1,0:T(8,128)(2,1)S(1)}, u32[]{:S(2)}, u32[]{:S(2)}) async-start(bf16[64,2,32,128]{3,2,1,0:T(8,128)(2,1)} %bitcast.35), calls=%async_computation.9 | async-start | bytes 2097152 | tf_op jit(solution)/shard_map/all_to_all | solution.py:296

commit v9 on v8

--- a/solution.py
+++ b/solution.py
@@ -55,46 +55,51 @@
     return code.reshape(-1), most
 
 
-def neighbour_entries(place, code, k, what):
-    z, x, core = place[0], place[1], place[2]
-    base = ((z * X + ((x + k) & (X - 1))) * CORE + core) * ENTRIES
-
-    @pl.loop(0, ENTRIES)
-    def _(e):
-        row, owner_core, owner_x, sl, fresh, _ = fields(code[base + e])
-
-        @pl.when((fresh == 1) & (owner_x == x))
-        def _():
-            what(e, row, owner_core == core, sl)
-
-
-def gather_kernel(place, code, own, oth, s1, s2, s3, sem):
-    def all_copies(act):
-        for k, out in ((1, s1), (2, s2), (3, s3)):
-
-            def one(e, row, same_core, sl, k=k, out=out):
-                for source, chosen in ((own, same_core), (oth, jnp.logical_not(same_core))):
-
-                    @pl.when(chosen)
-                    def _(source=source):
-                        done = sem.at[(k - 1) * ENTRIES + e]
-                        act(pltpu.make_async_copy(source.at[row], out.at[sl], done))
-
-            neighbour_entries(place, code, k, one)
-
-    all_copies(lambda copy: copy.start())
-    all_copies(lambda copy: copy.wait())
-
-
-def scatter_kernel(place, code, g0, g1, g2, g3, own_out, oth_out, acc):
+def neighbour_lists(place, code):
+    z, x, core = place
+    index = [(z * X + lax.rem(x + k, X)) * CORE + core for k in range(X)]
+    code = code.reshape(CTX, ENTRIES)
+    lines = jnp.stack([lax.dynamic_index_in_dim(code, d, 0, keepdims=False) for d in index])
+    row, owner_core, owner_x, slot, fresh, _ = fields(lines)
+    mine = (fresh == 1) & (owner_x == x)
+    at = row + jnp.where(owner_core == core, 0, ENTRIES)
+    slots = jnp.arange(ENTRIES, dtype=jnp.int32)[None, :, None]
+    here = mine[:, None, :] & (slot[:, None, :] == slots)
+    listed = jnp.sum(jnp.where(here, at[:, None, :], 0), axis=2)
+    count = jnp.sum(mine.astype(jnp.int32), axis=1)
+    return jnp.concatenate([listed.reshape(-1), count])
+
+
+def gather_kernel(lists, own, oth, s1, s2, s3, sem):
+    for k, out in ((2, s2), (1, s1), (3, s3)):
+
+        @pl.loop(0, lists[X * ENTRIES + k])
+        def _(sl, k=k, out=out):
+            at = lists[k * ENTRIES + sl]
+
+            @pl.when(at < ENTRIES)
+            def _():
+                pltpu.make_async_copy(own.at[at], out.at[sl], sem.at[k * ENTRIES + sl]).start()
+
+            @pl.when(at >= ENTRIES)
+            def _():
+                source = oth.at[at - ENTRIES]
+                pltpu.make_async_copy(source, out.at[sl], sem.at[k * ENTRIES + sl]).start()
+
+    for k, out in ((2, s2), (1, s1), (3, s3)):
+
+        @pl.loop(0, lists[X * ENTRIES + k])
+        def _(sl, k=k, out=out):
+            pltpu.make_async_copy(own.at[0], out.at[sl], sem.at[k * ENTRIES + sl]).wait()
+
+
+def scatter_kernel(lists, g0, g1, g2, g3, own_out, oth_out, acc):
     acc[...] = jnp.zeros_like(acc)
     for k, buf in ((0, g0), (1, g1), (2, g2), (3, g3)):
 
-        def add(e, row, same_core, sl, buf=buf):
-            to = row + jnp.where(same_core, 0, ENTRIES)
-            acc[to] += buf[sl].astype(jnp.float32)
-
-        neighbour_entries(place, code, k, add)
+        @pl.loop(0, lists[X * ENTRIES + k])
+        def _(sl, k=k, buf=buf):
+            acc[lists[k * ENTRIES + sl]] += buf[sl].astype(jnp.float32)
 
     own_out[...] = acc[:ENTRIES].astype(jnp.bfloat16)
     oth_out[...] = acc[ENTRIES:].astype(jnp.bfloat16)
@@ -300,9 +305,9 @@
     return pl.pallas_call(
         gather_kernel,
         out_shape=[blocks(slots)] * 3,
-        in_specs=[SMEM] * 2 + [HBM] * 2,
+        in_specs=[SMEM] + [HBM] * 2,
         out_specs=[HBM] * 3,
-        scratch_shapes=[DMA((3 * ENTRIES,))],
+        scratch_shapes=[DMA((X * ENTRIES,))],
         compiler_params=params(4),
     )(*operands)
 
@@ -311,7 +316,7 @@
     return pl.pallas_call(
         scatter_kernel,
         out_shape=[blocks(ENTRIES)] * 2,
-        in_specs=[SMEM] * 2 + [VMEM] * 4,
+        in_specs=[SMEM] + [VMEM] * 4,
         out_specs=[VMEM] * 2,
         scratch_shapes=[pltpu.VMEM((2 * ENTRIES, 2 * BLOCK, WIDTH), jnp.float32)],
         compiler_params=params(14),
@@ -378,32 +383,33 @@
     )(*operands)
 
 
-def between(slots, place, code, own, qd, mask):
+def between(slots, place, code, lists, own, qd, mask):
     other = shift(own, "core", 1)
-    sends = gather(slots, place, code, own, other)
-    fetched = [shift(sends[k - 1], "x", k) for k in (1, 2, 3)]
+    sends = gather(slots, lists, own, other)
+    r2, r1, r3 = [shift(sends[k - 1], "x", k) for k in (2, 1, 3)]
     qd = exchange(qd, "head")
     out, g0, g1, g2, g3 = attend(
-        slots, place, code, qd, own, other, *fetched, mask
+        slots, place, code, qd, own, other, r1, r2, r3, mask
     )
 
-    returned = [shift(g, "x", -k) for k, g in ((1, g1), (2, g2), (3, g3))]
+    g2, g1, g3 = [shift(g, "x", -k) for k, g in ((2, g2), (1, g1), (3, g3))]
     out = exchange(out, "head")
-    *returned, out = lax.optimization_barrier((*returned, out))
-    own_sum, other_sum = scatter(place, code, g0, *returned)
+    g1, g2, g3, out = lax.optimization_barrier((g1, g2, g3, out))
+    own_sum, other_sum = scatter(lists, g0, g1, g2, g3)
     from_core = shift(other_sum, "core", 1)
     column_sum = add(own_sum, from_core)
     return out, column_sum
 
 
 def per_device(queries, keys, values, output_gradient, kv_list, kv_type, session_id):
-    where = [lax.axis_index(axis) for axis in ("z", "x", "core")]
-    place = jnp.stack(where).astype(jnp.int32)
+    where = [lax.axis_index(axis).astype(jnp.int32) for axis in ("z", "x", "core")]
+    place = jnp.stack(where)
 
     code, most = coded(kv_list)
     sess = session_id.astype(jnp.float32).reshape(-1, BLOCK)
 
-    code, most = lax.optimization_barrier((code, most))
+    lists = neighbour_lists(where, code)
+    code, most, lists = lax.optimization_barrier((code, most, lists))
 
     kv = jnp.stack([keys, values]).transpose(2, 0, 1, 3)
     kv = jnp.broadcast_to(kv, (Z, HEAD, 2, QUARTER, WIDTH))
@@ -418,7 +424,7 @@
     out, column_sum = lax.switch(
         sum((most > few).astype(jnp.int32) for few in SLOTS[:-1]),
         [functools.partial(between, slots) for slots in SLOTS],
-        place, code, own, qd, mask,
+        place, code, lists, own, qd, mask,
     )
 
     parts = exchange(column_sum.reshape(Z * HEAD, 2, QUARTER, WIDTH), ("z", "head"))

time: 196 us -> 193 us (0.985)
  Pallas kernels: 20.6 us -> 18.1 us
  transfers between devices with their start and end apart: 12 -> 12, of which waited for: 9 -> 9; matrix products, arithmetic and copies ran while one was open for 3% -> 4% of each run, Pallas kernels for 3% -> 2%
where the time goes in v9:
time: 193 us; the launch traced here: 191 us
  waiting for transfers between devices  88.5 us (46%)
  starting transfers between devices  65.3 us (34%)
  Pallas kernels  18.1 us (9%)
  local copies, waits for them, and re-layouts  12.5 us (6%)
  other arithmetic  3.49 us (2%)
  between operations  2.81 us (1%)
    ppermute x8, waiting for transfers between devices, shift(): lax.ppermute(array, axis, [(i, (i + by) % size) for i in range(size)])  47.6 us
    all_to_all x4, waiting for transfers between devices, exchange(): return lax.all_to_all(array, axis, split_axis=0, concat_axis=0, tiled=True)  40.9 us
    all_to_all x4, starting transfers between devices, exchange(): return lax.all_to_all(array, axis, split_axis=0, concat_axis=0, tiled=True)  38.2 us
    ppermute x8, starting transfers between devices, shift(): lax.ppermute(array, axis, [(i, (i + by) % size) for i in range(size)])  27.1 us
    pallas_call x1, Pallas kernels, attend(): pl.pallas_call(attend_kernel, out_shape=[outs, blocks(ENTRIES)] + [blocks...  11.9 us
    unnamed x17, local copies, waits for them, and re-layouts  5.49 us
  transfers between devices with their start and end apart: 12, of which 9 were waited for; matrix products, arithmetic and copies ran while one was open for 4% of the time, Pallas kernels for 2%

profile of v9, /device:TPU:1, one launch (start us, length us, event | category | flops | bytes accessed | tf_op | source)
XLA Modules:
  0.0 191.0 jit_solution(4260717653333879319)
XLA Ops:
  1.5 1.2 broadcast_in_dim.58
  2.8 17.1 %all-to-all-start.8 = ((bf16[64,2,32,128]{3,2,1,0:T(8,128)(2,1)}), bf16[64,2,32,128]{3,2,1,0:T(8,128)(2,1)S(1)}, u32[]{:S(2)}, u32[]{:S(2)}) async-start(bf16[64,2,32,128]{3,2,1,0:T(8,128)(2,1)} %bitcast.12), calls=%async_computation.8 | async-start | bytes 2097152 | tf_op jit(solution)/shard_map/all_to_all | solution.py:301
  27.9 2.5 %shard_map.102 = f32[16,128,128]{2,1,0:T(8,128)S(1)} custom-call(s32[3]{0:T(128)S(1)} %pad_add_fusion.2.place, s32[8,128]{1,0:T(8,128)S(1)} %bitcast.29, s32[8,128]{1,0:T(8,128)S(1)} %bitcast.30, f32[128,128]{1,0:T(8,128)S(1)} %convert_bitcast_fusion.sess), custom_call_target="tpu_custom_call" | custom-call | flops 2097152 | bytes 1048576 | tf_op jit(solution)/shard_map/pallas_call | solution.py:341
  30.3 1.1 maximum_bitcast_fusion
  31.4 16.0 %all-to-all-done.8 = bf16[64,2,32,128]{3,2,1,0:T(8,128)(2,1)S(1)} async-done(((bf16[64,2,32,128]{3,2,1,0:T(8,128)(2,1)}), bf16[64,2,32,128]{3,2,1,0:T(8,128)(2,1)S(1)}, u32[]{:S(2)}, u32[]{:S(2)}) %all-to-all-start.8) | async-done | bytes 1048608 | tf_op jit(solution)/shard_map/all_to_all | solution.py:301
  47.4 104.9 %conditional.1 = (bf16[8,2,8,32,128]{4,3,2,1,0:T(8,128)(2,1)}, bf16[16,256,128]{2,1,0:T(8,128)(2,1)S(1)}) conditional(s32[]{:T(128)} %clamp.3, (bf16[8,2,8,32,128]{4,3,2,1,0:T(8,128)(2,1)}, bf16[16,256,128]{2,1,0:T(8,128)(2,1)S(1)}, s32[68]{0:T(128)S(1)}, s32[3]{0:T(128)S(1)}, s32[1024]{0:T(1024)S(1)}, ...), branch_computations={%region_5.6_spmd, %region_6.7_spmd, %region_7.8_spmd, %region_8.9_... | conditional | flops 2684354560 | bytes 72876624 | solution.py:424
  47.4 5.4 %all-to-all-start.2 = ((bf16[8,2,8,32,128]{4,3,2,1,0:T(8,128)(2,1)}), bf16[8,2,8,32,128]{4,3,2,1,0:T(8,128)(2,1)S(1)}, u32[]{:S(2)}, u32[]{:S(2)}) async-start(bf16[8,2,8,32,128]{4,3,2,1,0:T(8,128)(2,1)} %get-tuple-element.70), calls=%async_computation.2 | async-start | bytes 2097152 | tf_op jit(solution)/shard_map/cond/branch_1_fun/all_to_all | solution.py:301
  52.7 4.5 %collective-permute-start.8 = (bf16[16,256,128]{2,1,0:T(8,128)(2,1)S(1)}, bf16[16,256,128]{2,1,0:T(8,128)(2,1)S(1)}, u32[]{:S(2)}, u32[]{:S(2)}) collective-permute-start(bf16[16,256,128]{2,1,0:T(8,128)(2,1)S(1)} %get-tuple-element.71.own), channel_id=1, source_target_pairs={{0,8},{8,0},{1,9},{9,1},{2,10},{10,2},{3,11},{11,3},{4,12},{12,4},... | collective-permute-start | bytes 3145736 | tf_op jit(solution)/shard_map/cond/branch_1_fun/ppermute | solution.py:293
  57.3 2.3 %collective-permute-done.8.oth = bf16[16,256,128]{2,1,0:T(8,128)(2,1)S(1)} collective-permute-done((bf16[16,256,128]{2,1,0:T(8,128)(2,1)S(1)}, bf16[16,256,128]{2,1,0:T(8,128)(2,1)S(1)}, u32[]{:S(2)}, u32[]{:S(2)}) %collective-permute-start.8) | collective-permute-done | bytes 1048608 | tf_op jit(solution)/shard_map/cond/branch_1_fun/ppermute | solution.py:293
  59.5 2.2 %branch_1_fun.4 = (bf16[8,256,128]{2,1,0:T(8,128)(2,1)S(1)}, bf16[8,256,128]{2,1,0:T(8,128)(2,1)S(1)}, bf16[8,256,128]{2,1,0:T(8,128)(2,1)S(1)}) custom-call(s32[68]{0:T(128)S(1)} %get-tuple-element.72.lists, bf16[16,256,128]{2,1,0:T(8,128)(2,1)S(1)} %get-tuple-element.71.own, bf16[16,256,128]{2,1,0:T(8,128)(2,1)S(1)} %collective-permute-done.8.oth), custom_call_target="tpu_custom_call" | custom-call | tf_op jit(solution)/shard_map/cond/branch_1_fun/pallas_call | solution.py:305
  61.8 3.1 %collective-permute-start.9 = (bf16[8,256,128]{2,1,0:T(8,128)(2,1)S(1)}, bf16[8,256,128]{2,1,0:T(8,128)(2,1)S(1)}, u32[]{:S(2)}, u32[]{:S(2)}) collective-permute-start(bf16[8,256,128]{2,1,0:T(8,128)(2,1)S(1)} %get-tuple-element.73), channel_id=1, source_target_pairs={{0,16},{16,32},{32,48},{48,0},{1,17},{17,33},{33,49},{49,1},{2,18}... | collective-permute-start | bytes 1572872 | tf_op jit(solution)/shard_map/cond/branch_1_fun/ppermute | solution.py:293
  64.9 4.8 %collective-permute-start.10 = (bf16[8,256,128]{2,1,0:T(8,128)(2,1)S(1)}, bf16[8,256,128]{2,1,0:T(8,128)(2,1)S(1)}, u32[]{:S(2)}, u32[]{:S(2)}) collective-permute-start(bf16[8,256,128]{2,1,0:T(8,128)(2,1)S(1)} %get-tuple-element.74), channel_id=1, source_target_pairs={{0,32},{16,48},{32,0},{48,16},{1,33},{17,49},{33,1},{49,17},{2,34}... | collective-permute-start | bytes 1572872 | tf_op jit(solution)/shard_map/cond/branch_1_fun/ppermute | solution.py:293
  69.7 2.5 %collective-permute-start.11 = (bf16[8,256,128]{2,1,0:T(8,128)(2,1)S(1)}, bf16[8,256,128]{2,1,0:T(8,128)(2,1)}, u32[]{:S(2)}, u32[]{:S(2)}) collective-permute-start(bf16[8,256,128]{2,1,0:T(8,128)(2,1)S(1)} %get-tuple-element.75), channel_id=1, source_target_pairs={{0,48},{16,0},{32,16},{48,32},{1,49},{17,1},{33,17},{49,33},{2,50}... | collective-permute-start | bytes 1572872 | tf_op jit(solution)/shard_map/cond/branch_1_fun/ppermute | solution.py:293
  72.2 5.9 %collective-permute-done.9.r1 = bf16[8,256,128]{2,1,0:T(8,128)(2,1)S(1)} collective-permute-done((bf16[8,256,128]{2,1,0:T(8,128)(2,1)S(1)}, bf16[8,256,128]{2,1,0:T(8,128)(2,1)S(1)}, u32[]{:S(2)}, u32[]{:S(2)}) %collective-permute-start.9) | collective-permute-done | bytes 524320 | tf_op jit(solution)/shard_map/cond/branch_1_fun/ppermute | solution.py:293
  78.1 13.2 %collective-permute-done.10.r2 = bf16[8,256,128]{2,1,0:T(8,128)(2,1)S(1)} collective-permute-done((bf16[8,256,128]{2,1,0:T(8,128)(2,1)S(1)}, bf16[8,256,128]{2,1,0:T(8,128)(2,1)S(1)}, u32[]{:S(2)}, u32[]{:S(2)}) %collective-permute-start.10) | collective-permute-done | bytes 524320 | tf_op jit(solution)/shard_map/cond/branch_1_fun/ppermute | solution.py:293
  92.1 1.0 copy-done.16
  93.1 11.9 %branch_1_fun.5 = (bf16[8,2,8,32,128]{4,3,2,1,0:T(8,128)(2,1)}, bf16[16,256,128]{2,1,0:T(8,128)(2,1)}, bf16[8,256,128]{2,1,0:T(8,128)(2,1)}, bf16[8,256,128]{2,1,0:T(8,128)(2,1)}, bf16[8,256,128]{2,1,0:T(8,128)(2,1)}) custom-call(s32[3]{0:T(128)S(1)} %get-tuple-element.68.place, s32[1024]{0:T(1024)S(1)} %get-tuple-element.69.code, ...), custom_call_target="tpu_custom_call" | custom-call | flops 2684354560 | bytes 8388608 | tf_op jit(solution)/shard_map/cond/branch_1_fun/pallas_call | solution.py:353
  105.0 7.1 %all-to-all-start.3 = ((bf16[8,2,8,32,128]{4,3,2,1,0:T(8,128)(2,1)}), bf16[8,2,8,32,128]{4,3,2,1,0:T(8,128)(2,1)}, u32[]{:S(2)}, u32[]{:S(2)}) async-start(bf16[8,2,8,32,128]{4,3,2,1,0:T(8,128)(2,1)} %get-tuple-element.80), calls=%async_computation.3 | async-start | bytes 2097152 | tf_op jit(solution)/shard_map/cond/branch_1_fun/all_to_all | solution.py:301
  112.1 5.0 %collective-permute-start.12 = (bf16[8,256,128]{2,1,0:T(8,128)(2,1)}, bf16[8,256,128]{2,1,0:T(8,128)(2,1)S(1)}, u32[]{:S(2)}, u32[]{:S(2)}) collective-permute-start(bf16[8,256,128]{2,1,0:T(8,128)(2,1)} %get-tuple-element.77), channel_id=1, source_target_pairs={{0,48},{16,0},{32,16},{48,32},{1,49},{17,1},{33,17},{49,33},{2,50}... | collective-permute-start | bytes 1572872 | tf_op jit(solution)/shard_map/cond/branch_1_fun/ppermute | solution.py:293
  117.1 2.8 %collective-permute-start.13 = (bf16[8,256,128]{2,1,0:T(8,128)(2,1)}, bf16[8,256,128]{2,1,0:T(8,128)(2,1)S(1)}, u32[]{:S(2)}, u32[]{:S(2)}) collective-permute-start(bf16[8,256,128]{2,1,0:T(8,128)(2,1)} %get-tuple-element.78), channel_id=1, source_target_pairs={{0,32},{16,48},{32,0},{48,16},{1,33},{17,49},{33,1},{49,17},{2,34}... | collective-permute-start | bytes 1572872 | tf_op jit(solution)/shard_map/cond/branch_1_fun/ppermute | solution.py:293
  119.9 1.9 %collective-permute-start.14 = (bf16[8,256,128]{2,1,0:T(8,128)(2,1)S(1)}, bf16[8,256,128]{2,1,0:T(8,128)(2,1)S(1)}, u32[]{:S(2)}, u32[]{:S(2)}) collective-permute-start(bf16[8,256,128]{2,1,0:T(8,128)(2,1)S(1)} %copy-done.25), channel_id=1, source_target_pairs={{0,16},{16,32},{32,48},{48,0},{1,17},{17,33},{33,49},{49,1},{2,18}... | collective-permute-start | bytes 1572872 | tf_op jit(solution)/shard_map/cond/branch_1_fun/ppermute | solution.py:293
  121.8 6.7 %collective-permute-done.12.g1 = bf16[8,256,128]{2,1,0:T(8,128)(2,1)S(1)} collective-permute-done((bf16[8,256,128]{2,1,0:T(8,128)(2,1)}, bf16[8,256,128]{2,1,0:T(8,128)(2,1)S(1)}, u32[]{:S(2)}, u32[]{:S(2)}) %collective-permute-start.12) | collective-permute-done | bytes 524320 | tf_op jit(solution)/shard_map/cond/branch_1_fun/ppermute | solution.py:293
  128.6 4.5 %collective-permute-done.13.g2 = bf16[8,256,128]{2,1,0:T(8,128)(2,1)S(1)} collective-permute-done((bf16[8,256,128]{2,1,0:T(8,128)(2,1)}, bf16[8,256,128]{2,1,0:T(8,128)(2,1)S(1)}, u32[]{:S(2)}, u32[]{:S(2)}) %collective-permute-start.13) | collective-permute-done | bytes 524320 | tf_op jit(solution)/shard_map/cond/branch_1_fun/ppermute | solution.py:293
  133.1 12.7 %collective-permute-done.14.g3 = bf16[8,256,128]{2,1,0:T(8,128)(2,1)S(1)} collective-permute-done((bf16[8,256,128]{2,1,0:T(8,128)(2,1)S(1)}, bf16[8,256,128]{2,1,0:T(8,128)(2,1)S(1)}, u32[]{:S(2)}, u32[]{:S(2)}) %collective-permute-start.14) | collective-permute-done | bytes 524320 | tf_op jit(solution)/shard_map/cond/branch_1_fun/ppermute | solution.py:293
  145.8 1.3 branch_1_fun.6
  147.0 2.5 %collective-permute-start.15 = (bf16[16,256,128]{2,1,0:T(8,128)(2,1)S(1)}, bf16[16,256,128]{2,1,0:T(8,128)(2,1)S(1)}, u32[]{:S(2)}, u32[]{:S(2)}) collective-permute-start(bf16[16,256,128]{2,1,0:T(8,128)(2,1)S(1)} %get-tuple-element.87), channel_id=1, source_target_pairs={{0,8},{8,0},{1,9},{9,1},{2,10},{10,2},{3,11},{11,3},{4,12},{12,4},... | collective-permute-start | bytes 3145736 | tf_op jit(solution)/shard_map/cond/branch_1_fun/ppermute | solution.py:293
  149.5 2.3 %collective-permute-done.15.right = bf16[16,256,128]{2,1,0:T(8,128)(2,1)S(1)} collective-permute-done((bf16[16,256,128]{2,1,0:T(8,128)(2,1)S(1)}, bf16[16,256,128]{2,1,0:T(8,128)(2,1)S(1)}, u32[]{:S(2)}, u32[]{:S(2)}) %collective-permute-start.15) | collective-permute-done | bytes 1048608 | tf_op jit(solution)/shard_map/cond/branch_1_fun/ppermute | solution.py:293
  152.2 1.0 copy-done.13
  153.2 8.7 %all-to-all-start.9 = ((bf16[64,2,32,128]{3,2,1,0:T(8,128)(2,1)}), bf16[64,2,32,128]{3,2,1,0:T(8,128)(2,1)S(1)}, u32[]{:S(2)}, u32[]{:S(2)}) async-start(bf16[64,2,32,128]{3,2,1,0:T(8,128)(2,1)} %bitcast.35), calls=%async_computation.9 | async-start | bytes 2097152 | tf_op jit(solution)/shard_map/all_to_all | solution.py:301
  161.9 1.3 fusion.36
  163.2 1.4 copy_bitcast_fusion
  164.6 25.0 %all-to-all-done.9 = bf16[64,2,32,128]{3,2,1,0:T(8,128)(2,1)S(1)} async-done(((bf16[64,2,32,128]{3,2,1,0:T(8,128)(2,1)}), bf16[64,2,32,128]{3,2,1,0:T(8,128)(2,1)S(1)}, u32[]{:S(2)}, u32[]{:S(2)}) %all-to-all-start.9) | async-done | bytes 1048608 | tf_op jit(solution)/shard_map/all_to_all | solution.py:301
  (63 shorter events, 9.3 us)
Async XLA Ops:
  2.8 44.6 %all-to-all-start.8 = ((bf16[64,2,32,128]{3,2,1,0:T(8,128)(2,1)}), bf16[64,2,32,128]{3,2,1,0:T(8,128)(2,1)S(1)}, u32[]{:S(2)}, u32[]{:S(2)}) async-start(bf16[64,2,32,128]{3,2,1,0:T(8,128)(2,1)} %bitcast.12), calls=%async_computation.8 | async-start | bytes 2097152 | tf_op jit(solution)/shard_map/all_to_all | solution.py:301
  20.0 0.7 copy-start.10
  20.0 5.3 %copy-start.18 = (bf16[32,64,128]{2,1,0:T(8,128)(2,1)S(1)}, bf16[32,64,128]{2,1,0:T(8,128)(2,1)}, u32[]{:S(2)}) copy-start(bf16[32,64,128]{2,1,0:T(8,128)(2,1)} %param.11) | copy-start | bytes 1572868
  25.3 1.0 copy-start.19
  26.3 0.8 copy-start.20
  27.2 0.7 copy-start.11
  47.4 44.7 %all-to-all-start.2 = ((bf16[8,2,8,32,128]{4,3,2,1,0:T(8,128)(2,1)}), bf16[8,2,8,32,128]{4,3,2,1,0:T(8,128)(2,1)S(1)}, u32[]{:S(2)}, u32[]{:S(2)}) async-start(bf16[8,2,8,32,128]{4,3,2,1,0:T(8,128)(2,1)} %get-tuple-element.70), calls=%async_computation.2 | async-start | bytes 2097152 | tf_op jit(solution)/shard_map/cond/branch_1_fun/all_to_all | solution.py:301
  52.7 6.8 %collective-permute-start.8 = (bf16[16,256,128]{2,1,0:T(8,128)(2,1)S(1)}, bf16[16,256,128]{2,1,0:T(8,128)(2,1)S(1)}, u32[]{:S(2)}, u32[]{:S(2)}) collective-permute-start(bf16[16,256,128]{2,1,0:T(8,128)(2,1)S(1)} %get-tuple-element.71.own), channel_id=1, source_target_pairs={{0,8},{8,0},{1,9},{9,1},{2,10},{10,2},{3,11},{11,3},{4,12},{12,4},... | collective-permute-start | bytes 3145736 | tf_op jit(solution)/shard_map/cond/branch_1_fun/ppermute | solution.py:293
  59.5 2.2 %copy-start.3 = (bf16[16,256,128]{2,1,0:T(8,128)(2,1)}, bf16[16,256,128]{2,1,0:T(8,128)(2,1)S(1)}, u32[]{:S(2)}) copy-start(bf16[16,256,128]{2,1,0:T(8,128)(2,1)S(1)} %collective-permute-done.8.oth) | copy-start | bytes 3145732 | tf_op jit(solution)/shard_map/cond
  61.8 16.3 %collective-permute-start.9 = (bf16[8,256,128]{2,1,0:T(8,128)(2,1)S(1)}, bf16[8,256,128]{2,1,0:T(8,128)(2,1)S(1)}, u32[]{:S(2)}, u32[]{:S(2)}) collective-permute-start(bf16[8,256,128]{2,1,0:T(8,128)(2,1)S(1)} %get-tuple-element.73), channel_id=1, source_target_pairs={{0,16},{16,32},{32,48},{48,0},{1,17},{17,33},{33,49},{49,1},{2,18}... | collective-permute-start | bytes 1572872 | tf_op jit(solution)/shard_map/cond/branch_1_fun/ppermute | solution.py:293
  64.9 26.4 %collective-permute-start.10 = (bf16[8,256,128]{2,1,0:T(8,128)(2,1)S(1)}, bf16[8,256,128]{2,1,0:T(8,128)(2,1)S(1)}, u32[]{:S(2)}, u32[]{:S(2)}) collective-permute-start(bf16[8,256,128]{2,1,0:T(8,128)(2,1)S(1)} %get-tuple-element.74), channel_id=1, source_target_pairs={{0,32},{16,48},{32,0},{48,16},{1,33},{17,49},{33,1},{49,17},{2,34}... | collective-permute-start | bytes 1572872 | tf_op jit(solution)/shard_map/cond/branch_1_fun/ppermute | solution.py:293
  69.7 22.4 %collective-permute-start.11 = (bf16[8,256,128]{2,1,0:T(8,128)(2,1)S(1)}, bf16[8,256,128]{2,1,0:T(8,128)(2,1)}, u32[]{:S(2)}, u32[]{:S(2)}) collective-permute-start(bf16[8,256,128]{2,1,0:T(8,128)(2,1)S(1)} %get-tuple-element.75), channel_id=1, source_target_pairs={{0,48},{16,0},{32,16},{48,32},{1,49},{17,1},{33,17},{49,33},{2,50}... | collective-permute-start | bytes 1572872 | tf_op jit(solution)/shard_map/cond/branch_1_fun/ppermute | solution.py:293
  78.1 13.2 %copy-start.24 = (bf16[8,256,128]{2,1,0:T(8,128)(2,1)}, bf16[8,256,128]{2,1,0:T(8,128)(2,1)S(1)}, u32[]{:S(2)}) copy-start(bf16[8,256,128]{2,1,0:T(8,128)(2,1)S(1)} %collective-permute-done.9.r1) | copy-start | bytes 1572868 | tf_op jit(solution)/shard_map/cond
  91.3 0.8 copy-start.26
  92.1 1.0 copy-start.16
  105.0 14.9 %copy-start.25 = (bf16[8,256,128]{2,1,0:T(8,128)(2,1)S(1)}, bf16[8,256,128]{2,1,0:T(8,128)(2,1)}, u32[]{:S(2)}) copy-start(bf16[8,256,128]{2,1,0:T(8,128)(2,1)} %get-tuple-element.79) | copy-start | bytes 1572868 | tf_op jit(solution)/shard_map/cond
  105.0 40.7 %copy-start.5 = (bf16[16,256,128]{2,1,0:T(8,128)(2,1)S(1)}, bf16[16,256,128]{2,1,0:T(8,128)(2,1)}, u32[]{:S(2)}) copy-start(bf16[16,256,128]{2,1,0:T(8,128)(2,1)} %get-tuple-element.82.g0) | copy-start | bytes 3145732 | tf_op jit(solution)/shard_map/cond
  105.0 40.7 %all-to-all-start.3 = ((bf16[8,2,8,32,128]{4,3,2,1,0:T(8,128)(2,1)}), bf16[8,2,8,32,128]{4,3,2,1,0:T(8,128)(2,1)}, u32[]{:S(2)}, u32[]{:S(2)}) async-start(bf16[8,2,8,32,128]{4,3,2,1,0:T(8,128)(2,1)} %get-tuple-element.80), calls=%async_computation.3 | async-start | bytes 2097152 | tf_op jit(solution)/shard_map/cond/branch_1_fun/all_to_all | solution.py:301
  112.1 16.5 %collective-permute-start.12 = (bf16[8,256,128]{2,1,0:T(8,128)(2,1)}, bf16[8,256,128]{2,1,0:T(8,128)(2,1)S(1)}, u32[]{:S(2)}, u32[]{:S(2)}) collective-permute-start(bf16[8,256,128]{2,1,0:T(8,128)(2,1)} %get-tuple-element.77), channel_id=1, source_target_pairs={{0,48},{16,0},{32,16},{48,32},{1,49},{17,1},{33,17},{49,33},{2,50}... | collective-permute-start | bytes 1572872 | tf_op jit(solution)/shard_map/cond/branch_1_fun/ppermute | solution.py:293
  117.1 16.0 %collective-permute-start.13 = (bf16[8,256,128]{2,1,0:T(8,128)(2,1)}, bf16[8,256,128]{2,1,0:T(8,128)(2,1)S(1)}, u32[]{:S(2)}, u32[]{:S(2)}) collective-permute-start(bf16[8,256,128]{2,1,0:T(8,128)(2,1)} %get-tuple-element.78), channel_id=1, source_target_pairs={{0,32},{16,48},{32,0},{48,16},{1,33},{17,49},{33,1},{49,17},{2,34}... | collective-permute-start | bytes 1572872 | tf_op jit(solution)/shard_map/cond/branch_1_fun/ppermute | solution.py:293
  119.9 25.9 %collective-permute-start.14 = (bf16[8,256,128]{2,1,0:T(8,128)(2,1)S(1)}, bf16[8,256,128]{2,1,0:T(8,128)(2,1)S(1)}, u32[]{:S(2)}, u32[]{:S(2)}) collective-permute-start(bf16[8,256,128]{2,1,0:T(8,128)(2,1)S(1)} %copy-done.25), channel_id=1, source_target_pairs={{0,16},{16,32},{32,48},{48,0},{1,17},{17,33},{33,49},{49,1},{2,18}... | collective-permute-start | bytes 1572872 | tf_op jit(solution)/shard_map/cond/branch_1_fun/ppermute | solution.py:293
  147.0 4.7 %collective-permute-start.15 = (bf16[16,256,128]{2,1,0:T(8,128)(2,1)S(1)}, bf16[16,256,128]{2,1,0:T(8,128)(2,1)S(1)}, u32[]{:S(2)}, u32[]{:S(2)}) collective-permute-start(bf16[16,256,128]{2,1,0:T(8,128)(2,1)S(1)} %get-tuple-element.87), channel_id=1, source_target_pairs={{0,8},{8,0},{1,9},{9,1},{2,10},{10,2},{3,11},{11,3},{4,12},{12,4},... | collective-permute-start | bytes 3145736 | tf_op jit(solution)/shard_map/cond/branch_1_fun/ppermute | solution.py:293
  152.2 1.0 copy-start.13
  153.2 36.3 %all-to-all-start.9 = ((bf16[64,2,32,128]{3,2,1,0:T(8,128)(2,1)}), bf16[64,2,32,128]{3,2,1,0:T(8,128)(2,1)S(1)}, u32[]{:S(2)}, u32[]{:S(2)}) async-start(bf16[64,2,32,128]{3,2,1,0:T(8,128)(2,1)} %bitcast.35), calls=%async_computation.9 | async-start | bytes 2097152 | tf_op jit(solution)/shard_map/all_to_all | solution.py:301

commit v10 on v9

--- a/solution.py
+++ b/solution.py
@@ -376,7 +376,7 @@
             DMA((2,)),
             DMA((ENTRIES,)),
         ],
-        compiler_params=params(60),
+        compiler_params=params(50),
         cost_estimate=pl.CostEstimate(
             flops=5 * 2 * 2048 * 1024 * 128, bytes_accessed=8 * MIB, transcendentals=2048 * 1024
         ),

time: 193 us -> 188 us (0.974)
  waiting for transfers between devices: 88.5 us -> 81.6 us
  Pallas kernels: 18.1 us -> 21.2 us
    ppermute x8, waiting for transfers between devices: 47.6 us -> 41.7 us  [shift(): lax.ppermute(array, axis, [(i, (i + by) % size) for i in range(size)])]
    unnamed x17 -> x15, local copies, waits for them, and re-layouts: 5.49 us -> 4.54 us
  transfers between devices with their start and end apart: 12 -> 12, of which waited for: 9 -> 10; matrix products, arithmetic and copies ran while one was open for 4% -> 4% of each run, Pallas kernels for 2% -> 3%
where the time goes in v10:
time: 188 us; the launch traced here: 186 us
  waiting for transfers between devices  81.6 us (43%)
  starting transfers between devices  66.2 us (35%)
  Pallas kernels  21.2 us (11%)
  local copies, waits for them, and re-layouts  10.8 us (6%)
  other arithmetic  3.51 us (2%)
  between operations  2.79 us (1%)
    ppermute x8, waiting for transfers between devices, shift(): lax.ppermute(array, axis, [(i, (i + by) % size) for i in range(size)])  41.7 us
    all_to_all x4, waiting for transfers between devices, exchange(): return lax.all_to_all(array, axis, split_axis=0, concat_axis=0, tiled=True)  39.9 us
    all_to_all x4, starting transfers between devices, exchange(): return lax.all_to_all(array, axis, split_axis=0, concat_axis=0, tiled=True)  38.4 us
    ppermute x8, starting transfers between devices, shift(): lax.ppermute(array, axis, [(i, (i + by) % size) for i in range(size)])  27.8 us
    pallas_call x1, Pallas kernels, attend(): pl.pallas_call(attend_kernel, out_shape=[outs, blocks(ENTRIES)] + [blocks...  12.6 us
    unnamed x15, local copies, waits for them, and re-layouts  4.54 us
  transfers between devices with their start and end apart: 12, of which 10 were waited for; matrix products, arithmetic and copies ran while one was open for 4% of the time, Pallas kernels for 3%

profile of v10, /device:TPU:1, one launch (start us, length us, event | category | flops | bytes accessed | tf_op | source)
XLA Modules:
  0.0 186.2 jit_solution(17810908677879184078)
XLA Ops:
  1.5 1.3 broadcast_in_dim.58
  2.8 17.1 %all-to-all-start.8 = ((bf16[64,2,32,128]{3,2,1,0:T(8,128)(2,1)}), bf16[64,2,32,128]{3,2,1,0:T(8,128)(2,1)S(1)}, u32[]{:S(2)}, u32[]{:S(2)}) async-start(bf16[64,2,32,128]{3,2,1,0:T(8,128)(2,1)} %bitcast.12), calls=%async_computation.8 | async-start | bytes 2097152 | tf_op jit(solution)/shard_map/all_to_all | solution.py:301
  27.9 3.4 %shard_map.102 = f32[16,128,128]{2,1,0:T(8,128)} custom-call(s32[3]{0:T(128)S(1)} %pad_add_fusion.2.place, s32[8,128]{1,0:T(8,128)S(1)} %bitcast.29, s32[8,128]{1,0:T(8,128)S(1)} %bitcast.30, f32[128,128]{1,0:T(8,128)S(1)} %convert_bitcast_fusion.sess), custom_call_target="tpu_custom_call" | custom-call | flops 2097152 | bytes 1048576 | tf_op jit(solution)/shard_map/pallas_call | solution.py:341
  31.3 1.1 maximum_bitcast_fusion
  32.4 15.0 %all-to-all-done.8 = bf16[64,2,32,128]{3,2,1,0:T(8,128)(2,1)S(1)} async-done(((bf16[64,2,32,128]{3,2,1,0:T(8,128)(2,1)}), bf16[64,2,32,128]{3,2,1,0:T(8,128)(2,1)S(1)}, u32[]{:S(2)}, u32[]{:S(2)}) %all-to-all-start.8) | async-done | bytes 1048608 | tf_op jit(solution)/shard_map/all_to_all | solution.py:301
  47.4 100.8 %conditional.1 = (bf16[8,2,8,32,128]{4,3,2,1,0:T(8,128)(2,1)}, bf16[16,256,128]{2,1,0:T(8,128)(2,1)}) conditional(s32[]{:T(128)} %clamp.3, (bf16[8,2,8,32,128]{4,3,2,1,0:T(8,128)(2,1)}, bf16[16,256,128]{2,1,0:T(8,128)(2,1)S(1)}, s32[68]{0:T(128)S(1)}, s32[3]{0:T(128)S(1)}, s32[1024]{0:T(1024)S(1)}, ...), branch_computations={%region_5.6_spmd, %region_6.7_spmd, %region_7.8_spmd, %region_8.9_... | conditional | flops 2684354560 | bytes 72352336 | solution.py:424
  47.4 5.4 %all-to-all-start = ((bf16[8,2,8,32,128]{4,3,2,1,0:T(8,128)(2,1)}), bf16[8,2,8,32,128]{4,3,2,1,0:T(8,128)(2,1)S(1)}, u32[]{:S(2)}, u32[]{:S(2)}) async-start(bf16[8,2,8,32,128]{4,3,2,1,0:T(8,128)(2,1)} %get-tuple-element.50), calls=%async_computation | async-start | bytes 2097152 | tf_op jit(solution)/shard_map/cond/branch_0_fun/all_to_all | solution.py:301
  52.8 4.5 %collective-permute-start = (bf16[16,256,128]{2,1,0:T(8,128)(2,1)S(1)}, bf16[16,256,128]{2,1,0:T(8,128)(2,1)S(1)}, u32[]{:S(2)}, u32[]{:S(2)}) collective-permute-start(bf16[16,256,128]{2,1,0:T(8,128)(2,1)S(1)} %get-tuple-element.51.own), channel_id=1, source_target_pairs={{0,8},{8,0},{1,9},{9,1},{2,10},{10,2},{3,11},{11,3},{4,12},{12,4},... | collective-permute-start | bytes 3145736 | tf_op jit(solution)/shard_map/cond/branch_0_fun/ppermute | solution.py:293
  57.3 2.3 %collective-permute-done.oth = bf16[16,256,128]{2,1,0:T(8,128)(2,1)S(1)} collective-permute-done((bf16[16,256,128]{2,1,0:T(8,128)(2,1)S(1)}, bf16[16,256,128]{2,1,0:T(8,128)(2,1)S(1)}, u32[]{:S(2)}, u32[]{:S(2)}) %collective-permute-start) | collective-permute-done | bytes 1048608 | tf_op jit(solution)/shard_map/cond/branch_0_fun/ppermute | solution.py:293
  59.6 2.5 %branch_0_fun.4 = (bf16[7,256,128]{2,1,0:T(8,128)(2,1)S(1)}, bf16[7,256,128]{2,1,0:T(8,128)(2,1)S(1)}, bf16[7,256,128]{2,1,0:T(8,128)(2,1)S(1)}) custom-call(s32[68]{0:T(128)S(1)} %get-tuple-element.52.lists, bf16[16,256,128]{2,1,0:T(8,128)(2,1)S(1)} %get-tuple-element.51.own, bf16[16,256,128]{2,1,0:T(8,128)(2,1)S(1)} %collective-permute-done.oth), custom_call_target="tpu_custom_call" | custom-call | tf_op jit(solution)/shard_map/cond/branch_0_fun/pallas_call | solution.py:305
  62.1 2.1 %collective-permute-start.1 = (bf16[7,256,128]{2,1,0:T(8,128)(2,1)S(1)}, bf16[7,256,128]{2,1,0:T(8,128)(2,1)S(1)}, u32[]{:S(2)}, u32[]{:S(2)}) collective-permute-start(bf16[7,256,128]{2,1,0:T(8,128)(2,1)S(1)} %get-tuple-element.53), channel_id=1, source_target_pairs={{0,16},{16,32},{32,48},{48,0},{1,17},{17,33},{33,49},{49,1},{2,18}... | collective-permute-start | bytes 1376264 | tf_op jit(solution)/shard_map/cond/branch_0_fun/ppermute | solution.py:293
  64.3 5.0 %collective-permute-start.2 = (bf16[7,256,128]{2,1,0:T(8,128)(2,1)S(1)}, bf16[7,256,128]{2,1,0:T(8,128)(2,1)S(1)}, u32[]{:S(2)}, u32[]{:S(2)}) collective-permute-start(bf16[7,256,128]{2,1,0:T(8,128)(2,1)S(1)} %get-tuple-element.54), channel_id=1, source_target_pairs={{0,32},{16,48},{32,0},{48,16},{1,33},{17,49},{33,1},{49,17},{2,34}... | collective-permute-start | bytes 1376264 | tf_op jit(solution)/shard_map/cond/branch_0_fun/ppermute | solution.py:293
  69.3 3.2 %collective-permute-start.3 = (bf16[7,256,128]{2,1,0:T(8,128)(2,1)S(1)}, bf16[7,256,128]{2,1,0:T(8,128)(2,1)S(1)}, u32[]{:S(2)}, u32[]{:S(2)}) collective-permute-start(bf16[7,256,128]{2,1,0:T(8,128)(2,1)S(1)} %get-tuple-element.55), channel_id=1, source_target_pairs={{0,48},{16,0},{32,16},{48,32},{1,49},{17,1},{33,17},{49,33},{2,50}... | collective-permute-start | bytes 1376264 | tf_op jit(solution)/shard_map/cond/branch_0_fun/ppermute | solution.py:293
  72.5 4.7 %collective-permute-done.1.r1 = bf16[7,256,128]{2,1,0:T(8,128)(2,1)S(1)} collective-permute-done((bf16[7,256,128]{2,1,0:T(8,128)(2,1)S(1)}, bf16[7,256,128]{2,1,0:T(8,128)(2,1)S(1)}, u32[]{:S(2)}, u32[]{:S(2)}) %collective-permute-start.1) | collective-permute-done | bytes 458784 | tf_op jit(solution)/shard_map/cond/branch_0_fun/ppermute | solution.py:293
  77.2 10.2 %collective-permute-done.2.r2 = bf16[7,256,128]{2,1,0:T(8,128)(2,1)S(1)} collective-permute-done((bf16[7,256,128]{2,1,0:T(8,128)(2,1)S(1)}, bf16[7,256,128]{2,1,0:T(8,128)(2,1)S(1)}, u32[]{:S(2)}, u32[]{:S(2)}) %collective-permute-start.2) | collective-permute-done | bytes 458784 | tf_op jit(solution)/shard_map/cond/branch_0_fun/ppermute | solution.py:293
  87.5 1.8 collective-permute-done.3.r3
  90.3 12.6 %branch_0_fun.5 = (bf16[8,2,8,32,128]{4,3,2,1,0:T(8,128)(2,1)}, bf16[16,256,128]{2,1,0:T(8,128)(2,1)}, bf16[7,256,128]{2,1,0:T(8,128)(2,1)}, bf16[7,256,128]{2,1,0:T(8,128)(2,1)S(1)}, bf16[7,256,128]{2,1,0:T(8,128)(2,1)S(1)}) custom-call(s32[3]{0:T(128)S(1)} %get-tuple-element.48.place, s32[1024]{0:T(1024)S(1)} %get-tuple-element.49.code, ...), custom_call_target="tpu_custom_call" | custom-call | flops 2684354560 | bytes 8388608 | tf_op jit(solution)/shard_map/cond/branch_0_fun/pallas_call | solution.py:353
  102.9 7.1 %all-to-all-start.1 = ((bf16[8,2,8,32,128]{4,3,2,1,0:T(8,128)(2,1)}), bf16[8,2,8,32,128]{4,3,2,1,0:T(8,128)(2,1)}, u32[]{:S(2)}, u32[]{:S(2)}) async-start(bf16[8,2,8,32,128]{4,3,2,1,0:T(8,128)(2,1)} %get-tuple-element.60), calls=%async_computation.1 | async-start | bytes 2097152 | tf_op jit(solution)/shard_map/cond/branch_0_fun/all_to_all | solution.py:301
  110.0 5.3 %collective-permute-start.4 = (bf16[7,256,128]{2,1,0:T(8,128)(2,1)}, bf16[7,256,128]{2,1,0:T(8,128)(2,1)S(1)}, u32[]{:S(2)}, u32[]{:S(2)}) collective-permute-start(bf16[7,256,128]{2,1,0:T(8,128)(2,1)} %get-tuple-element.57), channel_id=1, source_target_pairs={{0,48},{16,0},{32,16},{48,32},{1,49},{17,1},{33,17},{49,33},{2,50}... | collective-permute-start | bytes 1376264 | tf_op jit(solution)/shard_map/cond/branch_0_fun/ppermute | solution.py:293
  115.3 3.4 %collective-permute-start.5 = (bf16[7,256,128]{2,1,0:T(8,128)(2,1)S(1)}, bf16[7,256,128]{2,1,0:T(8,128)(2,1)S(1)}, u32[]{:S(2)}, u32[]{:S(2)}) collective-permute-start(bf16[7,256,128]{2,1,0:T(8,128)(2,1)S(1)} %get-tuple-element.58), channel_id=1, source_target_pairs={{0,32},{16,48},{32,0},{48,16},{1,33},{17,49},{33,1},{49,17},{2,34}... | collective-permute-start | bytes 1376264 | tf_op jit(solution)/shard_map/cond/branch_0_fun/ppermute | solution.py:293
  118.7 1.9 %collective-permute-start.6 = (bf16[7,256,128]{2,1,0:T(8,128)(2,1)S(1)}, bf16[7,256,128]{2,1,0:T(8,128)(2,1)S(1)}, u32[]{:S(2)}, u32[]{:S(2)}) collective-permute-start(bf16[7,256,128]{2,1,0:T(8,128)(2,1)S(1)} %get-tuple-element.59), channel_id=1, source_target_pairs={{0,16},{16,32},{32,48},{48,0},{1,17},{17,33},{33,49},{49,1},{2,18}... | collective-permute-start | bytes 1376264 | tf_op jit(solution)/shard_map/cond/branch_0_fun/ppermute | solution.py:293
  120.6 4.7 %collective-permute-done.4.g1 = bf16[7,256,128]{2,1,0:T(8,128)(2,1)S(1)} collective-permute-done((bf16[7,256,128]{2,1,0:T(8,128)(2,1)}, bf16[7,256,128]{2,1,0:T(8,128)(2,1)S(1)}, u32[]{:S(2)}, u32[]{:S(2)}) %collective-permute-start.4) | collective-permute-done | bytes 458784 | tf_op jit(solution)/shard_map/cond/branch_0_fun/ppermute | solution.py:293
  125.4 4.2 %collective-permute-done.5.g2 = bf16[7,256,128]{2,1,0:T(8,128)(2,1)S(1)} collective-permute-done((bf16[7,256,128]{2,1,0:T(8,128)(2,1)S(1)}, bf16[7,256,128]{2,1,0:T(8,128)(2,1)S(1)}, u32[]{:S(2)}, u32[]{:S(2)}) %collective-permute-start.5) | collective-permute-done | bytes 458784 | tf_op jit(solution)/shard_map/cond/branch_0_fun/ppermute | solution.py:293
  129.6 11.4 %collective-permute-done.6.g3 = bf16[7,256,128]{2,1,0:T(8,128)(2,1)S(1)} collective-permute-done((bf16[7,256,128]{2,1,0:T(8,128)(2,1)S(1)}, bf16[7,256,128]{2,1,0:T(8,128)(2,1)S(1)}, u32[]{:S(2)}, u32[]{:S(2)}) %collective-permute-start.6) | collective-permute-done | bytes 458784 | tf_op jit(solution)/shard_map/cond/branch_0_fun/ppermute | solution.py:293
  141.0 1.3 branch_0_fun.6
  142.3 2.3 %collective-permute-start.7 = (bf16[16,256,128]{2,1,0:T(8,128)(2,1)S(1)}, bf16[16,256,128]{2,1,0:T(8,128)(2,1)S(1)}, u32[]{:S(2)}, u32[]{:S(2)}) collective-permute-start(bf16[16,256,128]{2,1,0:T(8,128)(2,1)S(1)} %get-tuple-element.67), channel_id=1, source_target_pairs={{0,8},{8,0},{1,9},{9,1},{2,10},{10,2},{3,11},{11,3},{4,12},{12,4},... | collective-permute-start | bytes 3145736 | tf_op jit(solution)/shard_map/cond/branch_0_fun/ppermute | solution.py:293
  144.7 2.3 %collective-permute-done.7.right = bf16[16,256,128]{2,1,0:T(8,128)(2,1)S(1)} collective-permute-done((bf16[16,256,128]{2,1,0:T(8,128)(2,1)S(1)}, bf16[16,256,128]{2,1,0:T(8,128)(2,1)S(1)}, u32[]{:S(2)}, u32[]{:S(2)}) %collective-permute-start.7) | collective-permute-done | bytes 1048608 | tf_op jit(solution)/shard_map/cond/branch_0_fun/ppermute | solution.py:293
  146.9 1.3 branch_0_fun.7
  148.2 8.8 %all-to-all-start.9 = ((bf16[64,2,32,128]{3,2,1,0:T(8,128)(2,1)}), bf16[64,2,32,128]{3,2,1,0:T(8,128)(2,1)S(1)}, u32[]{:S(2)}, u32[]{:S(2)}) async-start(bf16[64,2,32,128]{3,2,1,0:T(8,128)(2,1)} %bitcast.17), calls=%async_computation.9 | async-start | bytes 2097152 | tf_op jit(solution)/shard_map/all_to_all | solution.py:301
  157.0 1.3 fusion.36
  158.3 1.4 copy_bitcast_fusion
  159.7 25.0 %all-to-all-done.9 = bf16[64,2,32,128]{3,2,1,0:T(8,128)(2,1)S(1)} async-done(((bf16[64,2,32,128]{3,2,1,0:T(8,128)(2,1)}), bf16[64,2,32,128]{3,2,1,0:T(8,128)(2,1)S(1)}, u32[]{:S(2)}, u32[]{:S(2)}) %all-to-all-start.9) | async-done | bytes 1048608 | tf_op jit(solution)/shard_map/all_to_all | solution.py:301
  (55 shorter events, 9.3 us)
Async XLA Ops:
  2.8 44.6 %all-to-all-start.8 = ((bf16[64,2,32,128]{3,2,1,0:T(8,128)(2,1)}), bf16[64,2,32,128]{3,2,1,0:T(8,128)(2,1)S(1)}, u32[]{:S(2)}, u32[]{:S(2)}) async-start(bf16[64,2,32,128]{3,2,1,0:T(8,128)(2,1)} %bitcast.12), calls=%async_computation.8 | async-start | bytes 2097152 | tf_op jit(solution)/shard_map/all_to_all | solution.py:301
  20.0 0.7 copy-start.10
  20.0 5.3 %copy-start.20 = (bf16[32,64,128]{2,1,0:T(8,128)(2,1)S(1)}, bf16[32,64,128]{2,1,0:T(8,128)(2,1)}, u32[]{:S(2)}) copy-start(bf16[32,64,128]{2,1,0:T(8,128)(2,1)} %param.11) | copy-start | bytes 1572868
  25.3 1.0 copy-start.21
  26.4 0.8 copy-start.22
  27.2 0.7 copy-start.11
  47.4 41.9 %all-to-all-start = ((bf16[8,2,8,32,128]{4,3,2,1,0:T(8,128)(2,1)}), bf16[8,2,8,32,128]{4,3,2,1,0:T(8,128)(2,1)S(1)}, u32[]{:S(2)}, u32[]{:S(2)}) async-start(bf16[8,2,8,32,128]{4,3,2,1,0:T(8,128)(2,1)} %get-tuple-element.50), calls=%async_computation | async-start | bytes 2097152 | tf_op jit(solution)/shard_map/cond/branch_0_fun/all_to_all | solution.py:301
  52.8 6.8 %collective-permute-start = (bf16[16,256,128]{2,1,0:T(8,128)(2,1)S(1)}, bf16[16,256,128]{2,1,0:T(8,128)(2,1)S(1)}, u32[]{:S(2)}, u32[]{:S(2)}) collective-permute-start(bf16[16,256,128]{2,1,0:T(8,128)(2,1)S(1)} %get-tuple-element.51.own), channel_id=1, source_target_pairs={{0,8},{8,0},{1,9},{9,1},{2,10},{10,2},{3,11},{11,3},{4,12},{12,4},... | collective-permute-start | bytes 3145736 | tf_op jit(solution)/shard_map/cond/branch_0_fun/ppermute | solution.py:293
  59.6 2.6 %copy-start.2 = (bf16[16,256,128]{2,1,0:T(8,128)(2,1)}, bf16[16,256,128]{2,1,0:T(8,128)(2,1)S(1)}, u32[]{:S(2)}) copy-start(bf16[16,256,128]{2,1,0:T(8,128)(2,1)S(1)} %collective-permute-done.oth) | copy-start | bytes 3145732 | tf_op jit(solution)/shard_map/cond
  62.1 15.1 %collective-permute-start.1 = (bf16[7,256,128]{2,1,0:T(8,128)(2,1)S(1)}, bf16[7,256,128]{2,1,0:T(8,128)(2,1)S(1)}, u32[]{:S(2)}, u32[]{:S(2)}) collective-permute-start(bf16[7,256,128]{2,1,0:T(8,128)(2,1)S(1)} %get-tuple-element.53), channel_id=1, source_target_pairs={{0,16},{16,32},{32,48},{48,0},{1,17},{17,33},{33,49},{49,1},{2,18}... | collective-permute-start | bytes 1376264 | tf_op jit(solution)/shard_map/cond/branch_0_fun/ppermute | solution.py:293
  64.3 23.2 %collective-permute-start.2 = (bf16[7,256,128]{2,1,0:T(8,128)(2,1)S(1)}, bf16[7,256,128]{2,1,0:T(8,128)(2,1)S(1)}, u32[]{:S(2)}, u32[]{:S(2)}) collective-permute-start(bf16[7,256,128]{2,1,0:T(8,128)(2,1)S(1)} %get-tuple-element.54), channel_id=1, source_target_pairs={{0,32},{16,48},{32,0},{48,16},{1,33},{17,49},{33,1},{49,17},{2,34}... | collective-permute-start | bytes 1376264 | tf_op jit(solution)/shard_map/cond/branch_0_fun/ppermute | solution.py:293
  69.3 20.0 %collective-permute-start.3 = (bf16[7,256,128]{2,1,0:T(8,128)(2,1)S(1)}, bf16[7,256,128]{2,1,0:T(8,128)(2,1)S(1)}, u32[]{:S(2)}, u32[]{:S(2)}) collective-permute-start(bf16[7,256,128]{2,1,0:T(8,128)(2,1)S(1)} %get-tuple-element.55), channel_id=1, source_target_pairs={{0,48},{16,0},{32,16},{48,32},{1,49},{17,1},{33,17},{49,33},{2,50}... | collective-permute-start | bytes 1376264 | tf_op jit(solution)/shard_map/cond/branch_0_fun/ppermute | solution.py:293
  89.3 1.0 copy-start.17
  102.9 38.1 %copy-start.6 = (bf16[16,256,128]{2,1,0:T(8,128)(2,1)S(1)}, bf16[16,256,128]{2,1,0:T(8,128)(2,1)}, u32[]{:S(2)}) copy-start(bf16[16,256,128]{2,1,0:T(8,128)(2,1)} %get-tuple-element.62.g0) | copy-start | bytes 3145732 | tf_op jit(solution)/shard_map/cond
  102.9 38.1 %all-to-all-start.1 = ((bf16[8,2,8,32,128]{4,3,2,1,0:T(8,128)(2,1)}), bf16[8,2,8,32,128]{4,3,2,1,0:T(8,128)(2,1)}, u32[]{:S(2)}, u32[]{:S(2)}) async-start(bf16[8,2,8,32,128]{4,3,2,1,0:T(8,128)(2,1)} %get-tuple-element.60), calls=%async_computation.1 | async-start | bytes 2097152 | tf_op jit(solution)/shard_map/cond/branch_0_fun/all_to_all | solution.py:301
  110.0 15.4 %collective-permute-start.4 = (bf16[7,256,128]{2,1,0:T(8,128)(2,1)}, bf16[7,256,128]{2,1,0:T(8,128)(2,1)S(1)}, u32[]{:S(2)}, u32[]{:S(2)}) collective-permute-start(bf16[7,256,128]{2,1,0:T(8,128)(2,1)} %get-tuple-element.57), channel_id=1, source_target_pairs={{0,48},{16,0},{32,16},{48,32},{1,49},{17,1},{33,17},{49,33},{2,50}... | collective-permute-start | bytes 1376264 | tf_op jit(solution)/shard_map/cond/branch_0_fun/ppermute | solution.py:293
  115.3 14.3 %collective-permute-start.5 = (bf16[7,256,128]{2,1,0:T(8,128)(2,1)S(1)}, bf16[7,256,128]{2,1,0:T(8,128)(2,1)S(1)}, u32[]{:S(2)}, u32[]{:S(2)}) collective-permute-start(bf16[7,256,128]{2,1,0:T(8,128)(2,1)S(1)} %get-tuple-element.58), channel_id=1, source_target_pairs={{0,32},{16,48},{32,0},{48,16},{1,33},{17,49},{33,1},{49,17},{2,34}... | collective-permute-start | bytes 1376264 | tf_op jit(solution)/shard_map/cond/branch_0_fun/ppermute | solution.py:293
  118.7 22.3 %collective-permute-start.6 = (bf16[7,256,128]{2,1,0:T(8,128)(2,1)S(1)}, bf16[7,256,128]{2,1,0:T(8,128)(2,1)S(1)}, u32[]{:S(2)}, u32[]{:S(2)}) collective-permute-start(bf16[7,256,128]{2,1,0:T(8,128)(2,1)S(1)} %get-tuple-element.59), channel_id=1, source_target_pairs={{0,16},{16,32},{32,48},{48,0},{1,17},{17,33},{33,49},{49,1},{2,18}... | collective-permute-start | bytes 1376264 | tf_op jit(solution)/shard_map/cond/branch_0_fun/ppermute | solution.py:293
  142.3 4.6 %collective-permute-start.7 = (bf16[16,256,128]{2,1,0:T(8,128)(2,1)S(1)}, bf16[16,256,128]{2,1,0:T(8,128)(2,1)S(1)}, u32[]{:S(2)}, u32[]{:S(2)}) collective-permute-start(bf16[16,256,128]{2,1,0:T(8,128)(2,1)S(1)} %get-tuple-element.67), channel_id=1, source_target_pairs={{0,8},{8,0},{1,9},{9,1},{2,10},{10,2},{3,11},{11,3},{4,12},{12,4},... | collective-permute-start | bytes 3145736 | tf_op jit(solution)/shard_map/cond/branch_0_fun/ppermute | solution.py:293
  148.2 36.5 %all-to-all-start.9 = ((bf16[64,2,32,128]{3,2,1,0:T(8,128)(2,1)}), bf16[64,2,32,128]{3,2,1,0:T(8,128)(2,1)S(1)}, u32[]{:S(2)}, u32[]{:S(2)}) async-start(bf16[64,2,32,128]{3,2,1,0:T(8,128)(2,1)} %bitcast.17), calls=%async_computation.9 | async-start | bytes 2097152 | tf_op jit(solution)/shard_map/all_to_all | solution.py:301
